TPU v7x, 32 devices: a whole 2x2x4 slice. The times are simulated.
32 devices in a mesh: wide: 8 (over z, x), narrow: 4 (over y, core).
Axes of the slice: x: 2, y: 2, z: 4, core: 2. Of those that a mesh axis runs over, the one named last changes fastest.
Arguments:
- cell_tokens: bfloat16 [32, 2208, 256], P('wide'), may hold values from -6 to 6
- library_size: int32 [32], P('wide'), may hold values from 1000 to 19999
- gene_counts: int32 [32, 2200], P('wide'), may hold values from 0 to 7
- attend_in: float32 [3, 256, 256], P(None, None, 'narrow'), as said below
- attend_out: float32 [256, 256], P('narrow'), as said below
- up_weight: float32 [256, 1024], P(None, 'narrow'), as said below
- down_weight: float32 [1024, 256], P('narrow'), as said below
- norm_params: float32 [4, 256], replicated, as said below
- head_weight: float32 [3, 256], replicated, as said below
- first_in: float32 [3, 256, 256], P(None, None, 'narrow'), may hold values from -0.00018310547 to 0.00018310547
- first_out: float32 [256, 256], P('narrow'), may hold values from -0.00018310547 to 0.00018310547
- first_up: float32 [256, 1024], P(None, 'narrow'), may hold values from -0.00018310547 to 0.00018310547
- first_down: float32 [1024, 256], P('narrow'), may hold values from -0.00018310547 to 0.00018310547
- first_norm: float32 [4, 256], replicated, may hold values from -0.00048828125 to 0.00048828125
- first_head: float32 [3, 256], replicated, may hold values from -0.00048828125 to 0.00048828125
- second_in: float32 [3, 256, 256], P(None, None, 'narrow'), may hold values from 7.9292184e-11 to 3.1716874e-10
- second_out: float32 [256, 256], P('narrow'), may hold values from 7.9292184e-11 to 3.1716874e-10
- second_up: float32 [256, 1024], P(None, 'narrow'), may hold values from 7.9292184e-11 to 3.1716874e-10
- second_down: float32 [1024, 256], P('narrow'), may hold values from 7.9292184e-11 to 3.1716874e-10
- second_norm: float32 [4, 256], replicated, may hold values from 6.3433747e-10 to 2.5373499e-09
- second_head: float32 [3, 256], replicated, may hold values from 6.3433747e-10 to 2.5373499e-09
- average_in: float32 [3, 256, 256], P(None, 'wide', 'narrow'), may hold values from -0.375 to 0.375
- average_out: float32 [256, 256], P('narrow', 'wide'), may hold values from -0.375 to 0.375
- average_up: float32 [256, 1024], P('wide', 'narrow'), may hold values from -0.375 to 0.375
- average_down: float32 [1024, 256], P('narrow', 'wide'), may hold values from -0.1875 to 0.1875
- average_norm: float32 [4, 256], P(None, 'wide'), may hold values from 0.5 to 1.5
- average_head: float32 [3, 256], P(None, 'wide'), may hold values from -0.375 to 0.375
Outputs:
- output: bfloat16 [32, 2208, 256], P('wide')
- input_grad: float32 [32, 2208, 256], P('wide')
- grad_norm: float32 [], replicated
- clipped_in: float32 [3, 256, 256], P(None, None, 'narrow')
- new_first_in: float32 [3, 256, 256], P(None, None, 'narrow')
- new_second_in: float32 [3, 256, 256], P(None, None, 'narrow')
- new_attend_in: float32 [3, 256, 256], P(None, None, 'narrow')
- new_average_in: float32 [3, 256, 256], P(None, 'wide', 'narrow')
- clipped_out: float32 [256, 256], P('narrow')
- new_first_out: float32 [256, 256], P('narrow')
- new_second_out: float32 [256, 256], P('narrow')
- new_attend_out: float32 [256, 256], P('narrow')
- new_average_out: float32 [256, 256], P('narrow', 'wide')
- clipped_up: float32 [256, 1024], P(None, 'narrow')
- new_first_up: float32 [256, 1024], P(None, 'narrow')
- new_second_up: float32 [256, 1024], P(None, 'narrow')
- new_up_weight: float32 [256, 1024], P(None, 'narrow')
- new_average_up: float32 [256, 1024], P('wide', 'narrow')
- clipped_down: float32 [1024, 256], P('narrow')
- new_first_down: float32 [1024, 256], P('narrow')
- new_second_down: float32 [1024, 256], P('narrow')
- new_down_weight: float32 [1024, 256], P('narrow')
- new_average_down: float32 [1024, 256], P('narrow', 'wide')
- clipped_norm: float32 [4, 256], replicated
- new_first_norm: float32 [4, 256], replicated
- new_second_norm: float32 [4, 256], replicated
- new_norm_params: float32 [4, 256], replicated
- new_average_norm: float32 [4, 256], P(None, 'wide')
- clipped_head: float32 [3, 256], replicated
- new_first_head: float32 [3, 256], replicated
- new_second_head: float32 [3, 256], replicated
- new_head_weight: float32 [3, 256], replicated
- new_average_head: float32 [3, 256], P(None, 'wide')
Inputs may be any that keep to these rules, and one draw needn't show every extreme that they name: `attend_in`: real values. `attend_out`: real values. `up_weight`: real values. `down_weight`: real values. `norm_params`: gains in rows 0 and 2 are positive. `head_weight`: real values.
All inputs are finite; a program needn't handle non-finite values.
Results may differ from a plain program's by a relative error of at most 0.017.
The roundings to bfloat16 on the way count: a program that leaves them out, or rounds other values in their place, can miss the bound.
Values may be sent and summed in bfloat16 or wider, within the bound.
A program may use at most 192 MiB of HBM per device.

v0:
```python
import jax
import jax.numpy as jnp
from jax import lax
from jax.sharding import PartitionSpec as P

D = 256
HEADS = 4
CLASS_TOK = 8
QBLOCKS = 4
STEP = 10


TOP_PRECISION = lax.Precision.HIGHEST
layer_eps = 1e-05
clip_limit = 0.25
decay_first = 0.9
decay_second = 0.999
learn_rate = 0.06
norm_rate = 0.6
adam_eps = 1e-08
weight_decay = 0.01
ema_keep = 0.75


def normalize(values, gain, shift):
    center = values - jnp.mean(values, axis=-1, keepdims=True)
    spread = jnp.mean(center * center, axis=-1, keepdims=True)
    return center * lax.rsqrt(spread + layer_eps) * gain + shift


def cell_nll(logits, counts, library):
    gene_row_block = logits[CLASS_TOK:]
    log_expected_mean = jax.nn.log_softmax(gene_row_block[:, 0]) + jnp.log(
        library.astype(jnp.float32)
    )
    dispersion_shape = 0.5 + jax.nn.softplus(gene_row_block[:, 1])
    log_disp = jnp.log(dispersion_shape)
    zero_inflation_logit = gene_row_block[:, 2]
    log_mean_plus_dispersion = jnp.logaddexp(log_disp, log_expected_mean)
    observed_counts = counts.astype(jnp.float32)
    shared_tensors = dispersion_shape * (log_disp - log_mean_plus_dispersion)
    zero_count_term = jax.nn.softplus(-zero_inflation_logit) - jax.nn.softplus(
        shared_tensors - zero_inflation_logit
    )
    nonzero_count_term = (
        zero_inflation_logit
        + jax.nn.softplus(-zero_inflation_logit)
        - shared_tensors
        - observed_counts * (log_expected_mean - log_mean_plus_dispersion)
        - lax.lgamma(observed_counts + dispersion_shape)
        + lax.lgamma(dispersion_shape)
        + lax.lgamma(observed_counts + 1.0)
    )
    return jnp.mean(jnp.where(counts == 0, zero_count_term, nonzero_count_term))


def to_heads(block, head_dim):
    cell_count, length, local_width = block.shape
    per_cell = local_width // head_dim
    moved = block.reshape(cell_count, length, per_cell, head_dim).transpose(0, 2, 1, 3)
    return moved.reshape(cell_count * per_cell, length, head_dim)


def from_heads(block, cell_count):
    groups, length, head_dim = block.shape
    per_cell = groups // cell_count
    moved = block.reshape(cell_count, per_cell, length, head_dim).transpose(0, 2, 1, 3)
    return moved.reshape(cell_count, length, per_cell * head_dim)


def head_forward(query_rows, key_rows, value_rows):
    length, head_dim = query_rows.shape
    block_rows = length // QBLOCKS
    score_scale = head_dim ** (-0.5)

    def one_block(query_block):
        scores = (
            jnp.einsum("qd,kd->qk", query_block, key_rows, preferred_element_type=jnp.float32)
            * score_scale
        )
        row_max = jnp.max(scores, axis=-1, keepdims=True)
        exp_scores = jnp.exp(scores - row_max)
        row_total = jnp.sum(exp_scores, axis=-1, keepdims=True)
        weight_tensors = exp_scores / row_total
        head_out = jnp.dot(
            weight_tensors.astype(jnp.bfloat16), value_rows, preferred_element_type=jnp.float32
        )
        return (head_out, (row_max + jnp.log(row_total))[:, 0])

    outputs, log_total = lax.map(one_block, query_rows.reshape(QBLOCKS, block_rows, head_dim))
    return (outputs.reshape(length, head_dim), log_total.reshape(length))


def head_backward(query_rows, key_rows, value_rows, log_total, grad_rows):
    length, head_dim = query_rows.shape
    block_rows = length // QBLOCKS
    score_scale = head_dim ** (-0.5)

    def one_block(running, block_in):
        query_block, total_block, grad_block = block_in
        scores = (
            jnp.einsum("qd,kd->qk", query_block, key_rows, preferred_element_type=jnp.float32)
            * score_scale
        )
        weight_tensors = jnp.exp(scores - total_block[:, None])
        grad_weights = jnp.einsum(
            "qd,kd->qk", grad_block, value_rows, preferred_element_type=jnp.float32
        )
        row_inner = jnp.sum(weight_tensors * grad_weights, axis=-1, keepdims=True)
        grad_scores = (weight_tensors * (grad_weights - row_inner)).astype(jnp.bfloat16)
        grad_query = (
            jnp.dot(grad_scores, key_rows, preferred_element_type=jnp.float32) * score_scale
        )
        grad_key = (
            running[0]
            + jnp.einsum("qk,qd->kd", grad_scores, query_block, preferred_element_type=jnp.float32)
            * score_scale
        )
        grad_value = running[1] + jnp.einsum(
            "qk,qd->kd",
            weight_tensors.astype(jnp.bfloat16),
            grad_block,
            preferred_element_type=jnp.float32,
        )
        return ((grad_key, grad_value), grad_query)

    zero_rows = jnp.zeros((length, head_dim), jnp.float32)
    blocks_in = (
        query_rows.reshape(QBLOCKS, block_rows, head_dim),
        log_total.reshape(QBLOCKS, block_rows),
        grad_rows.reshape(QBLOCKS, block_rows, head_dim),
    )
    (grad_key, grad_value), grad_query = lax.scan(one_block, (zero_rows, zero_rows), blocks_in)
    return (grad_query.reshape(length, head_dim), grad_key, grad_value)


def adam_update(grad, first, second, weight, decay_rate, rate):
    first_new = decay_first * first + (1.0 - decay_first) * grad
    second_new = decay_second * second + (1.0 - decay_second) * grad * grad
    fix_first = 1.0 - decay_first**STEP
    fix_second = 1.0 - decay_second**STEP
    direction = first_new / fix_first / (jnp.sqrt(second_new / fix_second) + adam_eps)
    return (first_new, second_new, weight - rate * (direction + decay_rate * weight))


def average_update(average, weight_new, dim):
    count = average.shape[dim]
    piece = lax.dynamic_slice_in_dim(weight_new, lax.axis_index("wide") * count, count, dim)
    return ema_keep * average + (1.0 - ema_keep) * piece


def layer_pass(
    stream, gene_counts, library_size, in_low, out_low, up_low, down_low, norm_params, head_weight
):
    cell_count, length, model_width = stream.shape
    head_dim = D // HEADS
    normed_one = normalize(stream, norm_params[0], norm_params[1])
    first_act = normed_one.astype(jnp.bfloat16)
    joined = jnp.einsum(
        "cld,sde->scle", first_act, in_low, preferred_element_type=jnp.float32
    ).astype(jnp.bfloat16)
    query_heads = to_heads(joined[0], head_dim)
    key_heads = to_heads(joined[1], head_dim)
    value_heads = to_heads(joined[2], head_dim)
    head_out, log_total = lax.map(
        lambda trio: head_forward(trio[0], trio[1], trio[2]), (query_heads, key_heads, value_heads)
    )
    mixed_heads = from_heads(head_out, cell_count).astype(jnp.bfloat16)
    attended = lax.psum(
        jnp.einsum("cle,ed->cld", mixed_heads, out_low, preferred_element_type=jnp.float32),
        "narrow",
    )
    middle = stream + attended
    normed_two = normalize(middle, norm_params[2], norm_params[3])
    second_act = normed_two.astype(jnp.bfloat16)
    before = jnp.einsum("cld,df->clf", second_act, up_low, preferred_element_type=jnp.float32)
    hidden = jax.nn.gelu(before).astype(jnp.bfloat16)
    branch_two = jnp.einsum("clf,fd->cld", hidden, down_low, preferred_element_type=jnp.float32)
    branch_two = lax.psum(branch_two, "narrow")
    result = middle + branch_two

    def head_loss(incoming_rows, weight_tensors):
        logits = jnp.einsum(
            "mfg,ag->mfa",
            incoming_rows,
            weight_tensors,
            precision=TOP_PRECISION,
            preferred_element_type=jnp.float32,
        )
        return jnp.sum(jax.vmap(cell_nll)(logits, gene_counts, library_size))

    loss_value, pull_head = jax.vjp(head_loss, result, head_weight)
    grad_result, grad_head = pull_head(jnp.ones((), jnp.float32))
    result_low = grad_result.astype(jnp.bfloat16)
    grad_down = jnp.einsum("clf,cld->fd", hidden, result_low, preferred_element_type=jnp.float32)
    grad_hidden = jnp.einsum(
        "cld,fd->clf", result_low, down_low, preferred_element_type=jnp.float32
    )
    gelu_value, pull_gelu = jax.vjp(jax.nn.gelu, before)
    grad_before = pull_gelu(grad_hidden)[0].astype(jnp.bfloat16)
    grad_up = jnp.einsum("cld,clf->df", second_act, grad_before, preferred_element_type=jnp.float32)
    grad_normed_two = jnp.einsum(
        "clf,df->cld", grad_before, up_low, preferred_element_type=jnp.float32
    )
    grad_normed_two = lax.psum(grad_normed_two.astype(jnp.bfloat16), "narrow").astype(jnp.float32)
    norm_value_two, pull_two = jax.vjp(normalize, middle, norm_params[2], norm_params[3])
    back_middle, grad_gain_two, grad_shift_two = pull_two(grad_normed_two)
    grad_middle = grad_result + back_middle
    grad_norm_two = jnp.stack([grad_gain_two, grad_shift_two])
    middle_low = grad_middle.astype(jnp.bfloat16)
    grad_out = jnp.einsum(
        "cle,cld->ed", mixed_heads, middle_low, preferred_element_type=jnp.float32
    )
    grad_mixed = jnp.einsum(
        "cld,ed->cle", middle_low, out_low, preferred_element_type=jnp.float32
    ).astype(jnp.bfloat16)
    grad_query, grad_key, grad_value = lax.map(
        lambda packed: head_backward(packed[0], packed[1], packed[2], packed[3], packed[4]),
        (query_heads, key_heads, value_heads, log_total, to_heads(grad_mixed, head_dim)),
    )
    grad_joined = jnp.stack(
        [
            from_heads(grad_query, cell_count),
            from_heads(grad_key, cell_count),
            from_heads(grad_value, cell_count),
        ]
    ).astype(jnp.bfloat16)
    grad_in = jnp.einsum(
        "cld,scle->sde", first_act, grad_joined, preferred_element_type=jnp.float32
    )
    grad_normed_one = jnp.einsum(
        "scle,sde->cld", grad_joined, in_low, preferred_element_type=jnp.float32
    )
    grad_normed_one = lax.psum(grad_normed_one.astype(jnp.bfloat16), "narrow").astype(jnp.float32)
    norm_value_one, pull_one = jax.vjp(normalize, stream, norm_params[0], norm_params[1])
    back_stream, grad_gain_one, grad_shift_one = pull_one(grad_normed_one)
    input_grad = grad_middle + back_stream
    grad_norm_one = jnp.stack([grad_gain_one, grad_shift_one])
    grad_in, grad_out, grad_up, grad_down, grad_norm_one, grad_norm_two, grad_head = lax.psum(
        (grad_in, grad_out, grad_up, grad_down, grad_norm_one, grad_norm_two, grad_head), "wide"
    )
    return (
        result,
        input_grad,
        (grad_in, grad_out, grad_up, grad_down, grad_norm_one, grad_norm_two, grad_head),
    )


def on_device(
    cell_tokens,
    library_size,
    gene_counts,
    attend_in,
    attend_out,
    up_weight,
    down_weight,
    norm_params,
    head_weight,
    first_in,
    first_out,
    first_up,
    first_down,
    first_norm,
    first_head,
    second_in,
    second_out,
    second_up,
    second_down,
    second_norm,
    second_head,
    average_in,
    average_out,
    average_up,
    average_down,
    average_norm,
    average_head,
):
    stream = cell_tokens.astype(jnp.float32)
    in_low = attend_in.astype(jnp.bfloat16)
    out_low = attend_out.astype(jnp.bfloat16)
    up_low = up_weight.astype(jnp.bfloat16)
    down_low = down_weight.astype(jnp.bfloat16)
    result, input_grad, grads = layer_pass(
        stream,
        gene_counts,
        library_size,
        in_low,
        out_low,
        up_low,
        down_low,
        norm_params,
        head_weight,
    )
    grad_in, grad_out, grad_up, grad_down, grad_norm_one, grad_norm_two, grad_head = grads
    grad_norms = jnp.concatenate([grad_norm_one, grad_norm_two], axis=0)
    sharded_squares = (
        jnp.sum(grad_in * grad_in)
        + jnp.sum(grad_out * grad_out)
        + jnp.sum(grad_up * grad_up)
        + jnp.sum(grad_down * grad_down)
    )
    common_squares = jnp.sum(grad_norms * grad_norms) + jnp.sum(grad_head * grad_head)
    grad_norm = jnp.sqrt(lax.psum(sharded_squares, "narrow") + common_squares)
    output_rows = result.astype(jnp.bfloat16)
    factor = jnp.minimum(1.0, clip_limit / grad_norm)
    clipped_in = grad_in * factor
    first_in_new, second_in_new, weight_in_new = adam_update(
        clipped_in, first_in, second_in, attend_in, weight_decay, learn_rate
    )
    average_in_new = average_update(average_in, weight_in_new, 1)
    clipped_out = grad_out * factor
    first_out_new, second_out_new, weight_out_new = adam_update(
        clipped_out, first_out, second_out, attend_out, weight_decay, learn_rate
    )
    average_out_new = average_update(average_out, weight_out_new, 1)
    clipped_up = grad_up * factor
    first_up_new, second_up_new, weight_up_new = adam_update(
        clipped_up, first_up, second_up, up_weight, weight_decay, learn_rate
    )
    average_up_new = average_update(average_up, weight_up_new, 0)
    clipped_down = grad_down * factor
    first_down_new, second_down_new, weight_down_new = adam_update(
        clipped_down, first_down, second_down, down_weight, weight_decay, learn_rate
    )
    average_down_new = average_update(average_down, weight_down_new, 1)
    clipped_norm = grad_norms * factor
    first_norm_new, second_norm_new, weight_norm_new = adam_update(
        clipped_norm, first_norm, second_norm, norm_params, 0.0, norm_rate
    )
    average_norm_new = average_update(average_norm, weight_norm_new, 1)
    clipped_head = grad_head * factor
    first_head_new, second_head_new, weight_head_new = adam_update(
        clipped_head, first_head, second_head, head_weight, weight_decay, learn_rate
    )
    average_head_new = average_update(average_head, weight_head_new, 1)
    return (
        output_rows,
        input_grad,
        grad_norm,
        clipped_in,
        first_in_new,
        second_in_new,
        weight_in_new,
        average_in_new,
        clipped_out,
        first_out_new,
        second_out_new,
        weight_out_new,
        average_out_new,
        clipped_up,
        first_up_new,
        second_up_new,
        weight_up_new,
        average_up_new,
        clipped_down,
        first_down_new,
        second_down_new,
        weight_down_new,
        average_down_new,
        clipped_norm,
        first_norm_new,
        second_norm_new,
        weight_norm_new,
        average_norm_new,
        clipped_head,
        first_head_new,
        second_head_new,
        weight_head_new,
        average_head_new,
    )


def solution(mesh):
    placed = (
        P("wide", None, None),
        P("wide"),
        P("wide", None),
        P(None, None, "narrow"),
        P("narrow", None),
        P(None, "narrow"),
        P("narrow", None),
        P(),
        P(),
        P(None, None, "narrow"),
        P("narrow", None),
        P(None, "narrow"),
        P("narrow", None),
        P(),
        P(),
        P(None, None, "narrow"),
        P("narrow", None),
        P(None, "narrow"),
        P("narrow", None),
        P(),
        P(),
        P(None, "wide", "narrow"),
        P("narrow", "wide"),
        P("wide", "narrow"),
        P("narrow", "wide"),
        P(None, "wide"),
        P(None, "wide"),
    )
    return jax.shard_map(
        on_device,
        mesh=mesh,
        in_specs=placed,
        out_specs=(
            P("wide", None, None),
            P("wide", None, None),
            P(),
            P(None, None, "narrow"),
            P(None, None, "narrow"),
            P(None, None, "narrow"),
            P(None, None, "narrow"),
            P(None, "wide", "narrow"),
            P("narrow", None),
            P("narrow", None),
            P("narrow", None),
            P("narrow", None),
            P("narrow", "wide"),
            P(None, "narrow"),
            P(None, "narrow"),
            P(None, "narrow"),
            P(None, "narrow"),
            P("wide", "narrow"),
            P("narrow", None),
            P("narrow", None),
            P("narrow", None),
            P("narrow", None),
            P("narrow", "wide"),
            P(),
            P(),
            P(),
            P(),
            P(None, "wide"),
            P(),
            P(),
            P(),
            P(),
            P(None, "wide"),
        ),
        check_vma=False,
    )
```

profile of v0, /device:TPU:0, one launch (start us, length us, event | category | flops | bytes accessed | tf_op | source)
XLA Modules:
  0.0 1007.0 jit_solution(9720439106060249476)
XLA Ops:
  7.3 1.5 fusion.160
  8.8 3.6 convert_reduce_fusion.2
  12.4 4.3 fusion.44
  16.7 3.6 fusion.50
  20.4 1.9 slice_bitcast_fusion
  22.3 3.7 copy.64
  26.0 3.7 copy.63
  29.7 3.7 copy.62
  33.4 85.2 %while.54 = (s32[]{:T(128)}, bf16[4,2208,64]{2,1,0:T(8,128)(2,1)S(1)}, f32[4,2208]{1,0:T(4,128)}, bf16[4,2208,64]{2,1,0:T(8,128)(2,1)}, bf16[4,2208,64]{2,1,0:T(...) while((s32[]{:T(128)}, ...), condition=%wide.region_7.8_spmd, body=%wide.region_2.7_spmd.sunk | while | flops 320548064 | bytes 23122368 | solution.py:165
  34.6 2.1 dynamic-slice_bitcast_fusion.7
  36.7 15.2 %while.57 = (s32[]{:T(128)}, bf16[4,552,64]{1,2,0:T(8,128)(2,1)}, f32[4,552]{1,0:T(4,128)S(1)}, bf16[4,552,64]{2,1,0:T(8,128)(2,1)S(1)}, bf16[2208,64]{1,0:T(8,1...) while((s32[]{:T(128)}, bf16[4,552,64]{1,2,0:T(8,128)(2,1)}, f32[4,552]{1,0:T(4,128)S(1)}, ...), condition=%wide.region_6.6_spmd, body=%wide.region_3.5_spmd.sunk | while | flops 320548064 | bytes 19695356 | solution.py:90
  51.9 1.4 dynamic_update_slice.43
  55.9 2.1 dynamic-slice_bitcast_fusion.7
  58.0 15.2 %while.57 = (s32[]{:T(128)}, bf16[4,552,64]{1,2,0:T(8,128)(2,1)}, f32[4,552]{1,0:T(4,128)S(1)}, bf16[4,552,64]{2,1,0:T(8,128)(2,1)S(1)}, bf16[2208,64]{1,0:T(8,1...) while((s32[]{:T(128)}, bf16[4,552,64]{1,2,0:T(8,128)(2,1)}, f32[4,552]{1,0:T(4,128)S(1)}, ...), condition=%wide.region_6.6_spmd, body=%wide.region_3.5_spmd.sunk | while | flops 320548064 | bytes 19695356 | solution.py:90
  73.2 1.4 dynamic_update_slice.43
  77.2 2.1 dynamic-slice_bitcast_fusion.7
  79.3 15.2 %while.57 = (s32[]{:T(128)}, bf16[4,552,64]{1,2,0:T(8,128)(2,1)}, f32[4,552]{1,0:T(4,128)S(1)}, bf16[4,552,64]{2,1,0:T(8,128)(2,1)S(1)}, bf16[2208,64]{1,0:T(8,1...) while((s32[]{:T(128)}, bf16[4,552,64]{1,2,0:T(8,128)(2,1)}, f32[4,552]{1,0:T(4,128)S(1)}, ...), condition=%wide.region_6.6_spmd, body=%wide.region_3.5_spmd.sunk | while | flops 320548064 | bytes 19695356 | solution.py:90
  94.6 1.4 dynamic_update_slice.43
  98.5 2.1 dynamic-slice_bitcast_fusion.7
  100.6 15.2 %while.57 = (s32[]{:T(128)}, bf16[4,552,64]{1,2,0:T(8,128)(2,1)}, f32[4,552]{1,0:T(4,128)S(1)}, bf16[4,552,64]{2,1,0:T(8,128)(2,1)S(1)}, bf16[2208,64]{1,0:T(8,1...) while((s32[]{:T(128)}, bf16[4,552,64]{1,2,0:T(8,128)(2,1)}, f32[4,552]{1,0:T(4,128)S(1)}, ...), condition=%wide.region_6.6_spmd, body=%wide.region_3.5_spmd.sunk | while | flops 320548064 | bytes 19695356 | solution.py:90
  115.9 1.4 dynamic_update_slice.43
  118.7 4.9 fusion.68
  123.9 166.0 %all-reduce.12.cloned.1.call-done = f32[4,2208,256]{2,1,0:T(8,128)} async-done(((f32[4,2208,256]{2,1,0:T(8,128)}), f32[4,2208,256]{2,1,0:T(8,128)}) %all-reduce.12.cloned.1.call-update) | async-done | bytes 9043984 | tf_op jit(solution)/shard_map/psum | solution.py:169
  289.9 9.7 fusion.157
  299.7 5.8 multiply_reduce_fusion.1
  305.9 2.6 fusion.82
  308.4 3.5 copy-done.11
  312.0 5.2 fusion.79
  317.8 163.1 %all-reduce.14.cloned.1.call-done = f32[4,2208,256]{2,1,0:T(8,128)} async-done(((f32[4,2208,256]{2,1,0:T(8,128)}), f32[4,2208,256]{2,1,0:T(8,128)}) %all-reduce.14.cloned.1.call-update) | async-done | bytes 9043984 | tf_op jit(solution)/shard_map/psum | solution.py:179
  480.9 9.5 fusion.156
  490.5 7.7 fusion.139
  500.5 8.9 fusion.85
  509.4 10.9 %fusion.43 = bf16[4,2208,256]{2,1,0:T(8,128)(2,1)S(1)} fusion(f32[4,2208,256]{2,1,0:T(8,128)} %copy-done.11, f32[4,2208,256]{2,1,0:T(8,128)S(1)} %fusion.85, f32[256,256]{1,0:T(8,128)S(1)} %copy-done.35), kind=kOutput, calls=%fused_computation.79 | convolution fusion | flops 1205174272 | bytes 22872064 | tf_op jit(solution)/shard_map/cld,fd->clf/dot_general | solution.py:196
  520.4 2.1 copy-done.10
  522.4 3.5 convolution_convert_fusion
  526.0 10.3 %convolution_bitcast_fusion = f32[256,256]{1,0:T(8,128)} fusion(bf16[4,2208,256]{2,1,0:T(8,128)(2,1)} %copy-done.10, f32[4,2208,256]{2,1,0:T(8,128)} %get-tuple-element.385, f32[256]{0:T(256)S(1)} %bitcast.236, f32[256]{0:T(256)S(1)} %bitcast.226, f32[4,2208]{1,0:T(4,128)S(1)} %fusion.133, f32[4,2208]{1,0:T(4,128)S(1)} %broadcast_multiply_fusion.4), kind=kOutput, calls=%fused_computation.111 | convolution fusion | flops 1168932864 | bytes 13900800 | tf_op jit(solution)/shard_map/cld,clf->df/dot_general | solution.py:201
  536.3 6.6 fusion.61
  542.9 74.2 %all-reduce.16.cloned.1.call-done = bf16[4,2208,256]{2,1,0:T(8,128)(2,1)} async-done(((bf16[4,2208,256]{2,1,0:T(8,128)(2,1)}), bf16[4,2208,256]{2,1,0:T(8,128)(2,1)}) %all-reduce.16.cloned.1.call-update) | async-done | bytes 4522000 | tf_op jit(solution)/shard_map/psum | solution.py:205
  617.0 6.5 fusion.36
  623.6 9.0 fusion.46
  632.6 7.9 add_add_fusion.3
  640.6 2.0 fusion.70
  642.6 2.4 convolution_convert_fusion.2
  645.1 117.7 %while.56 = (s32[]{:T(128)}, bf16[4,2208,64]{1,2,0:T(8,128)(2,1)}, bf16[4,2208,64]{1,2,0:T(8,128)(2,1)}, bf16[4,2208,64]{1,2,0:T(8,128)(2,1)}, bf16[4,2208,64]{2...) while((s32[]{:T(128)}, bf16[4,2208,64]{1,2,0:T(8,128)(2,1)}, ...), condition=%wide.region_22.23_spmd, body=%wide.region_18.22_spmd.sunk | while | flops 790534144 | bytes 51089484 | solution.py:217
  650.9 20.7 %while.58 = (s32[]{:T(128)}, f32[2208,64]{0,1:T(8,128)S(1)}, f32[2208,64]{0,1:T(8,128)S(1)}, bf16[4,552,64]{1,2,0:T(8,128)(2,1)}, bf16[4,552,64]{2,1,0:T(8,128)(...) while((s32[]{:T(128)}, f32[2208,64]{0,1:T(8,128)S(1)}, ...), condition=%wide.region_21.21_spmd.clone, body=%wide.region_19.20_spmd.clone.sunk | while | flops 790534144 | bytes 44209484 | solution.py:133
  680.2 20.7 %while.58 = (s32[]{:T(128)}, f32[2208,64]{0,1:T(8,128)S(1)}, f32[2208,64]{0,1:T(8,128)S(1)}, bf16[4,552,64]{1,2,0:T(8,128)(2,1)}, bf16[4,552,64]{2,1,0:T(8,128)(...) while((s32[]{:T(128)}, f32[2208,64]{0,1:T(8,128)S(1)}, ...), condition=%wide.region_21.21_spmd.clone, body=%wide.region_19.20_spmd.clone.sunk | while | flops 790534144 | bytes 44209484 | solution.py:133
  709.6 20.7 %while.58 = (s32[]{:T(128)}, f32[2208,64]{0,1:T(8,128)S(1)}, f32[2208,64]{0,1:T(8,128)S(1)}, bf16[4,552,64]{1,2,0:T(8,128)(2,1)}, bf16[4,552,64]{2,1,0:T(8,128)(...) while((s32[]{:T(128)}, f32[2208,64]{0,1:T(8,128)S(1)}, ...), condition=%wide.region_21.21_spmd.clone, body=%wide.region_19.20_spmd.clone.sunk | while | flops 790534144 | bytes 44209484 | solution.py:133
  738.9 20.7 %while.58 = (s32[]{:T(128)}, f32[2208,64]{0,1:T(8,128)S(1)}, f32[2208,64]{0,1:T(8,128)S(1)}, bf16[4,552,64]{1,2,0:T(8,128)(2,1)}, bf16[4,552,64]{2,1,0:T(8,128)(...) while((s32[]{:T(128)}, f32[2208,64]{0,1:T(8,128)S(1)}, ...), condition=%wide.region_21.21_spmd.clone, body=%wide.region_19.20_spmd.clone.sunk | while | flops 790534144 | bytes 44209484 | solution.py:133
  762.9 6.7 fusion.64
  769.7 4.8 bitcast_convert_fusion
  774.9 6.3 convolution_bitcast_fusion.1
  781.2 63.9 %all-reduce.20.cloned.1.call-done = (f32[3,256,64]{1,2,0:T(8,128)}, f32[64,256]{1,0:T(8,128)}, f32[256,256]{1,0:T(8,128)}, f32[256,256]{1,0:T(8,128)}) async-done(((f32[3,256,64]{1,2,0:T(8,128)}, f32[64,256]{1,0:T(8,128)}, f32[256,256]{1,0:T(8,128)}, f32[256,256]{1,0:T(8,128)}), (f32[3,256,64]{1,2,0:T(8,128)}, f32[64,256]{1,0:T(8,128)}, f32[256,256]{1,0:T(8,128)}, ...) | async-done | bytes 786448 | tf_op jit(solution)/shard_map/psum | solution.py:239
  845.1 1.5 multiply_reduce_fusion.5
  846.5 1.6 multiply_reduce_fusion.4
  849.4 1.6 multiply_reduce_fusion.3
  851.7 1.7 multiply_reduce_fusion.2
  854.1 7.0 psum.92
  861.2 76.2 %all-reduce.18.cloned.1.call-done = bf16[4,2208,256]{2,1,0:T(8,128)(2,1)} async-done(((bf16[4,2208,256]{2,1,0:T(8,128)(2,1)}), bf16[4,2208,256]{2,1,0:T(8,128)(2,1)}) %all-reduce.18.cloned.1.call-update) | async-done | bytes 4522000 | tf_op jit(solution)/shard_map/psum | solution.py:234
  937.4 5.6 fusion.45
  943.1 7.4 fusion.47
  950.5 21.7 %all-reduce.4 = (f32[2,256]{1,0:T(2,128)S(1)}, f32[2,256]{1,0:T(2,128)S(1)}, f32[3,256]{1,0:T(4,128)S(1)}) all-reduce(f32[2,256]{1,0:T(2,128)S(1)} %pad_maximum_fusion.7, f32[2,256]{1,0:T(2,128)S(1)} %pad_maximum_fusion.6, f32[3,256]{1,0:T(4,128)S(1)} %convolution_bitcast_fusion.1), channel_id=1, replica_groups=mesh['wide'=8,'narrow'=4] {'wide'}, use_global_device_ids=true, to_apply=%region_40.41 | all-reduce | flops 1792 | bytes 14336 | tf_op jit(solution)/shard_map/psum | solution.py:239
  975.4 1.5 multiply_subtract_fusion.3
  977.7 1.8 multiply_subtract_fusion.2
  988.5 10.2 %add_add_fusion.2 = f32[4,2208,256]{2,1,0:T(8,128)} fusion(f32[4,2208,256]{2,1,0:T(8,128)} %copy-done.2, bf16[4,2208,256]{2,1,0:T(8,128)(2,1)} %param.35, bf16[4,2208,256]{2,1,0:T(8,128)(2,1)} %all-reduce.18.cloned.1.call-done, f32[4,2208]{1,0:T(4,128)S(1)} %negate_multiply_fusion, f32[4,2208]{1,0:T(4,128)S(1)} %multiply_multiply_fusion.6, ...), kind=kLoop, calls=%fused_computation.85 | loop fusion | flops 22609920 | bytes 27274240 | tf_op jit(solution)/shard_map/add | solution.py:237
  (633 shorter events, 201.4 us)
Async XLA Ops:
  7.2 9.5 copy-start.42
  7.2 282.7 %all-reduce.12.cloned.1.call-start = ((), (), s32[]{:S(2)}) async-start(), calls=%async_computation | async-start | bytes 18087936 | tf_op jit(solution)/shard_map/psum | solution.py:169
  7.3 9.4 copy-start.1
  8.8 11.6 %copy-start.55 = (f32[1,256]{1,0:T(1,128)}, f32[1,256]{1,0:T(1,128)S(1)}, u32[]{:S(2)}) copy-start(f32[1,256]{1,0:T(1,128)S(1)} %get-tuple-element.404) | copy-start | bytes 3076
  8.8 11.6 %copy-start.64 = (f32[1,256]{1,0:T(1,128)}, f32[1,256]{1,0:T(1,128)S(1)}, u32[]{:S(2)}) copy-start(f32[1,256]{1,0:T(1,128)S(1)} %get-tuple-element.403) | copy-start | bytes 3076
  12.4 8.0 copy-start.22
  33.4 85.2 %copy-start.25 = (f32[64,256]{1,0:T(8,128)S(1)}, f32[64,256]{1,0:T(8,128)}, u32[]{:S(2)}) copy-start(f32[64,256]{1,0:T(8,128)} %param.39) | copy-start | bytes 196612
  123.6 357.3 %all-reduce.14.cloned.1.call-start = ((), (), s32[]{:S(2)}) async-start(), calls=%async_computation.1 | async-start | bytes 18087936 | tf_op jit(solution)/shard_map/psum | solution.py:179
  289.9 15.6 %copy-start.16 = (f32[256,256]{1,0:T(8,128)S(1)}, f32[256,256]{1,0:T(8,128)}, u32[]{:S(2)}) copy-start(f32[256,256]{1,0:T(8,128)} %param.40) | copy-start | bytes 786436
  299.7 6.2 copy-start
  299.7 6.2 copy-start.49
  299.7 6.2 copy-start.57
  305.9 6.1 copy-start.34
  317.1 299.9 %all-reduce.16.cloned.1.call-start = ((), (), s32[]{:S(2)}) async-start(), calls=%async_computation.2 | async-start | bytes 9043968 | tf_op jit(solution)/shard_map/psum | solution.py:205
  317.8 172.7 %copy-start.50 = (f32[3,256]{1,0:T(4,128)S(1)}, f32[3,256]{1,0:T(4,128)}, u32[]{:S(2)}) copy-start(f32[3,256]{1,0:T(4,128)} %param.43) | copy-start | bytes 9220
  490.5 19.0 %copy-start.3 = (f32[4,2208,256]{2,1,0:T(8,128)}, f32[4,2208,256]{2,1,0:T(8,128)S(1)}, u32[]{:S(2)}) copy-start(f32[4,2208,256]{2,1,0:T(8,128)S(1)} %get-tuple-element.383) | copy-start | bytes 27131908
  490.5 8.3 copy-start.46
  490.5 18.9 %copy-start.35 = (f32[256,256]{1,0:T(8,128)S(1)}, f32[256,256]{1,0:T(8,128)}, u32[]{:S(2)}) copy-start(f32[256,256]{1,0:T(8,128)} %param.41) | copy-start | bytes 786436
  500.5 19.8 %copy-start.18 = (f32[4,2200,3]{1,2,0:T(4,128)}, f32[4,2200,3]{1,2,0:T(4,128)S(1)}, u32[]{:S(2)}) copy-start(f32[4,2200,3]{1,2,0:T(4,128)S(1)} %copy.120) | copy-start | bytes 316804
  509.4 10.9 %copy-start.6 = (f32[4,2208,256]{2,1,0:T(8,128)}, f32[4,2208,256]{2,1,0:T(8,128)S(1)}, u32[]{:S(2)}) copy-start(f32[4,2208,256]{2,1,0:T(8,128)S(1)} %fusion.85) | copy-start | bytes 27131908
  525.9 319.2 %all-reduce.20.cloned.1.call-start = ((), (), s32[]{:S(2)}) async-start(), calls=%async_computation.4 | async-start | bytes 1572864 | tf_op jit(solution)/shard_map/psum | solution.py:239
  526.0 10.3 %copy-start.7 = (f32[4,2208,256]{2,1,0:T(8,128)S(1)}, f32[4,2208,256]{2,1,0:T(8,128)}, u32[]{:S(2)}) copy-start(f32[4,2208,256]{2,1,0:T(8,128)} %copy-done.6) | copy-start | bytes 27131908
  617.0 6.6 copy-start.5
  617.0 15.6 %slice-start = ((s8[9043968]{0:T(1024)(128)(4,1)}), s8[4194304]{0:T(1024)(128)(4,1)S(1)}, s32[]{:S(2)}) async-start(s8[9043968]{0:T(1024)(128)(4,1)} %bitcast.218), calls=%async_computation.5 | async-start | bytes 8388608
  617.0 15.6 %slice-start.1 = ((s8[9043968]{0:T(1024)(128)(4,1)}), s8[655360]{0:T(1024)(128)(4,1)S(1)}, s32[]{:S(2)}) async-start(s8[9043968]{0:T(1024)(128)(4,1)} %bitcast.218), calls=%async_computation.6 | async-start | bytes 1310720
  623.5 9.1 copy-start.8
  623.6 9.0 slice-start.2
  645.1 117.8 %copy-start.23 = (f32[4,2208]{1,0:T(4,128)S(1)}, f32[4,2208]{1,0:T(4,128)}, u32[]{:S(2)}) copy-start(f32[4,2208]{1,0:T(4,128)} %copy-done.22) | copy-start | bytes 105988
  645.1 117.8 %copy-start.30 = (f32[4,2208]{1,0:T(4,128)S(1)}, f32[4,2208]{1,0:T(4,128)}, u32[]{:S(2)}) copy-start(f32[4,2208]{1,0:T(4,128)} %copy-done.29) | copy-start | bytes 105988
  645.1 117.8 %copy-start.56 = (f32[1,256]{1,0:T(1,128)S(1)}, f32[1,256]{1,0:T(1,128)}, u32[]{:S(2)}) copy-start(f32[1,256]{1,0:T(1,128)} %copy-done.55) | copy-start | bytes 3076
  645.1 117.8 %copy-start.65 = (f32[1,256]{1,0:T(1,128)S(1)}, f32[1,256]{1,0:T(1,128)}, u32[]{:S(2)}) copy-start(f32[1,256]{1,0:T(1,128)} %copy-done.64) | copy-start | bytes 3076
  762.8 6.8 copy-start.43
  762.9 6.8 copy-start.66
  762.9 6.8 copy-start.67
  769.6 5.1 copy-start.52
  769.6 5.2 copy-start.19
  769.6 167.7 %all-reduce.18.cloned.1.call-start = ((), (), s32[]{:S(2)}) async-start(), calls=%async_computation.3 | async-start | bytes 9043968 | tf_op jit(solution)/shard_map/psum | solution.py:234
  774.5 79.5 %copy-start.60 = (f32[256]{0:T(256)S(1)}, f32[256]{0:T(256)}, u32[]{:S(2)}) copy-start(f32[256]{0:T(256)} %get-tuple-element.280) | copy-start | bytes 3076
  774.5 79.6 %copy-start.61 = (f32[256]{0:T(256)S(1)}, f32[256]{0:T(256)}, u32[]{:S(2)}) copy-start(f32[256]{0:T(256)} %get-tuple-element.285) | copy-start | bytes 3076
  774.8 168.1 %copy-start.32 = (f32[4,2208]{1,0:T(4,128)S(1)}, f32[4,2208]{1,0:T(4,128)}, u32[]{:S(2)}) copy-start(f32[4,2208]{1,0:T(4,128)} %copy-done.31) | copy-start | bytes 105988
  861.0 114.4 %copy-start.26 = (f32[64,256]{1,0:T(8,128)S(1)}, f32[64,256]{1,0:T(8,128)}, u32[]{:S(2)}) copy-start(f32[64,256]{1,0:T(8,128)} %param.39) | copy-start | bytes 196612
  861.1 114.4 %copy-start.41 = (f32[64,256]{1,0:T(8,128)S(1)}, f32[64,256]{1,0:T(8,128)}, u32[]{:S(2)}) copy-start(f32[64,256]{1,0:T(8,128)} %get-tuple-element.350) | copy-start | bytes 196612
  861.1 114.4 %copy-start.47 = (f32[64,256]{1,0:T(8,128)S(1)}, f32[64,256]{1,0:T(8,128)}, u32[]{:S(2)}) copy-start(f32[64,256]{1,0:T(8,128)} %param.51) | copy-start | bytes 196612
  861.1 116.7 %copy-start.24 = (f32[3,256,64]{1,2,0:T(8,128)S(1)}, f32[3,256,64]{1,2,0:T(8,128)}, u32[]{:S(2)}) copy-start(f32[3,256,64]{1,2,0:T(8,128)} %get-tuple-element.349) | copy-start | bytes 589828
  861.1 116.7 %copy-start.44 = (f32[3,256,64]{1,2,0:T(8,128)S(1)}, f32[3,256,64]{1,2,0:T(8,128)}, u32[]{:S(2)}) copy-start(f32[3,256,64]{1,2,0:T(8,128)} %param.50) | copy-start | bytes 589828
  861.1 119.3 %copy-start.17 = (f32[256,256]{1,0:T(8,128)S(1)}, f32[256,256]{1,0:T(8,128)}, u32[]{:S(2)}) copy-start(f32[256,256]{1,0:T(8,128)} %param.40) | copy-start | bytes 786436
  861.1 119.3 %copy-start.20 = (f32[256,256]{1,0:T(8,128)S(1)}, f32[256,256]{1,0:T(8,128)}, u32[]{:S(2)}) copy-start(f32[256,256]{1,0:T(8,128)} %get-tuple-element.351) | copy-start | bytes 786436
  861.1 119.2 %copy-start.21 = (f32[256,256]{1,0:T(8,128)S(1)}, f32[256,256]{1,0:T(8,128)}, u32[]{:S(2)}) copy-start(f32[256,256]{1,0:T(8,128)} %get-tuple-element.352) | copy-start | bytes 786436
  861.1 119.2 %copy-start.36 = (f32[256,256]{1,0:T(8,128)S(1)}, f32[256,256]{1,0:T(8,128)}, u32[]{:S(2)}) copy-start(f32[256,256]{1,0:T(8,128)} %param.41) | copy-start | bytes 786436
  861.1 119.2 %copy-start.37 = (f32[256,256]{1,0:T(8,128)S(1)}, f32[256,256]{1,0:T(8,128)}, u32[]{:S(2)}) copy-start(f32[256,256]{1,0:T(8,128)} %param.53) | copy-start | bytes 786436
  861.1 119.2 %copy-start.38 = (f32[256,256]{1,0:T(8,128)S(1)}, f32[256,256]{1,0:T(8,128)}, u32[]{:S(2)}) copy-start(f32[256,256]{1,0:T(8,128)} %param.47) | copy-start | bytes 786436
  861.1 119.2 %copy-start.39 = (f32[256,256]{1,0:T(8,128)S(1)}, f32[256,256]{1,0:T(8,128)}, u32[]{:S(2)}) copy-start(f32[256,256]{1,0:T(8,128)} %param.52) | copy-start | bytes 786436
  861.1 119.2 %copy-start.40 = (f32[256,256]{1,0:T(8,128)S(1)}, f32[256,256]{1,0:T(8,128)}, u32[]{:S(2)}) copy-start(f32[256,256]{1,0:T(8,128)} %param.46) | copy-start | bytes 786436
  937.4 5.7 copy-start.4
  943.0 39.6 %copy-start.51 = (f32[3,256]{1,0:T(4,128)S(1)}, f32[3,256]{1,0:T(4,128)}, u32[]{:S(2)}) copy-start(f32[3,256]{1,0:T(4,128)} %param.43) | copy-start | bytes 9220
  943.0 39.6 %copy-start.62 = (f32[3,256]{1,0:T(4,128)S(1)}, f32[3,256]{1,0:T(4,128)}, u32[]{:S(2)}) copy-start(f32[3,256]{1,0:T(4,128)} %param.55) | copy-start | bytes 9220
  943.0 39.6 %copy-start.63 = (f32[3,256]{1,0:T(4,128)S(1)}, f32[3,256]{1,0:T(4,128)}, u32[]{:S(2)}) copy-start(f32[3,256]{1,0:T(4,128)} %param.49) | copy-start | bytes 9220
  943.0 41.5 %copy-start.54 = (f32[4,256]{1,0:T(4,128)S(1)}, f32[4,256]{1,0:T(4,128)}, u32[]{:S(2)}) copy-start(f32[4,256]{1,0:T(4,128)} %param.42) | copy-start | bytes 12292
  977.0 21.8 %copy-start.45 = (f32[64,256]{1,0:T(8,128)}, f32[64,256]{1,0:T(8,128)S(1)}, u32[]{:S(2)}) copy-start(f32[64,256]{1,0:T(8,128)S(1)} %get-tuple-element.369) | copy-start | bytes 196612
  979.5 19.3 %copy-start.28 = (f32[3,256,64]{1,2,0:T(8,128)}, f32[3,256,64]{1,2,0:T(8,128)S(1)}, u32[]{:S(2)}) copy-start(f32[3,256,64]{1,2,0:T(8,128)S(1)} %get-tuple-element.373) | copy-start | bytes 589828
  981.7 17.1 %copy-start.27 = (f32[256,256]{1,0:T(8,128)}, f32[256,256]{1,0:T(8,128)S(1)}, u32[]{:S(2)}) copy-start(f32[256,256]{1,0:T(8,128)S(1)} %get-tuple-element.361) | copy-start | bytes 786436
  981.7 17.1 %copy-start.33 = (f32[256,256]{1,0:T(8,128)}, f32[256,256]{1,0:T(8,128)S(1)}, u32[]{:S(2)}) copy-start(f32[256,256]{1,0:T(8,128)S(1)} %get-tuple-element.406) | copy-start | bytes 786436
  983.2 15.7 %copy-start.58 = (f32[3,256]{1,0:T(4,128)}, f32[3,256]{1,0:T(4,128)S(1)}, u32[]{:S(2)}) copy-start(f32[3,256]{1,0:T(4,128)S(1)} %get-tuple-element.353) | copy-start | bytes 9220
  985.8 13.0 %copy-start.59 = (f32[4,256]{1,0:T(4,128)}, f32[4,256]{1,0:T(4,128)S(1)}, u32[]{:S(2)}) copy-start(f32[4,256]{1,0:T(4,128)S(1)} %get-tuple-element.357) | copy-start | bytes 12292
  (88 other events, 128.8 us)
Sparse Core Ops, SparseCore 0:
  123.7 166.1 all-reduce.11
  317.3 163.5 all-reduce.13
  526.0 90.9 all-reduce.15
  769.7 75.3 all-reduce.19
  847.3 90.0 all-reduce.17
where the time goes:
time: 1020 us; the launch traced here: 1010 us
  waiting for transfers between devices  544 us (53%)
  matrix products  193 us (19%)
  other arithmetic  122 us (12%)
  local copies, waits for them, and re-layouts  95.3 us (9%)
  blocking collectives  28.6 us (3%)
  between operations  21.1 us (2%)
    psum x1, waiting for transfers between devices, layer_pass(): lax.psum(jnp.einsum('cle,ed->cld', mixed_heads, out_low, preferred_elemen...  166 us
    psum x1, waiting for transfers between devices, layer_pass(): branch_two = lax.psum(branch_two, 'narrow')  163 us
    psum x1, waiting for transfers between devices, layer_pass(): lax.psum(grad_normed_one.astype(jnp.bfloat16), 'narrow').astype(jnp.float32)  76.2 us
    psum x1, waiting for transfers between devices, layer_pass(): lax.psum(grad_normed_two.astype(jnp.bfloat16), 'narrow').astype(jnp.float32)  74.2 us
    psum x1, waiting for transfers between devices, layer_pass(): lax.psum((grad_in, grad_out, grad_up, grad_down, grad_norm_one, grad_norm...  63.9 us
    dot_general x32, matrix products, one_block(): jnp.einsum('qd,kd->qk', query_block, key_rows, preferred_element_type=jnp...  36.6 us
    reduce_sum x4, other arithmetic, normalize(): return center * lax.rsqrt(spread + layer_eps) * gain + shift  28.4 us
    dot_general x3, matrix products, head_loss(): jnp.einsum('mfg,ag->mfa', incoming_rows, weight_tensors, precision=TOP_PR...  22.9 us
  transfers between devices with their start and end apart: 5, of which 5 were waited for; matrix products, arithmetic and copies ran while one was open for 3% of the time, Pallas kernels for 0%

commit v1 on v0

v1 whole, which is shorter than its diff:
```python
import functools

import jax
import jax.numpy as jnp
from jax import lax
from jax.experimental import pallas as pl
from jax.experimental.pallas import tpu as pltpu
from jax.sharding import PartitionSpec as P

D = 256
FF = 1024
HEADS = 4
HEAD_DIM = 64
CLASS_TOK = 8
STEP = 10

layer_eps = 1e-05
clip_limit = 0.25
decay_first = 0.9
decay_second = 0.999
learn_rate = 0.06
norm_rate = 0.6
adam_eps = 1e-08
weight_decay = 0.01
ema_keep = 0.75

f32 = jnp.float32
bf16 = jnp.bfloat16
HI = lax.Precision.HIGHEST

NN = (((1,), (0,)), ((), ()))
NT = (((1,), (1,)), ((), ()))
TN = (((0,), (0,)), ((), ()))

BLK = 256
PAIR = 2 * HEAD_DIM
WIDE_COLS = 2 * BLK
LOG2E = 1.4426950408889634
SCORE = LOG2E * HEAD_DIM ** (-0.5)
GELU_A = 0.7978845608028654
GELU_B = 0.044715
VMEM_BYTES = 60 * 2**20


def dot(left, right, dims=NN, precision=None):
    return lax.dot_general(left, right, dims, precision=precision, preferred_element_type=f32)


def ceil_to(value, unit):
    return -(-value // unit) * unit


def key_chunk(length):
    for rows in (368, 384, 256, 128, 64, 48, 32, 16):
        if length % rows == 0:
            return rows
    return length


def vmem(count):
    return [pl.BlockSpec(memory_space=pltpu.VMEM)] * count


def params():
    return pltpu.CompilerParams(vmem_limit_bytes=VMEM_BYTES)


def norm_parts(values):
    center = values - jnp.mean(values, axis=-1, keepdims=True)
    spread = jnp.mean(center * center, axis=-1, keepdims=True)
    inverse = lax.rsqrt(spread + layer_eps)
    return center * inverse, inverse


def norm_back(xhat, inverse, gain, grad):
    scaled = gain * grad
    mean_one = jnp.mean(scaled, axis=-1, keepdims=True)
    mean_two = jnp.mean(scaled * xhat, axis=-1, keepdims=True)
    return inverse * (scaled - mean_one - xhat * mean_two)


def row_sums(values):
    return jnp.sum(values.reshape(-1, 8, values.shape[-1]), axis=0)


def block_of(step, width=BLK):
    return pl.ds(pl.multiple_of(step * width, width), width)


def front_kernel(length, tok, w_in, w_in_t, npar, x1, k_nat, v_nat, q_nat, q_t, k_t, out_t, lse, xbuf, v_t, probs, qbd, sem):
    padded = x1.shape[0]
    blocks = padded // BLK
    rows = key_chunk(length)
    me = lax.axis_index("narrow")
    copy = pltpu.make_async_copy(tok.at[me], xbuf.at[pl.ds(0, length)], sem)
    copy.start()
    if padded > length:
        xbuf[length:, :] = jnp.zeros((padded - length, D), bf16)
        probs[length:, :] = jnp.zeros((padded - length, WIDE_COLS), bf16)
    qbd[...] = jnp.zeros(qbd.shape, bf16)
    lse[...] = jnp.zeros(lse.shape, f32)
    copy.wait()
    gain = npar[0:1, :]
    shift = npar[1:2, :]

    @pl.loop(0, blocks)
    def project(step):
        here = block_of(step)
        xhat, _ = norm_parts(xbuf[here, :].astype(f32))
        act = (xhat * gain + shift).astype(bf16)
        x1[here, :] = act
        q_nat[here, :] = dot(act, w_in[0]).astype(bf16)
        k_nat[here, :] = dot(act, w_in[1]).astype(bf16)
        v_nat[here, :] = dot(act, w_in[2]).astype(bf16)
        q_t[:, here] = dot(w_in_t[0], act, NT).astype(bf16)
        k_t[:, here] = dot(w_in_t[1], act, NT).astype(bf16)
        v_t[:, here] = dot(w_in_t[2], act, NT).astype(bf16)

    if padded > length:
        v_t[:, length:] = jnp.zeros((D, padded - length), bf16)

    def attend(shifted):
        for pair in range(HEADS // 2):
            low = pair * PAIR

            @pl.loop(0, blocks)
            def block(step):
                here = block_of(step)
                qbd[0:HEAD_DIM, 0:BLK] = q_t[low : low + HEAD_DIM, here]
                qbd[HEAD_DIM:PAIR, BLK:WIDE_COLS] = q_t[low + HEAD_DIM : low + PAIR, here]
                queries = qbd[...]

                def scores(start):
                    return dot(k_nat[start : start + rows, low : low + PAIR], queries) * SCORE

                top = jnp.zeros((1, WIDE_COLS), f32)
                if shifted:
                    top = jnp.full((1, WIDE_COLS), -jnp.inf, f32)
                    for start in range(0, length, rows):
                        top = jnp.maximum(top, jnp.max(scores(start), axis=0, keepdims=True))
                total = jnp.zeros((8, WIDE_COLS), f32)
                for start in range(0, length, rows):
                    score = scores(start)
                    weight = jnp.exp2(score - top) if shifted else jnp.exp2(score)
                    total = total + row_sums(weight)
                    probs[start : start + rows, :] = weight.astype(bf16)
                total = jnp.sum(total, axis=0, keepdims=True)
                mixed = dot(v_t[low : low + PAIR, :], probs[...])
                mixed = mixed / total
                out_t[low : low + HEAD_DIM, here] = mixed[0:HEAD_DIM, 0:BLK]
                out_t[low + HEAD_DIM : low + PAIR, here] = mixed[HEAD_DIM:PAIR, BLK:WIDE_COLS]
                log_total = top + jnp.log2(total)
                lse[2 * pair : 2 * pair + 1, here] = log_total[:, 0:BLK]
                lse[2 * pair + 1 : 2 * pair + 2, here] = log_total[:, BLK:WIDE_COLS]

    attend(False)
    level = lse[...]
    good = (level > -80.0) & (level < 120.0)
    wrong = jnp.max(jnp.where(good, 0.0, 1.0))

    @pl.when(wrong > 0.0)
    def again():
        attend(True)


def front(tokens, w_in, w_in_t, npar):
    length = tokens.shape[1]
    padded = ceil_to(length, BLK)
    shape = jax.ShapeDtypeStruct
    return pl.pallas_call(
        functools.partial(front_kernel, length),
        out_shape=(
            shape((padded, D), bf16),
            shape((padded, D), bf16),
            shape((padded, D), bf16),
            shape((padded, D), bf16),
            shape((D, padded), bf16),
            shape((D, padded), bf16),
            shape((D, padded), f32),
            shape((8, padded), f32),
        ),
        in_specs=[pl.BlockSpec(memory_space=pl.ANY)] + vmem(3),
        out_specs=tuple(vmem(8)),
        scratch_shapes=[
            pltpu.VMEM((padded, D), bf16),
            pltpu.VMEM((D, padded), bf16),
            pltpu.VMEM((padded, WIDE_COLS), bf16),
            pltpu.VMEM((PAIR, WIDE_COLS), bf16),
            pltpu.SemaphoreType.DMA,
        ],
        compiler_params=params(),
        name="front",
    )(tokens, w_in, w_in_t, npar)


def softplus(values):
    return jnp.maximum(values, 0.0) + jnp.log1p(jnp.exp(-jnp.abs(values)))


def sigmoid(values):
    return 1.0 / (1.0 + jnp.exp(-values))


def head_grads(logits, counts, library, genes, length):
    lane = lax.broadcasted_iota(jnp.int32, logits[0].shape, 1)
    valid = (lane >= CLASS_TOK) & (lane < length)
    mean_logit = jnp.where(valid, logits[0], -jnp.inf)
    top = jnp.max(mean_logit, axis=1, keepdims=True)
    raised = jnp.exp(mean_logit - top)
    total = jnp.sum(raised, axis=1, keepdims=True)
    share = raised / total
    log_mean = jnp.where(valid, logits[0], 0.0) - top - jnp.log(total) + jnp.log(library)
    disp = 0.5 + softplus(logits[1])
    log_disp = jnp.log(disp)
    inflate = logits[2]
    gap = log_mean - log_disp
    mean_part = sigmoid(gap)
    disp_part = sigmoid(-gap)
    log_both = jnp.maximum(log_disp, log_mean) + jnp.log1p(jnp.exp(-jnp.abs(gap)))
    shared = disp * (log_disp - log_both)
    shared_disp = (log_disp - log_both) + mean_part
    shared_mean = -disp * mean_part
    none = counts == 0.0
    lean = sigmoid(shared - inflate)
    psi = jnp.zeros_like(disp)
    for step in range(7):
        psi = psi + jnp.where(counts > step, 1.0 / (disp + step), 0.0)
    grad_disp = jnp.where(none, -lean * shared_disp, counts * disp_part / disp - shared_disp - psi)
    grad_mean = jnp.where(none, -lean * shared_mean, -shared_mean - counts * disp_part)
    grad_inflate = jnp.where(none, lean - sigmoid(-inflate), sigmoid(inflate))
    part = 1.0 / genes
    grad_disp = jnp.where(valid, grad_disp * part, 0.0)
    grad_mean = jnp.where(valid, grad_mean * part, 0.0)
    grad_inflate = jnp.where(valid, grad_inflate * part, 0.0)
    grad_zero = grad_mean - share * jnp.sum(grad_mean, axis=1, keepdims=True)
    return (grad_zero, grad_disp * sigmoid(logits[1]), grad_inflate)


def middle_kernel(
    length,
    tok,
    out_t,
    w_out,
    w_up,
    w_down,
    npar,
    head,
    counts,
    library,
    output,
    grad_mid,
    g_nat,
    g_t,
    delta,
    grad_down,
    grad_up,
    grad_out,
    grad_norm,
    grad_head,
    xbuf,
    mixed_t,
    mid,
    res,
    act,
    hidden,
    slope,
    res_low,
    grad_before,
    mid_low,
    logits,
    sem,
):
    padded = xbuf.shape[0]
    blocks = padded // BLK
    me = lax.axis_index("narrow")
    copy = pltpu.make_async_copy(tok.at[me], xbuf.at[pl.ds(0, length)], sem)
    copy.start()
    if padded > length:
        xbuf[length:, :] = jnp.zeros((padded - length, D), bf16)
    grad_norm[...] = jnp.zeros(grad_norm.shape, f32)
    grad_head[...] = jnp.zeros(grad_head.shape, f32)
    copy.wait()
    gain = npar[2:3, :]
    shift = npar[3:4, :]

    @pl.loop(0, blocks)
    def forward(step):
        here = block_of(step)
        mixed = out_t[:, here].astype(bf16)
        mixed_t[:, here] = mixed
        middle = xbuf[here, :].astype(f32) + dot(mixed, w_out[...], TN)
        mid[here, :] = middle
        xhat, _ = norm_parts(middle)
        low = (xhat * gain + shift).astype(bf16)
        act[here, :] = low
        before = dot(low, w_up[...])
        square = before * before
        bend = jnp.tanh(GELU_A * before * (1.0 + GELU_B * square))
        half = 0.5 + 0.5 * bend
        hid = (before * half).astype(bf16)
        hidden[here, :] = hid
        slope[here, :] = half + 0.5 * before * (1.0 - bend * bend) * (GELU_A + 3.0 * GELU_A * GELU_B * square)
        result = middle + dot(hid, w_down[...])
        res[here, :] = result
        logits[:, here] = dot(head[...], result, NT, HI)

    output[...] = res[0:length, :].astype(bf16)
    genes = length - CLASS_TOK
    zero, disp, inflate = head_grads(
        (logits[0:1, :], logits[1:2, :], logits[2:3, :]),
        counts[0:1, :].astype(f32),
        library[0:1, 0:1].astype(f32),
        genes,
        length,
    )
    logits[0:1, :] = zero
    logits[1:2, :] = disp
    logits[2:3, :] = inflate
    logits[3:8, :] = jnp.zeros((5, padded), f32)

    @pl.loop(0, blocks)
    def backward(step):
        here = block_of(step)
        down_logits = logits[:, here]
        grad_res = dot(down_logits, head[...], TN, HI)
        grad_head[...] += dot(down_logits, res[here, :], NN, HI)
        low = grad_res.astype(bf16)
        res_low[here, :] = low
        grad_hidden = dot(low, w_down[...], NT)
        back = (slope[here, :] * grad_hidden).astype(bf16)
        grad_before[here, :] = back
        grad_two = dot(back, w_up[...], NT)
        xhat, inverse = norm_parts(mid[here, :])
        grad_norm[0:8, :] += row_sums(grad_two * xhat)
        grad_norm[8:16, :] += row_sums(grad_two)
        total = grad_res + norm_back(xhat, inverse, gain, grad_two)
        mid[here, :] = total
        total_low = total.astype(bf16)
        mid_low[here, :] = total_low
        g_nat[here, :] = dot(total_low, w_out[...], NT).astype(bf16)
        grad_t = dot(w_out[...], total_low, NT).astype(bf16)
        g_t[:, here] = grad_t
        inner = grad_t.astype(f32) * out_t[:, here]
        delta[:, here] = jnp.concatenate(
            [
                jnp.sum(inner[h * HEAD_DIM : (h + 1) * HEAD_DIM], axis=0, keepdims=True)
                for h in range(HEADS)
            ]
            + [jnp.zeros((8 - HEADS, BLK), f32)],
            axis=0,
        )

    grad_mid[...] = mid[0:length, :]
    grad_down[...] = dot(res_low[...], hidden[...], TN)
    grad_up[...] = dot(act[...], grad_before[...], TN)
    grad_out[...] = dot(mixed_t[...], mid_low[...])


def middle_stage(tokens, out_t, w_out, w_up, w_down, npar, head, counts, library):
    length = tokens.shape[1]
    padded = out_t.shape[1]
    shape = jax.ShapeDtypeStruct
    return pl.pallas_call(
        functools.partial(middle_kernel, length),
        out_shape=(
            shape((length, D), bf16),
            shape((length, D), f32),
            shape((padded, D), bf16),
            shape((D, padded), bf16),
            shape((8, padded), f32),
            shape((D, FF), f32),
            shape((D, FF), f32),
            shape((D, D), f32),
            shape((16, D), f32),
            shape((8, D), f32),
        ),
        in_specs=[pl.BlockSpec(memory_space=pl.ANY)] + vmem(8),
        out_specs=tuple(vmem(10)),
        scratch_shapes=[
            pltpu.VMEM((padded, D), bf16),
            pltpu.VMEM((D, padded), bf16),
            pltpu.VMEM((padded, D), f32),
            pltpu.VMEM((padded, D), f32),
            pltpu.VMEM((padded, D), bf16),
            pltpu.VMEM((padded, FF), bf16),
            pltpu.VMEM((padded, FF), f32),
            pltpu.VMEM((padded, D), bf16),
            pltpu.VMEM((padded, FF), bf16),
            pltpu.VMEM((padded, D), bf16),
            pltpu.VMEM((8, padded), f32),
            pltpu.SemaphoreType.DMA,
        ],
        compiler_params=params(),
        name="middle",
    )(tokens, out_t, w_out, w_up, w_down, npar, head, counts, library)


def back_kernel(
    length,
    tok,
    x1,
    k_nat,
    v_nat,
    q_nat,
    q_t,
    k_t,
    g_nat,
    g_t,
    lse,
    delta,
    grad_mid,
    w_in,
    npar,
    grad_input,
    grad_in,
    grad_norm,
    xbuf,
    probs,
    dscore,
    qbd,
    gbd,
    qnd,
    gnd,
    dk,
    dv,
    dq_t,
    joined,
    sem,
):
    padded = x1.shape[0]
    blocks = padded // BLK
    rows = key_chunk(length)
    me = lax.axis_index("narrow")
    copy = pltpu.make_async_copy(tok.at[me], xbuf.at[pl.ds(0, length)], sem)
    copy.start()
    if padded > length:
        xbuf[length:, :] = jnp.zeros((padded - length, D), bf16)
        dscore[length:, :] = jnp.zeros((padded - length, WIDE_COLS), bf16)
        joined[1, length:, :] = jnp.zeros((padded - length, D), bf16)
        joined[2, length:, :] = jnp.zeros((padded - length, D), bf16)
    for ref in (qbd, gbd, qnd, gnd):
        ref[...] = jnp.zeros(ref.shape, bf16)
    grad_norm[...] = jnp.zeros(grad_norm.shape, f32)
    scale = HEAD_DIM ** (-0.5)

    for pair in range(HEADS // 2):
        low = pair * PAIR
        mid = low + HEAD_DIM
        top = low + PAIR
        dk[...] = jnp.zeros(dk.shape, f32)
        dv[...] = jnp.zeros(dv.shape, f32)

        @pl.loop(0, blocks)
        def block(step):
            here = block_of(step)
            qbd[0:HEAD_DIM, 0:BLK] = q_t[low:mid, here]
            qbd[HEAD_DIM:PAIR, BLK:WIDE_COLS] = q_t[mid:top, here]
            gbd[0:HEAD_DIM, 0:BLK] = g_t[low:mid, here]
            gbd[HEAD_DIM:PAIR, BLK:WIDE_COLS] = g_t[mid:top, here]
            both = q_nat[here, low:top]
            qnd[0:BLK, 0:HEAD_DIM] = both[:, 0:HEAD_DIM]
            qnd[BLK:WIDE_COLS, HEAD_DIM:PAIR] = both[:, HEAD_DIM:PAIR]
            both = g_nat[here, low:top]
            gnd[0:BLK, 0:HEAD_DIM] = both[:, 0:HEAD_DIM]
            gnd[BLK:WIDE_COLS, HEAD_DIM:PAIR] = both[:, HEAD_DIM:PAIR]
            queries = qbd[...]
            grads = gbd[...]
            level = jnp.concatenate([lse[2 * pair : 2 * pair + 1, here], lse[2 * pair + 1 : 2 * pair + 2, here]], axis=1)
            inner = jnp.concatenate(
                [delta[2 * pair : 2 * pair + 1, here], delta[2 * pair + 1 : 2 * pair + 2, here]], axis=1
            )
            for start in range(0, length, rows):
                part = slice(start, start + rows)
                weight = jnp.exp2(dot(k_nat[part, low:top], queries) * SCORE - level)
                probs[part, :] = weight.astype(bf16)
                change = dot(v_nat[part, low:top], grads) - inner
                dscore[part, :] = (weight * change).astype(bf16)
            dv[...] += dot(probs[...], gnd[...])
            dk[...] += dot(dscore[0:length, :], qnd[...])
            moved = dot(k_t[low:top, :], dscore[...]) * scale
            dq_t[low:mid, here] = moved[0:HEAD_DIM, 0:BLK].astype(bf16)
            dq_t[mid:top, here] = moved[HEAD_DIM:PAIR, BLK:WIDE_COLS].astype(bf16)

        joined[1, 0:length, low:top] = (dk[...] * scale).astype(bf16)
        joined[2, 0:length, low:top] = dv[...].astype(bf16)

    copy.wait()
    gain = npar[0:1, :]

    @pl.loop(0, blocks)
    def close(step):
        here = block_of(step)
        grad_q = dq_t[:, here].T
        joined[0, here, :] = grad_q
        total = dot(grad_q, w_in[0], NT) + dot(joined[1, here, :], w_in[1], NT) + dot(joined[2, here, :], w_in[2], NT)
        xhat, inverse = norm_parts(xbuf[here, :].astype(f32))
        grad_norm[0:8, :] += row_sums(total * xhat)
        grad_norm[8:16, :] += row_sums(total)
        grad_input[here, :] = grad_mid[here, :] + norm_back(xhat, inverse, gain, total)

    for which in range(3):
        grad_in[which] = dot(joined[which], x1[...], TN)


def back_stage(tokens, x1, k_nat, v_nat, q_nat, q_t, k_t, g_nat, g_t, lse, delta, grad_mid, w_in, npar):
    length = tokens.shape[1]
    padded = x1.shape[0]
    shape = jax.ShapeDtypeStruct
    return pl.pallas_call(
        functools.partial(back_kernel, length),
        out_shape=(
            shape((padded, D), f32),
            shape((3, D, D), f32),
            shape((16, D), f32),
        ),
        in_specs=[pl.BlockSpec(memory_space=pl.ANY)] + vmem(13),
        out_specs=tuple(vmem(3)),
        scratch_shapes=[
            pltpu.VMEM((padded, D), bf16),
            pltpu.VMEM((length, WIDE_COLS), bf16),
            pltpu.VMEM((padded, WIDE_COLS), bf16),
            pltpu.VMEM((PAIR, WIDE_COLS), bf16),
            pltpu.VMEM((PAIR, WIDE_COLS), bf16),
            pltpu.VMEM((WIDE_COLS, PAIR), bf16),
            pltpu.VMEM((WIDE_COLS, PAIR), bf16),
            pltpu.VMEM((length, PAIR), f32),
            pltpu.VMEM((length, PAIR), f32),
            pltpu.VMEM((D, padded), bf16),
            pltpu.VMEM((3, padded, D), bf16),
            pltpu.SemaphoreType.DMA,
        ],
        compiler_params=params(),
        name="back",
    )(tokens, x1, k_nat, v_nat, q_nat, q_t, k_t, g_nat, g_t, lse, delta, grad_mid, w_in, npar)


def adam_update(grad, first, second, weight, decay_rate, rate):
    first_new = decay_first * first + (1.0 - decay_first) * grad
    second_new = decay_second * second + (1.0 - decay_second) * grad * grad
    fix_first = 1.0 - decay_first**STEP
    fix_second = 1.0 - decay_second**STEP
    direction = first_new / fix_first / (jnp.sqrt(second_new / fix_second) + adam_eps)
    return (first_new, second_new, weight - rate * (direction + decay_rate * weight))


def average_update(average, weight_new, dim):
    count = average.shape[dim]
    piece = lax.dynamic_slice_in_dim(weight_new, lax.axis_index("wide") * count, count, dim)
    return ema_keep * average + (1.0 - ema_keep) * piece


def on_device(cell_tokens, library_size, gene_counts, *state):
    weights, firsts, seconds, averages = state[0:6], state[6:12], state[12:18], state[18:24]
    attend_in, attend_out, up_weight, down_weight, norm_params, head_weight = weights
    cells, length, _ = cell_tokens.shape
    padded = ceil_to(length, BLK)
    me = lax.axis_index("narrow")

    w_in = lax.all_gather(attend_in.astype(bf16), "narrow", axis=2, tiled=True)
    w_out = lax.all_gather(attend_out.astype(bf16), "narrow", axis=0, tiled=True)
    w_up = lax.all_gather(up_weight.astype(bf16), "narrow", axis=1, tiled=True)
    w_down = lax.all_gather(down_weight.astype(bf16), "narrow", axis=0, tiled=True)
    w_in_t = w_in.transpose(0, 2, 1)
    head = jnp.pad(head_weight, ((0, 5), (0, 0)))
    counts = lax.dynamic_slice_in_dim(gene_counts, me, 1, 0)
    counts = jnp.pad(counts, ((0, 0), (CLASS_TOK, padded - length)))
    library = lax.dynamic_slice_in_dim(library_size, me, 1, 0).reshape(1, 1)

    x1, k_nat, v_nat, q_nat, q_t, k_t, out_t, lse = front(cell_tokens, w_in, w_in_t, norm_params)
    out_own, grad_mid, g_nat, g_t, delta, grad_down, grad_up, grad_out, norm_two, grad_head = middle_stage(
        cell_tokens, out_t, w_out, w_up, w_down, norm_params, head, counts, library
    )
    output = lax.all_gather(out_own, "narrow")
    grad_mid = jnp.pad(grad_mid, ((0, padded - length), (0, 0)))
    grad_input, grad_in, norm_one = back_stage(
        cell_tokens, x1, k_nat, v_nat, q_nat, q_t, k_t, g_nat, g_t, lse, delta, grad_mid, w_in, norm_params
    )
    input_grad = lax.all_gather(grad_input[:length].astype(bf16), "narrow").astype(f32)

    narrow = lax.axis_size("narrow")
    shard = lambda v, dim: lax.psum(lax.psum_scatter(v, "narrow", scatter_dimension=dim, tiled=True), "wide")
    grad_in = shard(grad_in.transpose(0, 2, 1), 2)
    grad_out = shard(grad_out, 0)
    grad_up = shard(grad_up, 1)
    grad_down = shard(grad_down.T, 0)
    fold = lambda v: jnp.stack([jnp.sum(v[0:8], axis=0), jnp.sum(v[8:16], axis=0)])
    grad_norms, grad_head = lax.psum(
        (jnp.concatenate([fold(norm_one), fold(norm_two)], axis=0), grad_head[0:3]), ("wide", "narrow")
    )
    sharded = (
        jnp.sum(grad_in * grad_in)
        + jnp.sum(grad_out * grad_out)
        + jnp.sum(grad_up * grad_up)
        + jnp.sum(grad_down * grad_down)
    )
    common = jnp.sum(grad_norms * grad_norms) + jnp.sum(grad_head * grad_head)
    grad_norm = jnp.sqrt(lax.psum(sharded, "narrow") + common)
    factor = jnp.minimum(1.0, clip_limit / grad_norm)
    grads = (grad_in, grad_out, grad_up, grad_down, grad_norms, grad_head)
    decays = (weight_decay,) * 4 + (0.0, weight_decay)
    rates = (learn_rate,) * 4 + (norm_rate, learn_rate)
    dims = (1, 1, 0, 1, 1, 1)
    outs = [output, input_grad, grad_norm]
    for index in range(6):
        clipped = grads[index] * factor
        first_new, second_new, weight_new = adam_update(
            clipped, firsts[index], seconds[index], weights[index], decays[index], rates[index]
        )
        outs += [clipped, first_new, second_new, weight_new, average_update(averages[index], weight_new, dims[index])]
    return tuple(outs)


def solution(mesh):
    by_in, by_rows, by_cols = P(None, None, "narrow"), P("narrow", None), P(None, "narrow")
    kinds = (by_in, by_rows, by_cols, by_rows, P(), P())
    means = (
        P(None, "wide", "narrow"),
        P("narrow", "wide"),
        P("wide", "narrow"),
        P("narrow", "wide"),
        P(None, "wide"),
        P(None, "wide"),
    )
    cell = P("wide", None, None)
    outs = (cell, cell, P())
    for kind, mean in zip(kinds, means):
        outs += (kind, kind, kind, kind, mean)
    return jax.shard_map(
        on_device,
        mesh=mesh,
        in_specs=(cell, P("wide"), P("wide", None)) + kinds * 3 + means,
        out_specs=outs,
        check_vma=False,
    )
```

time: 1020 us -> 423 us (0.41); the launches traced: 1010 us -> 423 us
  waiting for transfers between devices: 544 us -> 155 us
  matrix products: 193 us -> 0 us
  Pallas kernels: 0 us -> 131 us
  other arithmetic: 122 us -> 22.6 us
  local copies, waits for them, and re-layouts: 95.3 us -> 17.3 us
  blocking collectives: 28.6 us -> 75.8 us
    psum x5 -> x1, waiting for transfers between devices: 543 us -> 33.1 us  [on_device(): lax.psum(lax.psum_scatter(v, 'narrow', scatter_dimension=dim, tiled=True)...]
    dot_general x127 -> x0, matrix products: 193 us -> none  [the longest x32 36.6 us: one_block(): jnp.einsum('qd,kd->qk', query_block, key_rows, preferred_element_type=jnp...]
    pallas_call x0 -> x3, Pallas kernels: none -> 131 us  [the longest x1 62.5 us: back_stage(): pl.pallas_call(functools.partial(back_kernel, length), out_shape=(shape((...]
    reduce_scatter x0 -> x4, waiting for transfers between devices: none -> 77.8 us  [on_device(): lax.psum_scatter(v, 'narrow', scatter_dimension=dim, tiled=True)]
    reduce_sum x28 -> x4, other arithmetic: 67.8 us -> 1.24 us  [the longest x2 1.2 us: on_device(): common = jnp.sum(grad_norms * grad_norms) + jnp.sum(grad_head * grad_head)]
    all_gather x0 -> x2, waiting for transfers between devices: none -> 42.6 us  [the longest x1 31.3 us: on_device(): output = lax.all_gather(out_own, 'narrow')]
    while x171 -> x0, local copies, waits for them, and re-layouts: 33 us -> none
    all_gather x0 -> x4, blocking collectives: none -> 29.4 us  [the longest x1 8.07 us: on_device(): w_in = lax.all_gather(attend_in.astype(bf16), 'narrow', axis=2, tiled=True)]
  transfers between devices with their start and end apart: 5 -> 7, of which waited for: 5 -> 6; matrix products, arithmetic and copies ran while one was open for 3% -> 7% of each run, Pallas kernels for 0% -> 15%
where the time goes in v1:
time: 423 us
  waiting for transfers between devices  155 us (37%)
  Pallas kernels  131 us (31%)
  blocking collectives  75.8 us (18%)
  other arithmetic  22.6 us (5%)
  between operations  20.4 us (5%)
  local copies, waits for them, and re-layouts  17.3 us (4%)
    reduce_scatter x4, waiting for transfers between devices, on_device(): lax.psum_scatter(v, 'narrow', scatter_dimension=dim, tiled=True)  77.8 us
    pallas_call x1, Pallas kernels, back_stage(): pl.pallas_call(functools.partial(back_kernel, length), out_shape=(shape((...  62.5 us
    psum x1, blocking collectives, on_device(): lax.psum((jnp.concatenate([fold(norm_one), fold(norm_two)], axis=0), grad...  39.5 us
    pallas_call x1, Pallas kernels, middle_stage(): pl.pallas_call(functools.partial(middle_kernel, length), out_shape=(shape...  38.3 us
    psum x1, waiting for transfers between devices, on_device(): lax.psum(lax.psum_scatter(v, 'narrow', scatter_dimension=dim, tiled=True)...  33.1 us
    all_gather x1, waiting for transfers between devices, on_device(): output = lax.all_gather(out_own, 'narrow')  31.3 us
    pallas_call x1, Pallas kernels, front(): pl.pallas_call(functools.partial(front_kernel, length), out_shape=(shape(...  30.4 us
    all_gather x1, waiting for transfers between devices, on_device(): lax.all_gather(grad_input[:length].astype(bf16), 'narrow').astype(f32)  11.3 us
  transfers between devices with their start and end apart: 7, of which 6 were waited for; matrix products, arithmetic and copies ran while one was open for 7% of the time, Pallas kernels for 15%

profile of v1, /device:TPU:0, one launch (start us, length us, event | category | flops | bytes accessed | tf_op | source)
XLA Modules:
  0.0 422.6 jit_solution(16109089227393344888)
XLA Ops:
  7.2 0.0 copy-start
  7.2 0.0 reduce-scatter.7.cloned.1.call-start
  7.3 1.0 convert_element_type.20
  8.3 8.1 %all_gather.24 = bf16[3,256,256]{1,2,0:T(8,128)(2,1)S(1)} all-gather(bf16[3,256,64]{1,2,0:T(8,128)(2,1)S(1)} %convert_element_type.20), channel_id=1, replica_groups=mesh['wide'=8,'narrow'=4] {'narrow'}, dimensions={2}, use_global_device_ids=true | all-gather | bytes 491520 | tf_op jit(solution)/shard_map/all_gather | solution.py:559
  16.4 0.9 copy.69.w_in
  17.3 0.7 pad.13.counts
  18.0 0.6 dynamic_slice.25
  18.6 7.8 %all_gather.26.w_up = bf16[256,1024]{1,0:T(8,128)(2,1)} all-gather(bf16[256,256]{1,0:T(8,128)(2,1)S(1)} %convert_element_type.22), channel_id=1, replica_groups=mesh['wide'=8,'narrow'=4] {'narrow'}, dimensions={1}, use_global_device_ids=true | all-gather | bytes 655360 | tf_op jit(solution)/shard_map/all_gather | solution.py:561
  26.4 7.7 %all_gather.27.w_down = bf16[1024,256]{1,0:T(8,128)(2,1)} all-gather(bf16[256,256]{1,0:T(8,128)(2,1)S(1)} %convert_element_type.23), channel_id=1, replica_groups=mesh['wide'=8,'narrow'=4] {'narrow'}, dimensions={0}, use_global_device_ids=true | all-gather | bytes 655360 | tf_op jit(solution)/shard_map/all_gather | solution.py:562
  34.1 5.9 %all_gather.25.w_out = bf16[256,256]{1,0:T(8,128)(2,1)} all-gather(bf16[64,256]{1,0:T(8,128)(2,1)S(1)} %convert_element_type.21), channel_id=1, replica_groups=mesh['wide'=8,'narrow'=4] {'narrow'}, dimensions={0}, use_global_device_ids=true | all-gather | bytes 163840 | tf_op jit(solution)/shard_map/all_gather | solution.py:560
  40.0 0.6 pad.12.head
  40.6 30.4 %front.1 = (bf16[2304,256]{1,0:T(8,128)(2,1)}, bf16[2304,256]{1,0:T(8,128)(2,1)}, bf16[2304,256]{1,0:T(8,128)(2,1)}, bf16[2304,256]{1,0:T(8,128)(2,1)}, bf16[256...) custom-call(bf16[4,2208,256]{2,1,0:T(8,128)(2,1)} %tok.5, ...), custom_call_target="tpu_custom_call" | custom-call | tf_op jit(solution)/shard_map/front/pallas_call | solution.py:170
  71.0 38.3 %middle.1 = (bf16[2208,256]{1,0:T(8,128)(2,1)}, f32[2208,256]{1,0:T(8,128)}, bf16[2304,256]{1,0:T(8,128)(2,1)}, bf16[256,2304]{1,0:T(8,128)(2,1)}, f32[8,2304]{1...) custom-call(bf16[4,2208,256]{2,1,0:T(8,128)(2,1)} %tok.5, ...), custom_call_target="tpu_custom_call" | custom-call | tf_op jit(solution)/shard_map/middle/pallas_call | solution.py:363
  109.3 0.0 reduce-scatter.7.cloned.1.call-update
  109.3 0.3 reduce-scatter.5.cloned.1.call-start
  109.6 3.2 pad.14.grad_mid
  112.8 62.5 %back.1 = (f32[2304,256]{1,0:T(8,128)}, f32[3,256,256]{2,1,0:T(8,128)}, f32[16,256]{1,0:T(8,128)}) custom-call(bf16[4,2208,256]{2,1,0:T(8,128)(2,1)} %tok.5, bf16[2304,256]{1,0:T(8,128)(2,1)} %get-tuple-element.56.x1, bf16[2304,256]{1,0:T(8,128)(2,1)} %get-tuple-element.57.k_nat, bf16[2304,256]{1,0:T(8,128)(2,1)} %get-tuple-element.58.v_nat, ...), custom_call_target="tpu_custom_call" | custom-call | tf_op jit(solution)/shard_map/back/pallas_call | solution.py:509
  175.3 0.0 reduce-scatter.5.cloned.1.call-update
  175.3 0.0 reduce-scatter.11.cloned.1.call-start
  175.4 1.3 copy.71
  176.7 0.0 reduce-scatter.11.cloned.1.call-update
  176.7 0.0 reduce-scatter.9.cloned.1.call-start
  176.8 0.5 reduce-scatter.9.cloned.1.call-update
  177.3 0.0 all-reduce.7.cloned.1.call-start
  177.3 0.0 reduce-scatter.7.cloned.1.call-done
  177.4 22.3 %reduce-scatter.5.cloned.1.call-done = f32[3,256,64]{1,2,0:T(8,128)} async-done(((f32[3,256,256]{1,2,0:T(8,128)}), f32[3,256,64]{1,2,0:T(8,128)}) %reduce-scatter.5.cloned.1.call-update) | async-done | bytes 196624 | tf_op jit(solution)/shard_map/reduce_scatter | solution.py:581
  199.6 28.0 %reduce-scatter.11.cloned.1.call-done = f32[256,256]{1,0:T(8,128)} async-done(((f32[1024,256]{1,0:T(8,128)}), f32[256,256]{1,0:T(8,128)}) %reduce-scatter.11.cloned.1.call-update) | async-done | bytes 262160 | tf_op jit(solution)/shard_map/reduce_scatter | solution.py:581
  227.7 27.5 %reduce-scatter.9.cloned.1.call-done = f32[256,256]{1,0:T(8,128)} async-done(((f32[256,1024]{1,0:T(8,128)}), f32[256,256]{1,0:T(8,128)}) %reduce-scatter.9.cloned.1.call-update) | async-done | bytes 262160 | tf_op jit(solution)/shard_map/reduce_scatter | solution.py:581
  255.1 0.0 all-reduce.7.cloned.1.call-update
  255.2 0.0 all-gather.7.cloned.1.call-start
  255.2 2.7 slice.31
  258.0 0.0 all-gather.7.cloned.1.call-update
  258.0 0.0 all-gather.5.cloned.1.call-start
  258.1 0.6 all-gather.5.cloned.1.call-update
  258.8 0.1 copy.74
  258.9 0.1 copy.73
  259.0 0.1 copy.72
  259.2 39.5 %all-reduce.3 = (f32[4,256]{1,0:T(4,128)S(1)}, f32[3,256]{1,0:T(4,128)S(1)}) all-reduce(f32[4,256]{1,0:T(4,128)S(1)} %pad_maximum_fusion, f32[3,256]{1,0:T(4,128)S(1)} %slice.24), channel_id=1, replica_groups=mesh['wide'=8,'narrow'=4] {'wide','narrow'}, use_global_device_ids=true, to_apply=%region_17.18 | all-reduce | flops 1792 | bytes 14336 | tf_op jit(solution)/shard_map/psum | solution.py:587
  298.6 0.6 multiply_reduce_fusion.4
  299.2 0.6 multiply_reduce_fusion.5
  301.1 33.1 %all-reduce.7.cloned.1.call-done = (f32[3,256,64]{1,2,0:T(8,128)}, f32[64,256]{1,0:T(8,128)}, f32[256,256]{1,0:T(8,128)}, f32[256,256]{1,0:T(8,128)}) async-done(((f32[3,256,64]{1,2,0:T(8,128)}, f32[64,256]{1,0:T(8,128)}, f32[256,256]{1,0:T(8,128)}, f32[256,256]{1,0:T(8,128)}), (f32[3,256,64]{1,2,0:T(8,128)}, f32[64,256]{1,0:T(8,128)}, f32[256,256]{1,0:T(8,128)}, ...) | async-done | bytes 786448 | tf_op jit(solution)/shard_map/psum | solution.py:581
  334.3 1.5 multiply_reduce_fusion.3
  335.7 1.6 multiply_reduce_fusion.2
  338.6 1.6 multiply_reduce_fusion.1
  340.9 1.6 multiply_reduce_fusion
  343.2 6.9 %psum.53 = f32[]{:T(128)} all-reduce(f32[]{:T(128)S(6)} %add.160), channel_id=1, replica_groups=mesh['wide'=8,'narrow'=4] {'narrow'}, use_global_device_ids=true, to_apply=%region_12.13 | all-reduce | flops 1 | bytes 8 | tf_op jit(solution)/shard_map/psum | solution.py:597
  350.9 2.4 multiply_subtract_fusion
  353.4 0.1 multiply_add_fusion.3
  353.5 0.7 copy.77
  354.2 0.7 multiply_subtract_fusion.3
  355.0 0.1 multiply_add_fusion.7
  355.1 0.7 copy.76
  355.7 0.9 multiply_subtract_fusion.2
  356.6 0.1 multiply_add_fusion.4
  356.7 0.7 copy.75
  357.4 0.6 multiply_subtract_fusion.4
  358.0 0.7 multiply_add_fusion.10
  358.7 0.6 multiply_subtract_fusion.5
  359.3 0.7 multiply_add_fusion.11
  360.0 0.6 multiply_add_fusion.6
  360.6 11.3 %all-gather.7.cloned.1.call-done = bf16[8832,256]{1,0:T(8,128)(2,1)} async-done(((bf16[2208,256]{1,0:T(8,128)(2,1)}), bf16[8832,256]{1,0:T(8,128)(2,1)}) %all-gather.7.cloned.1.call-update) | async-done | bytes 4522000 | tf_op jit(solution)/shard_map/all_gather | solution.py:578
  371.9 6.7 %convert.4 = f32[4,2208,256]{2,1,0:T(8,128)} convert(bf16[4,2208,256]{2,1,0:T(8,128)(2,1)} %bitcast.12) | non-fusion elementwise | flops 2260992 | bytes 13565952 | tf_op jit(solution)/shard_map/convert_element_type | solution.py:578
  378.6 31.3 %all-gather.5.cloned.1.call-done = bf16[8832,256]{1,0:T(8,128)(2,1)} async-done(((bf16[2208,256]{1,0:T(8,128)(2,1)}), bf16[8832,256]{1,0:T(8,128)(2,1)}) %all-gather.5.cloned.1.call-update) | async-done | bytes 4522000 | tf_op jit(solution)/shard_map/all_gather | solution.py:573
  409.9 4.7 %copy.83 = bf16[4,2208,256]{2,1,0:T(8,128)(2,1)} copy(bf16[4,2208,256]{2,1,0:T(8,128)(2,1)} %bitcast.11) | data formatting | bytes 9043968
  (85 shorter events, 0.3 us)
Async XLA Ops:
  7.2 10.1 %copy-start = (s32[4,2200]{1,0:T(4,128)S(1)}, s32[4,2200]{1,0:T(4,128)}, u32[]{:S(2)}) copy-start(s32[4,2200]{1,0:T(4,128)} %param.29) | copy-start | bytes 105604
  7.2 10.8 %copy-start.38 = (s32[4]{0:T(128)S(1)}, s32[4]{0:T(128)}, u32[]{:S(2)}) copy-start(s32[4]{0:T(128)} %param.28) | copy-start | bytes 52
  7.2 11.4 %copy-start.2 = (f32[256,256]{1,0:T(8,128)S(1)}, f32[256,256]{1,0:T(8,128)}, u32[]{:S(2)}) copy-start(f32[256,256]{1,0:T(8,128)} %param.32) | copy-start | bytes 786436
  7.2 170.1 %reduce-scatter.7.cloned.1.call-start = ((), (), s32[]{:S(2)}) async-start(), calls=%async_computation.5 | async-start | bytes 327680 | tf_op jit(solution)/shard_map/reduce_scatter | solution.py:581
  8.3 18.1 %copy-start.3 = (f32[256,256]{1,0:T(8,128)S(1)}, f32[256,256]{1,0:T(8,128)}, u32[]{:S(2)}) copy-start(f32[256,256]{1,0:T(8,128)} %param.33) | copy-start | bytes 786436
  16.4 17.8 %copy-start.1 = (bf16[3,256,256]{1,2,0:T(8,128)(2,1)}, bf16[3,256,256]{1,2,0:T(8,128)(2,1)S(1)}, u32[]{:S(2)}) copy-start(bf16[3,256,256]{1,2,0:T(8,128)(2,1)S(1)} %all_gather.24) | copy-start | bytes 1179652
  17.3 16.8 %copy-start.14 = (f32[64,256]{1,0:T(8,128)S(1)}, f32[64,256]{1,0:T(8,128)}, u32[]{:S(2)}) copy-start(f32[64,256]{1,0:T(8,128)} %param.31) | copy-start | bytes 196612
  18.6 21.4 %copy-start.28 = (f32[3,256]{1,0:T(4,128)S(1)}, f32[3,256]{1,0:T(4,128)}, u32[]{:S(2)}) copy-start(f32[3,256]{1,0:T(4,128)} %param.35) | copy-start | bytes 9220
  109.3 90.3 %reduce-scatter.5.cloned.1.call-start = ((), (), s32[]{:S(2)}) async-start(), calls=%async_computation.4 | async-start | bytes 983040 | tf_op jit(solution)/shard_map/reduce_scatter | solution.py:581
  112.8 62.6 %copy-start.4 = (f32[256,1024]{1,0:T(8,128)S(1)}, f32[256,1024]{1,0:T(8,128)}, u32[]{:S(2)}) copy-start(f32[256,1024]{1,0:T(8,128)} %get-tuple-element.71) | copy-start | bytes 3145732
  175.3 52.3 %reduce-scatter.11.cloned.1.call-start = ((), (), s32[]{:S(2)}) async-start(), calls=%async_computation.7 | async-start | bytes 1310720 | tf_op jit(solution)/shard_map/reduce_scatter | solution.py:581
  176.7 78.4 %reduce-scatter.9.cloned.1.call-start = ((), (), s32[]{:S(2)}) async-start(), calls=%async_computation.6 | async-start | bytes 1310720 | tf_op jit(solution)/shard_map/reduce_scatter | solution.py:581
  177.3 157.0 %all-reduce.7.cloned.1.call-start = ((), (), s32[]{:S(2)}) async-start(), calls=%async_computation.10 | async-start | bytes 1572864 | tf_op jit(solution)/shard_map/psum | solution.py:581
  255.2 116.7 %all-gather.7.cloned.1.call-start = ((), (), s32[]{:S(2)}) async-start(), calls=%async_computation.9 | async-start | bytes 5652480 | tf_op jit(solution)/shard_map/all_gather | solution.py:578
  258.0 0.8 copy-start.35
  258.0 0.8 copy-start.23
  258.0 0.9 copy-start.25
  258.0 1.0 copy-start.22
  258.0 1.1 copy-start.27
  258.0 1.1 copy-start.26
  258.0 151.9 %all-gather.5.cloned.1.call-start = ((), (), s32[]{:S(2)}) async-start(), calls=%async_computation.8 | async-start | bytes 5652480 | tf_op jit(solution)/shard_map/all_gather | solution.py:573
  258.1 92.8 %copy-start.10 = (f32[256,256]{1,0:T(8,128)S(1)}, f32[256,256]{1,0:T(8,128)}, u32[]{:S(2)}) copy-start(f32[256,256]{1,0:T(8,128)} %param.45) | copy-start | bytes 786436
  258.1 92.8 %copy-start.11 = (f32[256,256]{1,0:T(8,128)S(1)}, f32[256,256]{1,0:T(8,128)}, u32[]{:S(2)}) copy-start(f32[256,256]{1,0:T(8,128)} %param.39) | copy-start | bytes 786436
  258.1 92.8 %copy-start.12 = (f32[256,256]{1,0:T(8,128)S(1)}, f32[256,256]{1,0:T(8,128)}, u32[]{:S(2)}) copy-start(f32[256,256]{1,0:T(8,128)} %param.44) | copy-start | bytes 786436
  258.1 92.8 %copy-start.13 = (f32[256,256]{1,0:T(8,128)S(1)}, f32[256,256]{1,0:T(8,128)}, u32[]{:S(2)}) copy-start(f32[256,256]{1,0:T(8,128)} %param.38) | copy-start | bytes 786436
  350.9 3.3 copy-start.15
  350.9 3.3 copy-start.19
  350.9 3.3 copy-start.20
  353.3 3.3 copy-start.7
  353.3 6.6 %copy-start.9 = (f32[256,256]{1,0:T(8,128)}, f32[256,256]{1,0:T(8,128)S(1)}, u32[]{:S(2)}) copy-start(f32[256,256]{1,0:T(8,128)S(1)} %get-tuple-element.228) | copy-start | bytes 786436
  353.3 2.4 copy-start.5
  353.4 2.4 copy-start.6
  353.4 2.4 copy-start.16
  353.4 2.4 copy-start.17
  354.9 23.7 %copy-start.18 = (f32[64,256]{1,0:T(8,128)}, f32[64,256]{1,0:T(8,128)S(1)}, u32[]{:S(2)}) copy-start(f32[64,256]{1,0:T(8,128)S(1)} %get-tuple-element.223) | copy-start | bytes 196612
  354.9 2.5 copy-start.31
  354.9 2.5 copy-start.32
  354.9 3.1 copy-start.36
  354.9 3.8 copy-start.21
  354.9 3.8 copy-start.33
  354.9 3.8 copy-start.34
  354.9 4.4 %copy-start.37 = (f32[4,32]{1,0:T(4,128)S(1)}, f32[4,32]{1,0:T(4,128)}, u32[]{:S(2)}) copy-start(f32[4,32]{1,0:T(4,128)} %param.52) | copy-start | bytes 1540
  355.0 5.0 %copy-start.24 = (f32[32,256]{1,0:T(8,128)S(1)}, f32[32,256]{1,0:T(8,128)}, u32[]{:S(2)}) copy-start(f32[32,256]{1,0:T(8,128)} %param.50) | copy-start | bytes 98308
  356.6 21.9 %copy-start.8 = (f32[3,256,64]{1,2,0:T(8,128)}, f32[3,256,64]{1,2,0:T(8,128)S(1)}, u32[]{:S(2)}) copy-start(f32[3,256,64]{1,2,0:T(8,128)S(1)} %get-tuple-element.218) | copy-start | bytes 589828
  358.0 20.5 %copy-start.29 = (f32[3,256]{1,0:T(4,128)}, f32[3,256]{1,0:T(4,128)S(1)}, u32[]{:S(2)}) copy-start(f32[3,256]{1,0:T(4,128)S(1)} %get-tuple-element.243) | copy-start | bytes 9220
  359.3 19.3 %copy-start.30 = (f32[4,256]{1,0:T(4,128)}, f32[4,256]{1,0:T(4,128)S(1)}, u32[]{:S(2)}) copy-start(f32[4,256]{1,0:T(4,128)S(1)} %get-tuple-element.238) | copy-start | bytes 12292
Sparse Core Ops, SparseCore 0:
  109.4 20.9 reduce-scatter.6
  175.5 24.1 reduce-scatter.4
  202.8 24.8 reduce-scatter.10
  230.2 24.8 reduce-scatter.8
  258.7 75.5 all-reduce.6
  336.3 35.5 all-gather.6
  373.5 36.3 all-gather.4

commit v2 on v1

--- a/solution.py
+++ b/solution.py
@@ -61,8 +61,47 @@
     return [pl.BlockSpec(memory_space=pltpu.VMEM)] * count
 
 
-def params():
-    return pltpu.CompilerParams(vmem_limit_bytes=VMEM_BYTES)
+def params(**more):
+    return pltpu.CompilerParams(vmem_limit_bytes=VMEM_BYTES, **more)
+
+
+def anywhere(count):
+    return [pl.BlockSpec(memory_space=pl.ANY)] * count
+
+
+def remote(src, dst, sems, index, axis, peer):
+    return pltpu.make_async_remote_copy(
+        src_ref=src,
+        dst_ref=dst,
+        send_sem=sems.at[0, index],
+        recv_sem=sems.at[1, index],
+        device_id={axis: peer},
+        device_id_type=pl.DeviceIdType.MESH,
+    )
+
+
+def narrow_mates():
+    me = lax.axis_index("narrow")
+    row, core = me // 2, me % 2
+    return me, row, core, (1 - row) * 2 + core, row * 2 + 1 - core
+
+
+def greet(wide_peers=0):
+    _, _, _, over, beside = narrow_mates()
+    barrier = pltpu.get_barrier_semaphore()
+    mesh_id = pl.DeviceIdType.MESH
+    pl.semaphore_signal(barrier, inc=1, device_id={"narrow": over}, device_id_type=mesh_id)
+    pl.semaphore_signal(barrier, inc=1, device_id={"narrow": beside}, device_id_type=mesh_id)
+    if wide_peers:
+        place = lax.axis_index("wide")
+        _, row, core, _, _ = narrow_mates()
+        pl.semaphore_signal(
+            barrier, inc=1, device_id={"narrow": (1 - row) * 2 + 1 - core}, device_id_type=mesh_id
+        )
+        for step in range(1, wide_peers):
+            peer = lax.rem(place + step, wide_peers)
+            pl.semaphore_signal(barrier, inc=1, device_id={"wide": peer}, device_id_type=mesh_id)
+    pl.semaphore_wait(barrier, 2 + (wide_peers if wide_peers else 0))
 
 
 def norm_parts(values):
@@ -87,13 +126,101 @@
     return pl.ds(pl.multiple_of(step * width, width), width)
 
 
-def front_kernel(length, tok, w_in, w_in_t, npar, x1, k_nat, v_nat, q_nat, q_t, k_t, out_t, lse, xbuf, v_t, probs, qbd, sem):
+def attention_block(length, shifted, pair, here, q_t, k_nat, v_t, out_t, lse, probs, qbd):
+    rows = key_chunk(length)
+    low = pair * PAIR
+    qbd[0:HEAD_DIM, 0:BLK] = q_t[low : low + HEAD_DIM, here]
+    qbd[HEAD_DIM:PAIR, BLK:WIDE_COLS] = q_t[low + HEAD_DIM : low + PAIR, here]
+    queries = qbd[...]
+
+    def scores(start):
+        return dot(k_nat[start : start + rows, low : low + PAIR], queries) * SCORE
+
+    top = jnp.zeros((1, WIDE_COLS), f32)
+    if shifted:
+        top = jnp.full((1, WIDE_COLS), -jnp.inf, f32)
+        for start in range(0, length, rows):
+            top = jnp.maximum(top, jnp.max(scores(start), axis=0, keepdims=True))
+    total = jnp.zeros((8, WIDE_COLS), f32)
+    for start in range(0, length, rows):
+        score = scores(start)
+        weight = jnp.exp2(score - top) if shifted else jnp.exp2(score)
+        total = total + row_sums(weight)
+        probs[start : start + rows, 0:WIDE_COLS] = weight.astype(bf16)
+    total = jnp.sum(total, axis=0, keepdims=True)
+    mixed = dot(v_t[low : low + PAIR, :], probs[:, 0:WIDE_COLS]) / total
+    out_t[low : low + HEAD_DIM, here] = mixed[0:HEAD_DIM, 0:BLK]
+    out_t[low + HEAD_DIM : low + PAIR, here] = mixed[HEAD_DIM:PAIR, BLK:WIDE_COLS]
+    log_total = top + jnp.log2(total)
+    lse[2 * pair : 2 * pair + 1, here] = log_total[:, 0:BLK]
+    lse[2 * pair + 1 : 2 * pair + 2, here] = log_total[:, BLK:WIDE_COLS]
+
+
+def front_kernel(
+    length,
+    tok,
+    own_in,
+    own_out,
+    own_up,
+    own_down,
+    npar,
+    w_in_out,
+    w_out,
+    w_up,
+    w_down,
+    x1,
+    k_nat,
+    v_nat,
+    q_nat,
+    q_t,
+    k_t,
+    v_t,
+    out_t,
+    lse,
+    xbuf,
+    probs,
+    qbd,
+    w_in,
+    low_out,
+    low_up,
+    low_down,
+    sem,
+    own_sem,
+    over_sem,
+    beside_sem,
+    pass_sem,
+):
     padded = x1.shape[0]
     blocks = padded // BLK
-    rows = key_chunk(length)
-    me = lax.axis_index("narrow")
+    me, _, _, over, beside = narrow_mates()
     copy = pltpu.make_async_copy(tok.at[me], xbuf.at[pl.ds(0, length)], sem)
     copy.start()
+
+    def slot(index, who):
+        if index == 0:
+            return w_in.at[:, pl.ds(pl.multiple_of(who * HEAD_DIM, HEAD_DIM), HEAD_DIM), :]
+        if index == 1:
+            return w_out.at[pl.ds(pl.multiple_of(who * HEAD_DIM, HEAD_DIM), HEAD_DIM), :]
+        if index == 2:
+            return w_up.at[:, pl.ds(pl.multiple_of(who * D, D), D)]
+        return w_down.at[pl.ds(pl.multiple_of(who * D, D), D), :]
+
+    def source(index):
+        return (slot(0, me), low_out, low_up, low_down)[index]
+
+    for which in range(3):
+        w_in[which, pl.ds(pl.multiple_of(me * HEAD_DIM, HEAD_DIM), HEAD_DIM), :] = own_in[which].astype(bf16)
+    low_out[...] = own_out[...].astype(bf16)
+    low_up[...] = own_up[...].astype(bf16)
+    low_down[...] = own_down[...].astype(bf16)
+    greet()
+    to_over = [remote(source(k), slot(k, me), over_sem, k, "narrow", over) for k in range(4)]
+    to_beside = [remote(source(k), slot(k, me), beside_sem, k, "narrow", beside) for k in range(4)]
+    passed = [remote(slot(k, over), slot(k, over), pass_sem, k, "narrow", beside) for k in range(4)]
+    mine = [pltpu.make_async_copy(source(k), slot(k, me), own_sem.at[k]) for k in range(1, 4)]
+    to_over[0].start()
+    to_beside[0].start()
+
     if padded > length:
         xbuf[length:, :] = jnp.zeros((padded - length, D), bf16)
         probs[length:, :] = jnp.zeros((padded - length, WIDE_COLS), bf16)
@@ -104,93 +231,108 @@
     shift = npar[1:2, :]
 
     @pl.loop(0, blocks)
+    def norm(step):
+        here = block_of(step)
+        xhat, _ = norm_parts(xbuf[here, :].astype(f32))
+        x1[here, :] = (xhat * gain + shift).astype(bf16)
+
+    to_over[0].wait_recv()
+    passed[0].start()
+    for k in range(1, 4):
+        to_over[k].start()
+        to_beside[k].start()
+        mine[k - 1].start()
+    to_beside[0].wait_recv()
+    passed[0].wait_recv()
+
+    @pl.loop(0, blocks)
     def project(step):
         here = block_of(step)
-        xhat, _ = norm_parts(xbuf[here, :].astype(f32))
-        act = (xhat * gain + shift).astype(bf16)
-        x1[here, :] = act
-        q_nat[here, :] = dot(act, w_in[0]).astype(bf16)
-        k_nat[here, :] = dot(act, w_in[1]).astype(bf16)
-        v_nat[here, :] = dot(act, w_in[2]).astype(bf16)
-        q_t[:, here] = dot(w_in_t[0], act, NT).astype(bf16)
-        k_t[:, here] = dot(w_in_t[1], act, NT).astype(bf16)
-        v_t[:, here] = dot(w_in_t[2], act, NT).astype(bf16)
-
+        act = x1[here, :]
+        q_nat[here, :] = dot(act, w_in[0], NT).astype(bf16)
+        k_nat[here, :] = dot(act, w_in[1], NT).astype(bf16)
+        v_nat[here, :] = dot(act, w_in[2], NT).astype(bf16)
+        q_t[:, here] = dot(w_in[0], act, NT).astype(bf16)
+        k_t[:, here] = dot(w_in[1], act, NT).astype(bf16)
+        v_t[:, here] = dot(w_in[2], act, NT).astype(bf16)
+
+    w_in_out[...] = w_in[...]
     if padded > length:
         v_t[:, length:] = jnp.zeros((D, padded - length), bf16)
 
-    def attend(shifted):
-        for pair in range(HEADS // 2):
-            low = pair * PAIR
-
-            @pl.loop(0, blocks)
-            def block(step):
-                here = block_of(step)
-                qbd[0:HEAD_DIM, 0:BLK] = q_t[low : low + HEAD_DIM, here]
-                qbd[HEAD_DIM:PAIR, BLK:WIDE_COLS] = q_t[low + HEAD_DIM : low + PAIR, here]
-                queries = qbd[...]
-
-                def scores(start):
-                    return dot(k_nat[start : start + rows, low : low + PAIR], queries) * SCORE
-
-                top = jnp.zeros((1, WIDE_COLS), f32)
-                if shifted:
-                    top = jnp.full((1, WIDE_COLS), -jnp.inf, f32)
-                    for start in range(0, length, rows):
-                        top = jnp.maximum(top, jnp.max(scores(start), axis=0, keepdims=True))
-                total = jnp.zeros((8, WIDE_COLS), f32)
-                for start in range(0, length, rows):
-                    score = scores(start)
-                    weight = jnp.exp2(score - top) if shifted else jnp.exp2(score)
-                    total = total + row_sums(weight)
-                    probs[start : start + rows, :] = weight.astype(bf16)
-                total = jnp.sum(total, axis=0, keepdims=True)
-                mixed = dot(v_t[low : low + PAIR, :], probs[...])
-                mixed = mixed / total
-                out_t[low : low + HEAD_DIM, here] = mixed[0:HEAD_DIM, 0:BLK]
-                out_t[low + HEAD_DIM : low + PAIR, here] = mixed[HEAD_DIM:PAIR, BLK:WIDE_COLS]
-                log_total = top + jnp.log2(total)
-                lse[2 * pair : 2 * pair + 1, here] = log_total[:, 0:BLK]
-                lse[2 * pair + 1 : 2 * pair + 2, here] = log_total[:, BLK:WIDE_COLS]
-
-    attend(False)
-    level = lse[...]
-    good = (level > -80.0) & (level < 120.0)
-    wrong = jnp.max(jnp.where(good, 0.0, 1.0))
-
-    @pl.when(wrong > 0.0)
-    def again():
-        attend(True)
-
-
-def front(tokens, w_in, w_in_t, npar):
+    for pair in range(HEADS // 2):
+
+        @pl.loop(0, blocks)
+        def block(step):
+            attention_block(length, False, pair, block_of(step), q_t, k_nat, v_t, out_t, lse, probs, qbd)
+
+        if pair == 0:
+            for k in range(1, 4):
+                to_over[k].wait_recv()
+                passed[k].start()
+
+    for k in range(1, 4):
+        to_beside[k].wait_recv()
+        passed[k].wait_recv()
+        mine[k - 1].wait()
+    for k in range(4):
+        to_over[k].wait_send()
+        to_beside[k].wait_send()
+        passed[k].wait_send()
+
+
+def front(tokens, own_in, own_out, own_up, own_down, npar):
     length = tokens.shape[1]
     padded = ceil_to(length, BLK)
     shape = jax.ShapeDtypeStruct
     return pl.pallas_call(
         functools.partial(front_kernel, length),
         out_shape=(
+            shape((3, D, D), bf16),
+            shape((D, D), bf16),
+            shape((D, FF), bf16),
+            shape((FF, D), bf16),
             shape((padded, D), bf16),
             shape((padded, D), bf16),
             shape((padded, D), bf16),
             shape((padded, D), bf16),
             shape((D, padded), bf16),
             shape((D, padded), bf16),
+            shape((D, padded), bf16),
             shape((D, padded), f32),
             shape((8, padded), f32),
         ),
-        in_specs=[pl.BlockSpec(memory_space=pl.ANY)] + vmem(3),
-        out_specs=tuple(vmem(8)),
+        in_specs=anywhere(1) + vmem(5),
+        out_specs=tuple(vmem(1) + anywhere(3) + vmem(9)),
         scratch_shapes=[
             pltpu.VMEM((padded, D), bf16),
-            pltpu.VMEM((D, padded), bf16),
             pltpu.VMEM((padded, WIDE_COLS), bf16),
             pltpu.VMEM((PAIR, WIDE_COLS), bf16),
+            pltpu.VMEM((3, D, D), bf16),
+            pltpu.VMEM(own_out.shape, bf16),
+            pltpu.VMEM(own_up.shape, bf16),
+            pltpu.VMEM(own_down.shape, bf16),
             pltpu.SemaphoreType.DMA,
+            pltpu.SemaphoreType.DMA((4,)),
+            pltpu.SemaphoreType.DMA((2, 4)),
+            pltpu.SemaphoreType.DMA((2, 4)),
+            pltpu.SemaphoreType.DMA((2, 4)),
         ],
-        compiler_params=params(),
+        compiler_params=params(collective_id=1, has_side_effects=True),
         name="front",
-    )(tokens, w_in, w_in_t, npar)
+    )(tokens, own_in, own_out, own_up, own_down, npar)
+
+
+def shared_rows(rows, wide):
+    return ceil_to(-(-rows // wide), 16) * wide
+
+
+def early_rows(wide):
+    return shared_rows(2 * D + HEAD_DIM, wide)
+
+
+def late_rows(wide):
+    return shared_rows(3 * HEAD_DIM + 8, wide)
 
 
 def softplus(values):
@@ -239,7 +381,11 @@
 def middle_kernel(
     length,
     tok,
-    out_t,
+    first_out_t,
+    first_lse,
+    q_t,
+    k_nat,
+    v_t,
     w_out,
     w_up,
     w_down,
@@ -252,12 +398,12 @@
     g_nat,
     g_t,
     delta,
-    grad_down,
-    grad_up,
-    grad_out,
+    lse,
+    early,
     grad_norm,
     grad_head,
     xbuf,
+    out_t,
     mixed_t,
     mid,
     res,
@@ -268,20 +414,46 @@
     grad_before,
     mid_low,
     logits,
+    qbd,
     sem,
+    out_sem,
 ):
     padded = xbuf.shape[0]
     blocks = padded // BLK
     me = lax.axis_index("narrow")
     copy = pltpu.make_async_copy(tok.at[me], xbuf.at[pl.ds(0, length)], sem)
     copy.start()
+    get_out = pltpu.make_async_copy(first_out_t, out_t, out_sem)
+    get_out.start()
     if padded > length:
         xbuf[length:, :] = jnp.zeros((padded - length, D), bf16)
     grad_norm[...] = jnp.zeros(grad_norm.shape, f32)
     grad_head[...] = jnp.zeros(grad_head.shape, f32)
     copy.wait()
+    get_out.wait()
     gain = npar[2:3, :]
     shift = npar[3:4, :]
+
+    level = first_lse[...]
+    lse[...] = level
+    good = (level > -80.0) & (level < 120.0)
+    wrong = jnp.max(jnp.where(good, 0.0, 1.0))
+
+    @pl.when(wrong > 0.0)
+    def again():
+        queries, keys, values = mixed_t, grad_before.at[:, 0:D], g_t
+        for src, dst in ((q_t, queries), (k_nat, keys), (v_t, values)):
+            fetch = pltpu.make_async_copy(src, dst, out_sem)
+            fetch.start()
+            fetch.wait()
+        if padded > length:
+            hidden[length:, 0:WIDE_COLS] = jnp.zeros((padded - length, WIDE_COLS), bf16)
+        qbd[...] = jnp.zeros(qbd.shape, bf16)
+        for pair in range(HEADS // 2):
+
+            @pl.loop(0, blocks)
+            def block(step):
+                attention_block(length, True, pair, block_of(step), queries, keys, values, out_t, lse, hidden, qbd)
 
     @pl.loop(0, blocks)
     def forward(step):
@@ -350,13 +522,21 @@
             axis=0,
         )
 
-    grad_mid[...] = mid[0:length, :]
-    grad_down[...] = dot(res_low[...], hidden[...], TN)
-    grad_up[...] = dot(act[...], grad_before[...], TN)
-    grad_out[...] = dot(mixed_t[...], mid_low[...])
-
-
-def middle_stage(tokens, out_t, w_out, w_up, w_down, npar, head, counts, library):
+    grad_mid[...] = mid[...]
+    grad_down = dot(res_low[...], hidden[...], TN)
+    grad_up = dot(act[...], grad_before[...], TN)
+    grad_out = dot(mixed_t[...], mid_low[...])
+    used = 2 * D + HEAD_DIM
+    for who in range(HEADS):
+        part = early.at[who % 2, who // 2]
+        part[0:D, :] = grad_down[:, who * D : (who + 1) * D]
+        part[D : 2 * D, :] = grad_up[:, who * D : (who + 1) * D]
+        part[2 * D : used, :] = grad_out[who * HEAD_DIM : (who + 1) * HEAD_DIM, :]
+        if early.shape[2] > used:
+            part[used:, :] = jnp.zeros((early.shape[2] - used, D), f32)
+
+
+def middle_stage(wide, tokens, out_t, lse, q_t, k_nat, v_t, w_out, w_up, w_down, npar, head, counts, library):
     length = tokens.shape[1]
     padded = out_t.shape[1]
     shape = jax.ShapeDtypeStruct
@@ -364,20 +544,20 @@
         functools.partial(middle_kernel, length),
         out_shape=(
             shape((length, D), bf16),
-            shape((length, D), f32),
+            shape((padded, D), f32),
             shape((padded, D), bf16),
             shape((D, padded), bf16),
             shape((8, padded), f32),
-            shape((D, FF), f32),
-            shape((D, FF), f32),
-            shape((D, D), f32),
+            shape((8, padded), f32),
+            shape((2, 2, early_rows(wide), D), f32),
             shape((16, D), f32),
             shape((8, D), f32),
         ),
-        in_specs=[pl.BlockSpec(memory_space=pl.ANY)] + vmem(8),
-        out_specs=tuple(vmem(10)),
+        in_specs=anywhere(2) + vmem(1) + anywhere(3) + vmem(7),
+        out_specs=tuple(vmem(9)),
         scratch_shapes=[
             pltpu.VMEM((padded, D), bf16),
+            pltpu.VMEM((D, padded), f32),
             pltpu.VMEM((D, padded), bf16),
             pltpu.VMEM((padded, D), f32),
             pltpu.VMEM((padded, D), f32),
@@ -388,51 +568,127 @@
             pltpu.VMEM((padded, FF), bf16),
             pltpu.VMEM((padded, D), bf16),
             pltpu.VMEM((8, padded), f32),
+            pltpu.VMEM((PAIR, WIDE_COLS), bf16),
+            pltpu.SemaphoreType.DMA,
             pltpu.SemaphoreType.DMA,
         ],
         compiler_params=params(),
         name="middle",
-    )(tokens, out_t, w_out, w_up, w_down, npar, head, counts, library)
-
-
-def back_kernel(
-    length,
-    tok,
-    x1,
-    k_nat,
-    v_nat,
-    q_nat,
-    q_t,
-    k_t,
-    g_nat,
-    g_t,
-    lse,
-    delta,
-    grad_mid,
-    w_in,
-    npar,
-    grad_input,
-    grad_in,
-    grad_norm,
-    xbuf,
-    probs,
-    dscore,
-    qbd,
-    gbd,
-    qnd,
-    gnd,
-    dk,
-    dv,
-    dq_t,
-    joined,
-    sem,
-):
+    )(tokens, out_t, lse, q_t, k_nat, v_t, w_out, w_up, w_down, npar, head, counts, library)
+
+
+class Shares:
+    def __init__(self, stack, bufs, sems, wide):
+        self.stack = stack
+        self.held, self.got, self.keep, self.send, self.come, self.parts, self.arrived, self.total = bufs
+        self.sems, self.wide = sems, wide
+        self.me, self.row, self.core, self.over, self.beside = narrow_mates()
+        self.place = lax.axis_index("wide")
+
+    def peer(self, step):
+        return lax.rem(self.place + step, self.wide)
+
+    def to_beside(self):
+        return remote(self.stack.at[1 - self.core], self.got, self.sems, 0, "narrow", self.beside)
+
+    def to_over(self):
+        return remote(self.send, self.come, self.sems, 1, "narrow", self.over)
+
+    def spread(self, step):
+        peer = self.peer(step)
+        return remote(
+            self.parts.at[peer], self.arrived.at[self.place], self.sems, 1 + step, "wide", peer
+        )
+
+    def share(self, step):
+        peer = self.peer(step)
+        mine = self.total.at[self.place]
+        return remote(mine, mine, self.sems, self.wide + step, "wide", peer)
+
+    def start_beside(self):
+        self.to_beside().start()
+
+    def start_over(self):
+        copy = self.to_beside()
+        copy.wait_recv()
+        self.send[...] = (self.held[1 - self.row] + self.got[1 - self.row]).astype(bf16)
+        self.to_over().start()
+        self.keep[...] = self.held[self.row] + self.got[self.row]
+
+    def start_spread(self):
+        self.to_over().wait_recv()
+        whole = (self.keep[...] + self.come[...].astype(f32)).astype(bf16)
+        self.parts[...] = whole.reshape(self.parts.shape)
+        for step in range(1, self.wide):
+            self.spread(step).start()
+        self.arrived[self.place] = self.parts[self.place]
+
+    def start_share(self):
+        for step in range(1, self.wide):
+            self.spread(step).wait_recv()
+        self.total[self.place] = jnp.sum(self.arrived[...].astype(f32), axis=0).astype(bf16)
+        for step in range(1, self.wide):
+            self.share(step).start()
+
+    def finish(self):
+        for step in range(1, self.wide):
+            self.share(step).wait_recv()
+
+    def settle(self):
+        self.to_beside().wait_send()
+        self.to_over().wait_send()
+        for step in range(1, self.wide):
+            self.spread(step).wait_send()
+            self.share(step).wait_send()
+
+
+def share_scratch(rows, wide, held):
+    own = [pltpu.VMEM((2, rows, D), f32)] if held else []
+    return own + [
+        pltpu.VMEM((2, rows, D), f32),
+        pltpu.VMEM((rows, D), f32),
+        pltpu.VMEM((rows, D), bf16),
+        pltpu.VMEM((rows, D), bf16),
+        pltpu.VMEM((wide, rows // wide, D), bf16),
+        pltpu.VMEM((wide, rows // wide, D), bf16),
+        pltpu.VMEM((wide, rows // wide, D), bf16),
+        pltpu.SemaphoreType.DMA((2, 2 * wide)),
+    ]
+
+
+def back_kernel(length, wide, *refs):
+    tok, out_own, early = refs[0:3]
+    x1, k_nat, v_nat, q_nat, q_t, k_t, g_nat, g_t, lse, delta, grad_mid, w_in, npar, norm_two, head_two = refs[3:18]
+    out_all, grad_all, early_sum, late_sum, squares_out = refs[18:23]
+    refs = refs[23:]
+    xbuf, probs, dscore, qbd, gbd, qnd, gnd, dk, dv, dq_t, joined, grad_low, norm_one, late, squares = refs[0:15]
+    sem, own_sems, out_sems, over_sems, beside_sems, pass_sems, square_sems = refs[15:22]
+    early_bufs = refs[22:30]
+    early_sems = refs[30]
+    late_bufs = refs[31:38]
+    late_sems = refs[38]
+
     padded = x1.shape[0]
     blocks = padded // BLK
     rows = key_chunk(length)
-    me = lax.axis_index("narrow")
+    chunks = length // rows
+    me, row, core, over, beside = narrow_mates()
     copy = pltpu.make_async_copy(tok.at[me], xbuf.at[pl.ds(0, length)], sem)
     copy.start()
+    hold = pltpu.make_async_copy(early.at[core], early_bufs[0], own_sems.at[0])
+    hold.start()
+    keep_out = pltpu.make_async_copy(out_own, out_all.at[me], own_sems.at[1])
+    keep_out.start()
+    greet(wide)
+    first = Shares(early, early_bufs, early_sems, wide)
+    last = Shares(late, (late.at[core],) + tuple(late_bufs), late_sems, wide)
+    out_over = remote(out_own, out_all.at[me], out_sems, 0, "narrow", over)
+    out_beside = remote(out_own, out_all.at[me], out_sems, 1, "narrow", beside)
+    out_pass = remote(out_all.at[over], out_all.at[over], out_sems, 2, "narrow", beside)
+    first.start_beside()
+    out_over.start()
+    out_beside.start()
+
     if padded > length:
         xbuf[length:, :] = jnp.zeros((padded - length, D), bf16)
         dscore[length:, :] = jnp.zeros((padded - length, WIDE_COLS), bf16)
@@ -440,8 +696,25 @@
         joined[2, length:, :] = jnp.zeros((padded - length, D), bf16)
     for ref in (qbd, gbd, qnd, gnd):
         ref[...] = jnp.zeros(ref.shape, bf16)
-    grad_norm[...] = jnp.zeros(grad_norm.shape, f32)
+    norm_one[...] = jnp.zeros(norm_one.shape, f32)
     scale = HEAD_DIM ** (-0.5)
+
+    def begin():
+        hold.wait()
+        first.start_over()
+
+    def hand_on():
+        out_over.wait_recv()
+        out_pass.start()
+
+    last_step = blocks - 1
+    events = {
+        (0, min(1, last_step)): begin,
+        (0, min(5, last_step)): first.start_spread,
+        (0, last_step): first.start_share,
+        (1, min(4, last_step)): first.finish,
+        (1, last_step): hand_on,
+    }
 
     for pair in range(HEADS // 2):
         low = pair * PAIR
@@ -453,6 +726,9 @@
         @pl.loop(0, blocks)
         def block(step):
             here = block_of(step)
+            for (which, when), event in events.items():
+                if which == pair:
+                    pl.when(step == when)(event)
             qbd[0:HEAD_DIM, 0:BLK] = q_t[low:mid, here]
             qbd[HEAD_DIM:PAIR, BLK:WIDE_COLS] = q_t[mid:top, here]
             gbd[0:HEAD_DIM, 0:BLK] = g_t[low:mid, here]
@@ -487,34 +763,104 @@
     copy.wait()
     gain = npar[0:1, :]
 
-    @pl.loop(0, blocks)
     def close(step):
         here = block_of(step)
         grad_q = dq_t[:, here].T
         joined[0, here, :] = grad_q
-        total = dot(grad_q, w_in[0], NT) + dot(joined[1, here, :], w_in[1], NT) + dot(joined[2, here, :], w_in[2], NT)
+        total = dot(grad_q, w_in[0]) + dot(joined[1, here, :], w_in[1]) + dot(joined[2, here, :], w_in[2])
         xhat, inverse = norm_parts(xbuf[here, :].astype(f32))
-        grad_norm[0:8, :] += row_sums(total * xhat)
-        grad_norm[8:16, :] += row_sums(total)
-        grad_input[here, :] = grad_mid[here, :] + norm_back(xhat, inverse, gain, total)
-
+        norm_one[0:8, :] += row_sums(total * xhat)
+        norm_one[8:16, :] += row_sums(total)
+        grad_low[here, :] = (grad_mid[here, :] + norm_back(xhat, inverse, gain, total)).astype(bf16)
+
+    def chunk(index, who):
+        return grad_all.at[who, pl.ds(index * rows, rows)]
+
+    def held(index):
+        return grad_low.at[pl.ds(index * rows, rows)]
+
+    to_over = [remote(held(k), chunk(k, me), over_sems, k, "narrow", over) for k in range(chunks)]
+    to_beside = [remote(held(k), chunk(k, me), beside_sems, k, "narrow", beside) for k in range(chunks)]
+    passed = [remote(chunk(k, over), chunk(k, over), pass_sems, k, "narrow", beside) for k in range(chunks)]
+    mine = pltpu.make_async_copy(grad_low.at[pl.ds(0, length)], grad_all.at[me], own_sems.at[2])
+
+    half = -(-blocks // 2)
+    ready = half * BLK // rows
+    pl.loop(0, half)(close)
+    for k in range(ready):
+        to_over[k].start()
+    pl.loop(half, blocks)(close)
+    mine.start()
+    for k in range(chunks):
+        to_beside[k].start()
+
+    late[...] = jnp.zeros(late.shape, f32)
     for which in range(3):
-        grad_in[which] = dot(joined[which], x1[...], TN)
-
-
-def back_stage(tokens, x1, k_nat, v_nat, q_nat, q_t, k_t, g_nat, g_t, lse, delta, grad_mid, w_in, npar):
-    length = tokens.shape[1]
-    padded = x1.shape[0]
+        grad_w = dot(joined[which], x1[...], TN)
+        for who in range(HEADS):
+            late[who % 2, who // 2, which * HEAD_DIM : (which + 1) * HEAD_DIM, :] = grad_w[
+                who * HEAD_DIM : (who + 1) * HEAD_DIM, :
+            ]
+    sums = [norm_one[0:8, :], norm_one[8:16, :], norm_two[0:8, :], norm_two[8:16, :]]
+    extra = jnp.concatenate([jnp.sum(v, axis=0, keepdims=True) for v in sums] + [head_two[0:4, :]], axis=0)
+    for who in range(HEADS):
+        late[who % 2, who // 2, 3 * HEAD_DIM : 3 * HEAD_DIM + 8, :] = extra
+    last.start_beside()
+    early_sum[...] = first.total[...].reshape(early_sum.shape)
+    last.start_over()
+    last.start_spread()
+    for k in range(ready, chunks):
+        to_over[k].start()
+    last.start_share()
+    for k in range(ready):
+        to_over[k].wait_recv()
+        passed[k].start()
+    last.finish()
+    late_sum[...] = last.total[...].reshape(late_sum.shape)
+    whole = early_sum[...].astype(f32)
+    part = late_sum[0 : 3 * HEAD_DIM, :].astype(f32)
+    level = jnp.sum(row_sums(whole * whole) + row_sums(part * part), axis=(0, 1), keepdims=True)
+    squares[me] = jnp.broadcast_to(level, squares.shape[1:])
+    told = []
+    for index, mate in enumerate((over, beside, (1 - row) * 2 + 1 - core)):
+        tell = remote(squares.at[me], squares.at[me], square_sems, index, "narrow", mate)
+        tell.start()
+        told.append(tell)
+    for k in range(ready, chunks):
+        to_over[k].wait_recv()
+        passed[k].start()
+    for tell in told:
+        tell.wait_recv()
+    squares_out[...] = squares[...]
+    keep_out.wait()
+    mine.wait()
+    out_beside.wait_recv()
+    out_pass.wait_recv()
+    for k in range(chunks):
+        to_beside[k].wait_recv()
+        passed[k].wait_recv()
+    for tell in told + [out_over, out_beside, out_pass] + to_over + to_beside + passed:
+        tell.wait_send()
+    first.settle()
+    last.settle()
+
+
+def back_stage(wide, tokens, out_own, early, *rest):
+    cells, length, _ = tokens.shape
+    padded = rest[0].shape[0]
+    chunks = length // key_chunk(length)
     shape = jax.ShapeDtypeStruct
     return pl.pallas_call(
-        functools.partial(back_kernel, length),
+        functools.partial(back_kernel, length, wide),
         out_shape=(
-            shape((padded, D), f32),
-            shape((3, D, D), f32),
-            shape((16, D), f32),
+            shape((cells, length, D), bf16),
+            shape((cells, length, D), bf16),
+            shape((early_rows(wide), D), bf16),
+            shape((late_rows(wide), D), bf16),
+            shape((HEADS, 8, 128), f32),
         ),
-        in_specs=[pl.BlockSpec(memory_space=pl.ANY)] + vmem(13),
-        out_specs=tuple(vmem(3)),
+        in_specs=anywhere(3) + vmem(15),
+        out_specs=tuple(anywhere(2) + vmem(3)),
         scratch_shapes=[
             pltpu.VMEM((padded, D), bf16),
             pltpu.VMEM((length, WIDE_COLS), bf16),
@@ -527,11 +873,23 @@
             pltpu.VMEM((length, PAIR), f32),
             pltpu.VMEM((D, padded), bf16),
             pltpu.VMEM((3, padded, D), bf16),
+            pltpu.VMEM((padded, D), bf16),
+            pltpu.VMEM((16, D), f32),
+            pltpu.VMEM((2, 2, late_rows(wide), D), f32),
+            pltpu.VMEM((HEADS, 8, 128), f32),
             pltpu.SemaphoreType.DMA,
-        ],
-        compiler_params=params(),
+            pltpu.SemaphoreType.DMA((3,)),
+            pltpu.SemaphoreType.DMA((2, 3)),
+            pltpu.SemaphoreType.DMA((2, chunks)),
+            pltpu.SemaphoreType.DMA((2, chunks)),
+            pltpu.SemaphoreType.DMA((2, chunks)),
+            pltpu.SemaphoreType.DMA((2, 3)),
+        ]
+        + share_scratch(early_rows(wide), wide, True)
+        + share_scratch(late_rows(wide), wide, False),
+        compiler_params=params(collective_id=2, has_side_effects=True),
         name="back",
-    )(tokens, x1, k_nat, v_nat, q_nat, q_t, k_t, g_nat, g_t, lse, delta, grad_mid, w_in, npar)
+    )(tokens, out_own, early, *rest)
 
 
 def adam_update(grad, first, second, weight, decay_rate, rate):
@@ -543,71 +901,118 @@
     return (first_new, second_new, weight - rate * (direction + decay_rate * weight))
 
 
-def average_update(average, weight_new, dim):
-    count = average.shape[dim]
-    piece = lax.dynamic_slice_in_dim(weight_new, lax.axis_index("wide") * count, count, dim)
-    return ema_keep * average + (1.0 - ema_keep) * piece
+def finish_kernel(early, late, squares, *refs):
+    ins, outs = refs[0:24], refs[24:]
+    grad_norm_ref, outs = outs[0], outs[1:]
+    place = lax.axis_index("wide")
+    whole = early[...].astype(f32)
+    small = late[...].astype(f32)
+    extra = small[3 * HEAD_DIM : 3 * HEAD_DIM + 8, :]
+    live = lax.broadcasted_iota(jnp.int32, extra.shape, 0) < 7
+    extra = jnp.where(live, extra, 0.0)
+    shards = jnp.sum(squares[...], axis=0)[0:1, 0:1]
+    grad_norm = jnp.sqrt(shards + jnp.sum(extra * extra, axis=(0, 1), keepdims=True))
+    grad_norm_ref[...] = grad_norm
+    factor = jnp.minimum(1.0, clip_limit / grad_norm)
+    grads = (
+        None,
+        whole[2 * D : 2 * D + HEAD_DIM, :],
+        whole[D : 2 * D, :],
+        whole[0:D, :].T,
+        extra[0:4, :],
+        extra[4:7, :],
+    )
+    decays = (weight_decay,) * 4 + (0.0, weight_decay)
+    rates = (learn_rate,) * 4 + (norm_rate, learn_rate)
+
+    def update(index, grad, at):
+        weight, first, second = ins[index][at], ins[6 + index][at], ins[12 + index][at]
+        clipped = grad * factor
+        first_new, second_new, weight_new = adam_update(clipped, first, second, weight, decays[index], rates[index])
+        outs[5 * index][at] = clipped
+        outs[5 * index + 1][at] = first_new
+        outs[5 * index + 2][at] = second_new
+        outs[5 * index + 3][at] = weight_new
+        return weight_new
+
+    def mean(index, at, piece):
+        outs[5 * index + 4][at] = ema_keep * ins[18 + index][at] + (1.0 - ema_keep) * piece
+
+    def rows_here(values, count):
+        return pltpu.roll(values, lax.rem(D - place * count, D), 0)[0:count, :]
+
+    for which in range(3):
+        weight_new = update(0, small[which * HEAD_DIM : (which + 1) * HEAD_DIM, :], which)
+        mean(0, which, rows_here(weight_new.T, ins[18].shape[1]))
+    for index in range(1, 4):
+        weight_new = update(index, grads[index], Ellipsis)
+        mean(index, Ellipsis, rows_here(weight_new if index == 2 else weight_new.T, ins[18 + index].shape[0]))
+    for index in range(4, 6):
+        weight_new = update(index, grads[index], Ellipsis)
+        rows, count = ins[18 + index].shape
+        full = jnp.concatenate([weight_new, jnp.zeros((8 - rows, D), f32)], axis=0)
+        turned = pltpu.roll(full, lax.rem(D - place * count, D), 1)
+        mean(index, Ellipsis, turned[0:rows, 0:count])
+
+
+def finish(early, late, squares, state):
+    shape = jax.ShapeDtypeStruct
+    outs = [shape((1, 1), f32)]
+    for index in range(6):
+        outs += [shape(state[index].shape, f32)] * 4 + [shape(state[18 + index].shape, f32)]
+    return pl.pallas_call(
+        finish_kernel,
+        out_shape=tuple(outs),
+        in_specs=vmem(27),
+        out_specs=tuple(vmem(31)),
+        compiler_params=params(),
+        name="finish",
+    )(early, late, squares, *state)
 
 
 def on_device(cell_tokens, library_size, gene_counts, *state):
-    weights, firsts, seconds, averages = state[0:6], state[6:12], state[12:18], state[18:24]
-    attend_in, attend_out, up_weight, down_weight, norm_params, head_weight = weights
+    turn = lambda v: jnp.swapaxes(v, -1, -2)
+    state = tuple(turn(v) if index in (0, 6, 12, 19, 21) else v for index, v in enumerate(state))
+    attend_in, attend_out, up_weight, down_weight, norm_params, head_weight = state[0:6]
     cells, length, _ = cell_tokens.shape
     padded = ceil_to(length, BLK)
     me = lax.axis_index("narrow")
-
-    w_in = lax.all_gather(attend_in.astype(bf16), "narrow", axis=2, tiled=True)
-    w_out = lax.all_gather(attend_out.astype(bf16), "narrow", axis=0, tiled=True)
-    w_up = lax.all_gather(up_weight.astype(bf16), "narrow", axis=1, tiled=True)
-    w_down = lax.all_gather(down_weight.astype(bf16), "narrow", axis=0, tiled=True)
-    w_in_t = w_in.transpose(0, 2, 1)
+    wide = lax.axis_size("wide")
     head = jnp.pad(head_weight, ((0, 5), (0, 0)))
     counts = lax.dynamic_slice_in_dim(gene_counts, me, 1, 0)
     counts = jnp.pad(counts, ((0, 0), (CLASS_TOK, padded - length)))
     library = lax.dynamic_slice_in_dim(library_size, me, 1, 0).reshape(1, 1)
 
-    x1, k_nat, v_nat, q_nat, q_t, k_t, out_t, lse = front(cell_tokens, w_in, w_in_t, norm_params)
-    out_own, grad_mid, g_nat, g_t, delta, grad_down, grad_up, grad_out, norm_two, grad_head = middle_stage(
-        cell_tokens, out_t, w_out, w_up, w_down, norm_params, head, counts, library
+    w_in, w_out, w_up, w_down, x1, k_nat, v_nat, q_nat, q_t, k_t, v_t, out_t, lse = front(
+        cell_tokens, attend_in, attend_out, up_weight, down_weight, norm_params
     )
-    output = lax.all_gather(out_own, "narrow")
-    grad_mid = jnp.pad(grad_mid, ((0, padded - length), (0, 0)))
-    grad_input, grad_in, norm_one = back_stage(
-        cell_tokens, x1, k_nat, v_nat, q_nat, q_t, k_t, g_nat, g_t, lse, delta, grad_mid, w_in, norm_params
+    out_own, grad_mid, g_nat, g_t, delta, lse, early, norm_two, head_two = middle_stage(
+        wide, cell_tokens, out_t, lse, q_t, k_nat, v_t, w_out, w_up, w_down, norm_params, head, counts, library
     )
-    input_grad = lax.all_gather(grad_input[:length].astype(bf16), "narrow").astype(f32)
-
-    narrow = lax.axis_size("narrow")
-    shard = lambda v, dim: lax.psum(lax.psum_scatter(v, "narrow", scatter_dimension=dim, tiled=True), "wide")
-    grad_in = shard(grad_in.transpose(0, 2, 1), 2)
-    grad_out = shard(grad_out, 0)
-    grad_up = shard(grad_up, 1)
-    grad_down = shard(grad_down.T, 0)
-    fold = lambda v: jnp.stack([jnp.sum(v[0:8], axis=0), jnp.sum(v[8:16], axis=0)])
-    grad_norms, grad_head = lax.psum(
-        (jnp.concatenate([fold(norm_one), fold(norm_two)], axis=0), grad_head[0:3]), ("wide", "narrow")
+    out_all, grad_all, early, late, squares = back_stage(
+        wide,
+        cell_tokens,
+        out_own,
+        early,
+        x1,
+        k_nat,
+        v_nat,
+        q_nat,
+        q_t,
+        k_t,
+        g_nat,
+        g_t,
+        lse,
+        delta,
+        grad_mid,
+        w_in,
+        norm_params,
+        norm_two,
+        head_two,
     )
-    sharded = (
-        jnp.sum(grad_in * grad_in)
-        + jnp.sum(grad_out * grad_out)
-        + jnp.sum(grad_up * grad_up)
-        + jnp.sum(grad_down * grad_down)
-    )
-    common = jnp.sum(grad_norms * grad_norms) + jnp.sum(grad_head * grad_head)
-    grad_norm = jnp.sqrt(lax.psum(sharded, "narrow") + common)
-    factor = jnp.minimum(1.0, clip_limit / grad_norm)
-    grads = (grad_in, grad_out, grad_up, grad_down, grad_norms, grad_head)
-    decays = (weight_decay,) * 4 + (0.0, weight_decay)
-    rates = (learn_rate,) * 4 + (norm_rate, learn_rate)
-    dims = (1, 1, 0, 1, 1, 1)
-    outs = [output, input_grad, grad_norm]
-    for index in range(6):
-        clipped = grads[index] * factor
-        first_new, second_new, weight_new = adam_update(
-            clipped, firsts[index], seconds[index], weights[index], decays[index], rates[index]
-        )
-        outs += [clipped, first_new, second_new, weight_new, average_update(averages[index], weight_new, dims[index])]
-    return tuple(outs)
+    grad_norm, *updates = finish(early, late, squares, state)
+    updates = [turn(v) if index in (0, 1, 2, 3, 9, 19) else v for index, v in enumerate(updates)]
+    return (out_all, grad_all.astype(f32), grad_norm.reshape(()), *updates)
 
 
 def solution(mesh):

time: 423 us -> 208 us (0.49)
  waiting for transfers between devices: 155 us -> 0 us
  blocking collectives: 75.8 us -> 0 us
  Pallas kernels: 131 us -> 195 us
  between operations: 20.4 us -> 0.75 us
  other arithmetic: 22.6 us -> 6.81 us
  local copies, waits for them, and re-layouts: 17.3 us -> 5.37 us
    reduce_scatter x4 -> x0, waiting for transfers between devices: 77.8 us -> none  [on_device(): lax.psum_scatter(v, 'narrow', scatter_dimension=dim, tiled=True)]
    pallas_call x1 -> x2, Pallas kernels: 62.5 us -> 121 us  [the longest x1 116 us: back_stage(): pl.pallas_call(functools.partial(back_kernel, length, wide), out_shape=(s...]
    psum x2 -> x0, blocking collectives: 46.4 us -> none  [the longest x1 39.5 us: on_device(): lax.psum((jnp.concatenate([fold(norm_one), fold(norm_two)], axis=0), grad...]
    all_gather x2 -> x0, waiting for transfers between devices: 42.6 us -> none  [the longest x1 31.3 us: on_device(): output = lax.all_gather(out_own, 'narrow')]
    psum x1 -> x0, waiting for transfers between devices: 33.1 us -> none  [on_device(): lax.psum(lax.psum_scatter(v, 'narrow', scatter_dimension=dim, tiled=True)...]
    all_gather x4 -> x0, blocking collectives: 29.4 us -> none  [the longest x1 8.07 us: on_device(): w_in = lax.all_gather(attend_in.astype(bf16), 'narrow', axis=2, tiled=True)]
    reduce_sum x8 -> x0, other arithmetic: 7.55 us -> none  [the longest x1 1.65 us: on_device(): jnp.sum(grad_down * grad_down)]
    sub x5 -> x0, other arithmetic: 5.16 us -> none  [adam_update(): weight - rate * (direction + decay_rate * weight)]
  transfers between devices with their start and end apart: 7 -> 0, of which waited for: 6 -> 0; matrix products, arithmetic and copies ran while one was open for 7% -> 0% of each run, Pallas kernels for 15% -> 0%
where the time goes in v2:
time: 208 us
  Pallas kernels  195 us (94%)
  other arithmetic  6.81 us (3%)
  local copies, waits for them, and re-layouts  5.37 us (3%)
    pallas_call x1, Pallas kernels, back_stage(): pl.pallas_call(functools.partial(back_kernel, length, wide), out_shape=(s...  116 us
    pallas_call x1, Pallas kernels, middle_stage(): pl.pallas_call(functools.partial(middle_kernel, length), out_shape=(shape...  38.9 us
    pallas_call x1, Pallas kernels, front(): pl.pallas_call(functools.partial(front_kernel, length), out_shape=(shape(...  35.4 us
    convert_element_type x1, other arithmetic, on_device(): return (out_all, grad_all.astype(f32), grad_norm.reshape(()), *updates)  6.8 us
    pallas_call x1, Pallas kernels, finish(): pl.pallas_call(finish_kernel, out_shape=tuple(outs), in_specs=vmem(27), o...  4.38 us

profile of v2, /device:TPU:0, one launch (start us, length us, event | category | flops | bytes accessed | tf_op | source)
XLA Modules:
  0.0 207.8 jit_solution(1992964219062232335)
XLA Ops:
  0.7 0.0 copy-start
  0.7 1.2 dynamic_slice.7
  1.9 1.3 pad.8.head
  3.2 0.0 copy-done
  3.2 0.7 pad.9.counts
  3.9 35.4 %front.1 = (bf16[3,256,256]{2,1,0:T(8,128)(2,1)}, bf16[256,256]{1,0:T(8,128)(2,1)}, bf16[256,1024]{1,0:T(8,128)(2,1)}, bf16[1024,256]{1,0:T(8,128)(2,1)}, bf16[2...) custom-call(bf16[4,2208,256]{2,1,0:T(8,128)(2,1)} %refs_0_.1, ...), custom_call_target="tpu_custom_call" | custom-call | tf_op jit(solution)/shard_map/front/pallas_call | solution.py:288
  39.3 38.9 %middle.1 = (bf16[2208,256]{1,0:T(8,128)(2,1)}, f32[2304,256]{1,0:T(8,128)}, bf16[2304,256]{1,0:T(8,128)(2,1)}, bf16[256,2304]{1,0:T(8,128)(2,1)}, f32[8,2304]{1...) custom-call(bf16[4,2208,256]{2,1,0:T(8,128)(2,1)} %refs_0_.1, ...), custom_call_target="tpu_custom_call" | custom-call | tf_op jit(solution)/shard_map/middle/pallas_call | solution.py:543
  78.3 116.2 %back.1 = (bf16[4,2208,256]{2,1,0:T(8,128)(2,1)}, bf16[4,2208,256]{2,1,0:T(8,128)(2,1)}, bf16[640,256]{1,0:T(8,128)(2,1)}, bf16[256,256]{1,0:T(8,128)(2,1)}, f32[4,8,128]{2,1,0:T(8,128)}) custom-call(bf16[4,2208,256]{2,1,0:T(8,128)(2,1)} %refs_0_.1, bf16[2208,256]{1,0:T(8,128)(2,1)} %get-tuple-element.99.refs_1_, ...), custom_call_target="tpu_custom_call" | custom-call | tf_op jit(solution)/shard_map/back/pallas_call | solution.py:853
  194.4 0.0 slice-start
  194.5 4.4 %finish.1 = (f32[1,1]{1,0:T(1,128)}, f32[3,64,256]{2,1,0:T(8,128)}, f32[3,64,256]{2,1,0:T(8,128)}, f32[3,64,256]{2,1,0:T(8,128)}, f32[3,64,256]{2,1,0:T(8,128)},...) custom-call(bf16[640,256]{1,0:T(8,128)(2,1)} %get-tuple-element.115., ...), custom_call_target="tpu_custom_call" | custom-call | tf_op jit(solution)/shard_map/finish/pallas_call | solution.py:963
  198.8 0.0 slice-start.1
  198.9 6.8 %convert_element_type.5 = f32[4,2208,256]{2,1,0:T(8,128)} convert(bf16[4,2208,256]{2,1,0:T(8,128)(2,1)} %get-tuple-element.114) | non-fusion elementwise | flops 2260992 | bytes 13565952 | tf_op jit(solution)/shard_map/convert_element_type | solution.py:1015
  205.7 0.0 slice-done
  205.7 0.0 slice-done.1
  205.7 2.1 %copy.61 = bf16[4,2208,256]{2,1,0:T(8,128)(2,1)} copy(bf16[4,2208,256]{2,1,0:T(8,128)(2,1)S(1)} %bitcast.14) | data formatting | bytes 9043968
  (2 shorter events, 0.0 us)
Async XLA Ops:
  0.7 2.6 %copy-start = (s32[4,2200]{1,0:T(4,128)S(1)}, s32[4,2200]{1,0:T(4,128)}, u32[]{:S(2)}) copy-start(s32[4,2200]{1,0:T(4,128)} %param.29) | copy-start | bytes 105604
  194.4 11.2 %slice-start = ((s8[4521984]{0:T(1024)(128)(4,1)}), s8[327680]{0:T(1024)(128)(4,1)S(1)}, s32[]{:S(2)}) async-start(s8[4521984]{0:T(1024)(128)(4,1)} %bitcast.13), calls=%async_computation | async-start | bytes 655360
  198.8 6.8 %slice-start.1 = ((s8[4521984]{0:T(1024)(128)(4,1)}), s8[4194304]{0:T(1024)(128)(4,1)S(1)}, s32[]{:S(2)}) async-start(s8[4521984]{0:T(1024)(128)(4,1)} %bitcast.13), calls=%async_computation.1 | async-start | bytes 8388608

commit v3 on v2

v3 whole, which is shorter than its diff:
```python
import functools

import jax
import jax.numpy as jnp
from jax import lax
from jax.experimental import pallas as pl
from jax.experimental.pallas import tpu as pltpu
from jax.sharding import PartitionSpec as P

D = 256
FF = 1024
HEADS = 4
HEAD_DIM = 64
CLASS_TOK = 8
STEP = 10

layer_eps = 1e-05
clip_limit = 0.25
decay_first = 0.9
decay_second = 0.999
learn_rate = 0.06
norm_rate = 0.6
adam_eps = 1e-08
weight_decay = 0.01
ema_keep = 0.75

f32 = jnp.float32
bf16 = jnp.bfloat16

NN = (((1,), (0,)), ((), ()))
NT = (((1,), (1,)), ((), ()))
TN = (((0,), (0,)), ((), ()))

BLK = 256
PAIR = 2 * HEAD_DIM
WIDE_COLS = 2 * BLK
LOG2E = 1.4426950408889634
SCORE = LOG2E * HEAD_DIM ** (-0.5)
GELU_A = 0.7978845608028654
GELU_B = 0.044715
GROUP = 3
VMEM_BYTES = 60 * 2**20


def dot(left, right, dims=NN, precision=None):
    return lax.dot_general(left, right, dims, precision=precision, preferred_element_type=f32)


def ceil_to(value, unit):
    return -(-value // unit) * unit


def key_chunk(length):
    for rows in (368, 464, 320, 592, 256, 224, 288, 208, 176, 128, 64, 48, 32, 16):
        if length % rows == 0:
            return rows
    return length


def vmem(count):
    return [pl.BlockSpec(memory_space=pltpu.VMEM)] * count


def params(**more):
    return pltpu.CompilerParams(vmem_limit_bytes=VMEM_BYTES, **more)


def anywhere(count):
    return [pl.BlockSpec(memory_space=pl.ANY)] * count


def remote(src, dst, sems, index, axis, peer):
    return pltpu.make_async_remote_copy(
        src_ref=src,
        dst_ref=dst,
        send_sem=sems.at[0, index],
        recv_sem=sems.at[1, index],
        device_id={axis: peer},
        device_id_type=pl.DeviceIdType.MESH,
    )


def narrow_mates():
    me = lax.axis_index("narrow")
    row, core = me // 2, me % 2
    return me, row, core, (1 - row) * 2 + core, row * 2 + 1 - core


def greet(wide_peers=0):
    _, _, _, over, beside = narrow_mates()
    barrier = pltpu.get_barrier_semaphore()
    mesh_id = pl.DeviceIdType.MESH
    pl.semaphore_signal(barrier, inc=1, device_id={"narrow": over}, device_id_type=mesh_id)
    pl.semaphore_signal(barrier, inc=1, device_id={"narrow": beside}, device_id_type=mesh_id)
    if wide_peers:
        place = lax.axis_index("wide")
        _, row, core, _, _ = narrow_mates()
        pl.semaphore_signal(
            barrier, inc=1, device_id={"narrow": (1 - row) * 2 + 1 - core}, device_id_type=mesh_id
        )
        for step in range(1, wide_peers):
            peer = lax.rem(place + step, wide_peers)
            pl.semaphore_signal(barrier, inc=1, device_id={"wide": peer}, device_id_type=mesh_id)
    pl.semaphore_wait(barrier, 2 + (wide_peers if wide_peers else 0))


def norm_parts(values):
    center = values - jnp.mean(values, axis=-1, keepdims=True)
    spread = jnp.mean(center * center, axis=-1, keepdims=True)
    inverse = lax.rsqrt(spread + layer_eps)
    return center * inverse, inverse


def norm_back(xhat, inverse, gain, grad):
    scaled = gain * grad
    mean_one = jnp.mean(scaled, axis=-1, keepdims=True)
    mean_two = jnp.mean(scaled * xhat, axis=-1, keepdims=True)
    return inverse * (scaled - mean_one - xhat * mean_two)


def row_sums(values):
    return jnp.sum(values.reshape(-1, 8, values.shape[-1]), axis=0)


def block_of(step, width=BLK):
    if isinstance(step, int):
        return pl.ds(step * width, width)
    return pl.ds(pl.multiple_of(step * width, width), width)


def attention_block(length, shifted, pair, here, q_t, k_nat, v_t, out_t, totals, probs, qbd):
    rows = key_chunk(length)
    low = pair * PAIR
    qbd[0:HEAD_DIM, 0:BLK] = q_t[low : low + HEAD_DIM, here]
    qbd[HEAD_DIM:PAIR, BLK:WIDE_COLS] = q_t[low + HEAD_DIM : low + PAIR, here]
    queries = qbd[...]

    def scores(start):
        return dot(k_nat[start : start + rows, low : low + PAIR], queries) * SCORE

    top = jnp.zeros((1, WIDE_COLS), f32)
    if shifted:
        top = jnp.full((1, WIDE_COLS), -jnp.inf, f32)
        for start in range(0, length, rows):
            top = jnp.maximum(top, jnp.max(scores(start), axis=0, keepdims=True))
    total = jnp.zeros((8, WIDE_COLS), f32)
    for start in range(0, length, rows):
        score = scores(start)
        weight = jnp.exp2(score - top) if shifted else jnp.exp2(score)
        total = total + row_sums(weight)
        probs[start : start + rows, 0:WIDE_COLS] = weight.astype(bf16)
    total = jnp.sum(total, axis=0, keepdims=True)
    mixed = dot(v_t[low : low + PAIR, :], probs[:, 0:WIDE_COLS]) / total
    out_t[low : low + HEAD_DIM, here] = mixed[0:HEAD_DIM, 0:BLK]
    out_t[low + HEAD_DIM : low + PAIR, here] = mixed[HEAD_DIM:PAIR, BLK:WIDE_COLS]
    totals[2 * pair : 2 * pair + 1, here] = total[:, 0:BLK]
    totals[2 * pair + 1 : 2 * pair + 2, here] = total[:, BLK:WIDE_COLS]


def front_kernel(
    length,
    tok,
    far_in,
    far_out,
    far_up,
    far_down,
    npar,
    w_out,
    w_up,
    w_down,
    *refs,
):
    weights, outs, refs = refs[0], refs[1:11], refs[11:]
    x1, k_nat, v_nat, q_nat, q_t, k_t, v_t, w_in, out_t, totals = refs[0:10]
    xbuf, probs, qbd, low_out, low_up, low_down, sem, own_sem, over_sem, beside_sem, pass_sem, save_sems = refs[10:22]
    weight_sems = refs[22]
    own_in, own_out, own_up, own_down = refs[23:27]
    padded = x1.shape[0]
    blocks = padded // BLK
    me, _, _, over, beside = narrow_mates()
    gets = save((far_in,), (own_in,), own_sem, 0)
    copy = pltpu.make_async_copy(tok.at[me], xbuf.at[pl.ds(0, length)], sem)
    copy.start()
    gets += save((far_out, far_up, far_down), (own_out, own_up, own_down), own_sem, 1)

    def slot(index, who):
        if index == 0:
            return w_in.at[:, pl.ds(pl.multiple_of(who * HEAD_DIM, HEAD_DIM), HEAD_DIM), :]
        if index == 1:
            return w_out.at[pl.ds(pl.multiple_of(who * HEAD_DIM, HEAD_DIM), HEAD_DIM), :]
        if index == 2:
            return w_up.at[:, pl.ds(pl.multiple_of(who * D, D), D)]
        return w_down.at[pl.ds(pl.multiple_of(who * D, D), D), :]

    def source(index):
        return (slot(0, me), low_out, low_up, low_down)[index]

    gets[0].wait()
    for which in range(3):
        w_in[which, pl.ds(pl.multiple_of(me * HEAD_DIM, HEAD_DIM), HEAD_DIM), :] = own_in[which].astype(bf16)
    greet()
    to_over = [remote(source(k), slot(k, me), over_sem, k, "narrow", over) for k in range(4)]
    to_beside = [remote(source(k), slot(k, me), beside_sem, k, "narrow", beside) for k in range(4)]
    passed = [remote(slot(k, over), slot(k, over), pass_sem, k, "narrow", beside) for k in range(4)]
    mine = [pltpu.make_async_copy(source(k), slot(k, me), own_sem.at[k]) for k in range(1, 4)]
    to_over[0].start()
    to_beside[0].start()
    for get in gets[1:]:
        get.wait()
    low_out[...] = own_out[...].astype(bf16)
    low_up[...] = own_up[...].astype(bf16)
    low_down[...] = own_down[...].astype(bf16)

    if padded > length:
        xbuf[length:, :] = jnp.zeros((padded - length, D), bf16)
        probs[:, :, length:, :] = jnp.zeros((2, HEADS // 2, padded - length, WIDE_COLS), bf16)
    qbd[...] = jnp.zeros(qbd.shape, bf16)
    totals[...] = jnp.ones(totals.shape, f32)
    copy.wait()
    gain = npar[0:1, :]
    shift = npar[1:2, :]

    @pl.loop(0, blocks)
    def norm(step):
        here = block_of(step)
        xhat, _ = norm_parts(xbuf[here, :].astype(f32))
        x1[here, :] = (xhat * gain + shift).astype(bf16)

    to_over[0].wait_recv()
    passed[0].start()
    for k in range(1, 4):
        to_over[k].start()
        to_beside[k].start()
        mine[k - 1].start()
    to_beside[0].wait_recv()
    passed[0].wait_recv()

    @pl.loop(0, blocks // GROUP)
    def project(step):
        here = block_of(step, GROUP * BLK)
        act = x1[here, :]
        q_nat[here, :] = dot(act, w_in[0], NT).astype(bf16)
        k_nat[here, :] = dot(act, w_in[1], NT).astype(bf16)
        v_nat[here, :] = dot(act, w_in[2], NT).astype(bf16)
        q_t[:, here] = dot(w_in[0], act, NT).astype(bf16)
        k_t[:, here] = dot(w_in[1], act, NT).astype(bf16)
        v_t[:, here] = dot(w_in[2], act, NT).astype(bf16)

    if padded > length:
        v_t[:, length:] = jnp.zeros((D, padded - length), bf16)

    half = (blocks // 2) * BLK

    def keep(step, pair, slot):
        return pltpu.make_async_copy(
            probs.at[slot, pair, pl.ds(0, length)], weights.at[step, pair], weight_sems.at[slot, pair]
        )

    def attend(step):
        here = block_of(step)
        slot = lax.rem(step, 2)

        @pl.when(step >= 2)
        def free():
            for pair in range(HEADS // 2):
                keep(step - 2, pair, slot).wait()

        for pair in range(HEADS // 2):
            attention_block(
                length, False, pair, here, q_t, k_nat, v_t, out_t, totals, probs.at[slot, pair], qbd.at[pair]
            )
            keep(step, pair, slot).start()

    saves = save((x1, k_nat, v_nat, q_nat, q_t, k_t, v_t, w_in), outs[0:8], save_sems, 0)
    pl.loop(0, blocks // 2)(attend)
    for k in range(1, 4):
        to_over[k].wait_recv()
        passed[k].start()
    saves += save((out_t.at[:, 0:half],), (outs[8].at[:, 0:half],), save_sems, 8)
    pl.loop(blocks // 2, blocks)(attend)
    saves += save((out_t.at[:, half:], totals), (outs[8].at[:, half:], outs[9]), save_sems, 9)
    for step in range(max(0, blocks - 2), blocks):
        for pair in range(HEADS // 2):
            keep(step, pair, step % 2).wait()
    for copy in saves:
        copy.wait()
    for k in range(1, 4):
        to_beside[k].wait_recv()
        passed[k].wait_recv()
        mine[k - 1].wait()
    for k in range(4):
        to_over[k].wait_send()
        to_beside[k].wait_send()
        passed[k].wait_send()


def save(sources, targets, sems, first):
    copies = [
        pltpu.make_async_copy(src, dst, sems.at[first + k]) for k, (src, dst) in enumerate(zip(sources, targets))
    ]
    for copy in copies:
        copy.start()
    return copies


def front(tokens, own_in, own_out, own_up, own_down, npar):
    length = tokens.shape[1]
    padded = ceil_to(length, BLK)
    shape = jax.ShapeDtypeStruct
    kept = (
        [((padded, D), bf16)] * 4
        + [((D, padded), bf16)] * 3
        + [((3, D, D), bf16), ((D, padded), f32), ((8, padded), f32)]
    )
    return pl.pallas_call(
        functools.partial(front_kernel, length),
        out_shape=tuple(
            [shape((D, D), bf16), shape((D, FF), bf16), shape((FF, D), bf16)]
            + [shape((padded // BLK, HEADS // 2, length, WIDE_COLS), bf16)]
            + [shape(*what) for what in kept]
        ),
        in_specs=anywhere(5) + vmem(1),
        out_specs=tuple(anywhere(14)),
        scratch_shapes=[pltpu.VMEM(*what) for what in kept]
        + [
            pltpu.VMEM((padded, D), bf16),
            pltpu.VMEM((2, HEADS // 2, padded, WIDE_COLS), bf16),
            pltpu.VMEM((HEADS // 2, PAIR, WIDE_COLS), bf16),
            pltpu.VMEM(own_out.shape, bf16),
            pltpu.VMEM(own_up.shape, bf16),
            pltpu.VMEM(own_down.shape, bf16),
            pltpu.SemaphoreType.DMA,
            pltpu.SemaphoreType.DMA((4,)),
            pltpu.SemaphoreType.DMA((2, 4)),
            pltpu.SemaphoreType.DMA((2, 4)),
            pltpu.SemaphoreType.DMA((2, 4)),
            pltpu.SemaphoreType.DMA((11,)),
            pltpu.SemaphoreType.DMA((2, HEADS // 2)),
            pltpu.VMEM(own_in.shape, f32),
            pltpu.VMEM(own_out.shape, f32),
            pltpu.VMEM(own_up.shape, f32),
            pltpu.VMEM(own_down.shape, f32),
        ],
        compiler_params=params(collective_id=1, has_side_effects=True),
        name="front",
    )(tokens, own_in, own_out, own_up, own_down, npar)


def shared_rows(rows, wide):
    return ceil_to(-(-rows // wide), 16) * wide


def early_rows(wide):
    return shared_rows(2 * D + HEAD_DIM, wide)


def late_rows(wide):
    return shared_rows(3 * HEAD_DIM + 16, wide)


def split(values):
    high = values.astype(bf16)
    return high, (values - high.astype(f32)).astype(bf16)


def softplus(values):
    return jnp.maximum(values, 0.0) + jnp.log1p(jnp.exp(-jnp.abs(values)))


def sigmoid(values):
    return 1.0 / (1.0 + jnp.exp(-values))


def head_grads(logits, counts, library, genes, length):
    lane = lax.broadcasted_iota(jnp.int32, logits[0].shape, 1)
    valid = (lane >= CLASS_TOK) & (lane < length)
    mean_logit = jnp.where(valid, logits[0], -jnp.inf)
    top = jnp.max(mean_logit, axis=1, keepdims=True)
    raised = jnp.exp(mean_logit - top)
    total = jnp.sum(raised, axis=1, keepdims=True)
    share = raised / total
    log_mean = jnp.where(valid, logits[0], 0.0) - top - jnp.log(total) + jnp.log(library)
    disp = 0.5 + softplus(logits[1])
    log_disp = jnp.log(disp)
    inflate = logits[2]
    gap = log_mean - log_disp
    mean_part = sigmoid(gap)
    disp_part = sigmoid(-gap)
    log_both = jnp.maximum(log_disp, log_mean) + jnp.log1p(jnp.exp(-jnp.abs(gap)))
    shared = disp * (log_disp - log_both)
    shared_disp = (log_disp - log_both) + mean_part
    shared_mean = -disp * mean_part
    none = counts == 0.0
    lean = sigmoid(shared - inflate)
    psi = jnp.zeros_like(disp)
    for step in range(7):
        psi = psi + jnp.where(counts > step, 1.0 / (disp + step), 0.0)
    grad_disp = jnp.where(none, -lean * shared_disp, counts * disp_part / disp - shared_disp - psi)
    grad_mean = jnp.where(none, -lean * shared_mean, -shared_mean - counts * disp_part)
    grad_inflate = jnp.where(none, lean - sigmoid(-inflate), sigmoid(inflate))
    part = 1.0 / genes
    grad_disp = jnp.where(valid, grad_disp * part, 0.0)
    grad_mean = jnp.where(valid, grad_mean * part, 0.0)
    grad_inflate = jnp.where(valid, grad_inflate * part, 0.0)
    grad_zero = grad_mean - share * jnp.sum(grad_mean, axis=1, keepdims=True)
    return (grad_zero, grad_disp * sigmoid(logits[1]), grad_inflate)


def middle_kernel(
    length,
    tok,
    first_out_t,
    first_totals,
    q_t,
    k_nat,
    v_t,
    weights,
    far_out,
    far_up,
    far_down,
    npar,
    head,
    counts,
    library,
    output,
    grad_mid,
    g_nat_out,
    g_t_out,
    early,
    weights_out,
    delta,
    inverse_totals,
    grad_norm,
    grad_head,
    xbuf,
    out_t,
    totals,
    g_nat,
    g_t,
    early_buf,
    mixed_t,
    mid,
    res_high,
    res_rest,
    act,
    hidden,
    slope,
    res_low,
    grad_before,
    mid_low,
    logits,
    downs,
    counted,
    qbd,
    w_out,
    w_up,
    w_down,
    sem,
    out_sem,
    send_sems,
):
    padded = xbuf.shape[0]
    blocks = padded // BLK
    me = lax.axis_index("narrow")
    copy = pltpu.make_async_copy(tok.at[me], xbuf.at[pl.ds(0, length)], sem)
    copy.start()
    get_out = pltpu.make_async_copy(first_out_t, out_t, out_sem)
    get_out.start()
    get_weights = save((far_out, far_up, far_down), (w_out, w_up, w_down), send_sems, 0)
    if padded > length:
        xbuf[length:, :] = jnp.zeros((padded - length, D), bf16)
    grad_norm[...] = jnp.zeros(grad_norm.shape, f32)
    copy.wait()
    get_out.wait()
    for get in get_weights:
        get.wait()
    gain = npar[2:3, :]
    shift = npar[3:4, :]

    level = first_totals[...]
    totals[...] = level
    good = (level > 1e-25) & (level < 1e36)
    wrong = jnp.max(jnp.where(good, 0.0, 1.0))

    @pl.when(wrong > 0.0)
    def again():
        queries, keys, values = mixed_t, grad_before.at[:, 0:D], g_t
        for src, dst in ((q_t, queries), (k_nat, keys), (v_t, values)):
            fetch = pltpu.make_async_copy(src, dst, out_sem)
            fetch.start()
            fetch.wait()
        if padded > length:
            hidden[length:, 0:WIDE_COLS] = jnp.zeros((padded - length, WIDE_COLS), bf16)
        qbd[...] = jnp.zeros(qbd.shape, bf16)
        for pair in range(HEADS // 2):

            @pl.loop(0, blocks)
            def block(step):
                attention_block(length, True, pair, block_of(step), queries, keys, values, out_t, totals, hidden, qbd)
                keep = pltpu.make_async_copy(
                    hidden.at[pl.ds(0, length), 0:WIDE_COLS], weights_out.at[step, pair], out_sem
                )
                keep.start()
                keep.wait()

    inverse_totals[...] = 1.0 / totals[...]
    place = lax.axis_index("narrow")
    counted[...] = jnp.zeros(counted.shape, f32)
    counted[:, CLASS_TOK:length] = counts[pl.ds(place, 1), :].astype(f32)
    head_parts = split(jnp.concatenate([head[...], jnp.zeros((5, D), f32)], axis=0))
    head_rows = jnp.concatenate(head_parts, axis=0)
    head_cols = jnp.concatenate([head_rows, jnp.zeros((128 - 16, D), bf16)], axis=0)
    head_deep = jnp.concatenate([head_parts[0], head_parts[1], head_parts[0], head_parts[1]], axis=0)

    @pl.loop(0, blocks // GROUP)
    def forward(step):
        spots = [block_of(step * GROUP + k) for k in range(GROUP)]
        middles, lows, befores, hids, results = [], [], [], [], []
        for here in spots:
            mixed = out_t[:, here].astype(bf16)
            mixed_t[:, here] = mixed
            middle = xbuf[here, :].astype(f32) + dot(mixed, w_out[...], TN)
            mid[here, :] = middle
            middles.append(middle)
        for here, middle in zip(spots, middles):
            xhat, _ = norm_parts(middle)
            low = (xhat * gain + shift).astype(bf16)
            act[here, :] = low
            lows.append(low)
        for here, low, middle in zip(spots, lows, middles):
            before = dot(low, w_up[...])
            square = before * before
            half = 0.5 + 0.5 * jnp.tanh(before * (GELU_A + (GELU_A * GELU_B) * square))
            wide = before * half
            hid = wide.astype(bf16)
            hidden[here, :] = hid
            bend = half + (wide - wide * half) * (2.0 * GELU_A + (6.0 * GELU_A * GELU_B) * square)
            slope[here, :] = bend
            results.append(middle + dot(hid, w_down[...]))
        for here, result in zip(spots, results):
            high, rest = split(result)
            res_high[here, :] = high
            res_rest[here, :] = rest
            found = dot(high, head_cols, NT) + dot(rest, head_cols, NT)
            found = found.T
            logits[:, here] = found[0:8, :] + found[8:16, :]

    send_out = pltpu.make_async_copy(res_high.at[pl.ds(0, length)], output, sem)
    send_out.start()
    genes = length - CLASS_TOK
    zero, disp, inflate = head_grads(
        (logits[0:1, :], logits[1:2, :], logits[2:3, :]),
        counted[...],
        jnp.full((1, 128), library[place].astype(f32))[:, 0:1],
        genes,
        length,
    )
    down_high, down_rest = split(jnp.concatenate([zero, disp, inflate, jnp.zeros((5, padded), f32)], axis=0))
    downs[0:8, :] = down_high
    downs[8:16, :] = down_rest

    @pl.loop(0, blocks // GROUP)
    def backward(step):
        spots = [block_of(step * GROUP + k) for k in range(GROUP)]
        grads, backs, twos, lows = [], [], [], []
        for here in spots:
            both = downs[:, here]
            deep = jnp.concatenate([both[0:8], both[0:8], both[8:16], both[8:16]], axis=0)
            grad_res = dot(deep, head_deep, TN)
            low = grad_res.astype(bf16)
            res_low[here, :] = low
            grads.append(grad_res)
            lows.append(low)
        for here, low in zip(spots, lows):
            back = (slope[here, :] * dot(low, w_down[...], NT)).astype(bf16)
            grad_before[here, :] = back
            backs.append(back)
        for back in backs:
            twos.append(dot(back, w_up[...], NT))
        lows = []
        for here, grad_two, grad_res in zip(spots, twos, grads):
            xhat, inverse = norm_parts(mid[here, :])
            grad_norm[0:8, :] += row_sums(grad_two * xhat)
            grad_norm[8:16, :] += row_sums(grad_two)
            total = grad_res + norm_back(xhat, inverse, gain, grad_two)
            mid[here, :] = total
            total_low = total.astype(bf16)
            mid_low[here, :] = total_low
            lows.append(total_low)
        for here, total_low in zip(spots, lows):
            grad_t = dot(w_out[...], total_low, NT).astype(bf16)
            g_t[:, here] = grad_t
            grad_t = grad_t.astype(f32)
            shares = [
                grad_t[h * HEAD_DIM : (h + 1) * HEAD_DIM] * inverse_totals[h : h + 1, here] for h in range(HEADS)
            ]
            g_nat[here, :] = jnp.concatenate(shares, axis=0).astype(bf16).T
            inner = grad_t * out_t[:, here]
            delta[:, here] = jnp.concatenate(
                [
                    jnp.sum(inner[h * HEAD_DIM : (h + 1) * HEAD_DIM], axis=0, keepdims=True)
                    for h in range(HEADS)
                ]
                + [jnp.zeros((8 - HEADS, BLK), f32)],
                axis=0,
            )

    sends = [
        pltpu.make_async_copy(src, dst, send_sems.at[index])
        for index, (src, dst) in enumerate(((mid, grad_mid), (g_nat, g_nat_out), (g_t, g_t_out)))
    ]
    for send in sends:
        send.start()
    found = dot(downs[...], res_high[...]) + dot(downs[...], res_rest[...])
    grad_head[...] = found[0:8, :] + found[8:16, :]
    used = 2 * D + HEAD_DIM
    if early.shape[2] > used:
        early_buf[:, :, used:, :] = jnp.zeros((2, 2, early.shape[2] - used, D), f32)

    def put(index, begin, end, pieces):
        for who in range(HEADS):
            early_buf[who % 2, who // 2, begin : begin + pieces[who].shape[0], :] = pieces[who]
        part = (slice(None), slice(None), pl.ds(begin, end - begin))
        return save((early_buf.at[part],), (early.at[part],), send_sems, index)

    grad = dot(res_low[...], hidden[...], TN)
    sends += put(3, 0, D, [grad[:, who * D : (who + 1) * D] for who in range(HEADS)])
    grad = dot(act[...], grad_before[...], TN)
    sends += put(4, D, 2 * D, [grad[:, who * D : (who + 1) * D] for who in range(HEADS)])
    grad = dot(mixed_t[...], mid_low[...])
    sends += put(
        5, 2 * D, early.shape[2], [grad[who * HEAD_DIM : (who + 1) * HEAD_DIM, :] for who in range(HEADS)]
    )
    for send in [send_out] + sends:
        send.wait()


def middle_stage(wide, tokens, out_t, totals, q_t, k_nat, v_t, weights, w_out, w_up, w_down, npar, head, counts, library):
    length = tokens.shape[1]
    padded = out_t.shape[1]
    shape = jax.ShapeDtypeStruct
    return pl.pallas_call(
        functools.partial(middle_kernel, length),
        out_shape=(
            shape((length, D), bf16),
            shape((padded, D), f32),
            shape((padded, D), bf16),
            shape((D, padded), bf16),
            shape((2, 2, early_rows(wide), D), f32),
            shape(weights.shape, bf16),
            shape((8, padded), f32),
            shape((8, padded), f32),
            shape((16, D), f32),
            shape((8, D), f32),
        ),
        in_specs=anywhere(2) + vmem(1) + anywhere(7) + vmem(3) + [pl.BlockSpec(memory_space=pltpu.SMEM)],
        out_specs=tuple(anywhere(6) + vmem(4)),
        input_output_aliases={6: 5},
        scratch_shapes=[
            pltpu.VMEM((padded, D), bf16),
            pltpu.VMEM((D, padded), f32),
            pltpu.VMEM((8, padded), f32),
            pltpu.VMEM((padded, D), bf16),
            pltpu.VMEM((D, padded), bf16),
            pltpu.VMEM((2, 2, early_rows(wide), D), f32),
            pltpu.VMEM((D, padded), bf16),
            pltpu.VMEM((padded, D), f32),
            pltpu.VMEM((padded, D), bf16),
            pltpu.VMEM((padded, D), bf16),
            pltpu.VMEM((padded, D), bf16),
            pltpu.VMEM((padded, FF), bf16),
            pltpu.VMEM((padded, FF), f32),
            pltpu.VMEM((padded, D), bf16),
            pltpu.VMEM((padded, FF), bf16),
            pltpu.VMEM((padded, D), bf16),
            pltpu.VMEM((8, padded), f32),
            pltpu.VMEM((16, padded), bf16),
            pltpu.VMEM((1, padded), f32),
            pltpu.VMEM((PAIR, WIDE_COLS), bf16),
            pltpu.VMEM(w_out.shape, bf16),
            pltpu.VMEM(w_up.shape, bf16),
            pltpu.VMEM(w_down.shape, bf16),
            pltpu.SemaphoreType.DMA,
            pltpu.SemaphoreType.DMA,
            pltpu.SemaphoreType.DMA((6,)),
        ],
        compiler_params=params(),
        name="middle",
    )(tokens, out_t, totals, q_t, k_nat, v_t, weights, w_out, w_up, w_down, npar, head, counts, library)


class Shares:
    def __init__(self, stack, bufs, sems, wide):
        self.stack = stack
        self.held, self.got, self.keep, self.send, self.come, self.parts, self.arrived, self.total = bufs
        self.sems, self.wide = sems, wide
        self.me, self.row, self.core, self.over, self.beside = narrow_mates()
        self.place = lax.axis_index("wide")

    def peer(self, step):
        return lax.rem(self.place + step, self.wide)

    def to_beside(self):
        return remote(self.stack.at[1 - self.core], self.got, self.sems, 0, "narrow", self.beside)

    def to_over(self):
        return remote(self.send, self.come, self.sems, 1, "narrow", self.over)

    def spread(self, step):
        peer = self.peer(step)
        return remote(
            self.parts.at[peer], self.arrived.at[self.place], self.sems, 1 + step, "wide", peer
        )

    def share(self, step):
        peer = self.peer(step)
        mine = self.total.at[self.place]
        return remote(mine, mine, self.sems, self.wide + step, "wide", peer)

    def start_beside(self):
        self.to_beside().start()

    def finish(self):
        for step in range(1, self.wide):
            self.share(step).wait_recv()

    def settle(self):
        self.to_beside().wait_send()
        self.to_over().wait_send()
        for step in range(1, self.wide):
            self.spread(step).wait_send()
            self.share(step).wait_send()

    def start_spreads(self):
        for step in range(1, self.wide):
            self.spread(step).start()
        self.arrived[self.place] = self.parts[self.place]

    def arrive(self):
        for step in range(1, self.wide):
            self.spread(step).wait_recv()
        return jnp.sum(self.arrived[...].astype(f32), axis=0)

    def start_shares(self, mine):
        self.total[self.place] = mine.astype(bf16)
        for step in range(1, self.wide):
            self.share(step).start()


class RowFirst(Shares):
    def start_over(self):
        self.to_beside().wait_recv()
        def both(row):
            return self.held[row].astype(f32) + self.got[row].astype(f32)

        self.send[...] = both(1 - self.row).astype(bf16)
        self.to_over().start()
        self.keep[...] = both(self.row)

    def start_spread(self):
        self.to_over().wait_recv()
        whole = (self.keep[...] + self.come[...].astype(f32)).astype(bf16)
        self.parts[...] = whole.reshape(self.parts.shape)
        self.start_spreads()

    def start_share(self):
        self.start_shares(self.arrive())


class WideFirst(Shares):
    def start_spread(self):
        self.to_beside().wait_recv()
        depth = self.parts.shape[2]
        for row in range(2):
            whole = (self.held[row] + self.got[row]).astype(bf16)
            for place in range(self.wide):
                self.parts[place, row] = whole[place * depth : (place + 1) * depth, :]
        self.start_spreads()

    def start_over(self):
        self.keep[...] = self.arrive()
        self.send[...] = self.keep[1 - self.row].astype(bf16)
        self.to_over().start()

    def start_share(self):
        self.to_over().wait_recv()
        self.start_shares(self.keep[self.row] + self.come[...].astype(f32))


def share_scratch(rows, wide, wide_first):
    depth = rows // wide
    if wide_first:
        shapes = [((2, rows, D), f32), ((2, rows, D), f32), ((2, depth, D), f32)]
        shapes += [((depth, D), bf16)] * 2 + [((wide, 2, depth, D), bf16)] * 2 + [((wide, depth, D), bf16)]
    else:
        shapes = [((2, rows, D), bf16), ((rows, D), f32)] + [((rows, D), bf16)] * 2 + [((wide, depth, D), bf16)] * 3
    return [pltpu.VMEM(*what) for what in shapes] + [pltpu.SemaphoreType.DMA((2, 2 * wide))]


SIDE = 1
STAGES = 3


def cuts_of(length):
    blocks = -(-length // BLK)
    stages = min(STAGES, blocks)
    return [blocks * k // stages for k in range(stages + 1)]


def phases_of(length):
    cuts = cuts_of(length)
    blocks, found = cuts[-1], []
    for k in range(len(cuts) - 1):
        begin, end = cuts[k] * BLK, min(cuts[k + 1] * BLK, length)
        if k + 2 == len(cuts):
            found.append((cuts[k], blocks, begin, length, "end", k))
        else:
            found.append((cuts[k], blocks, begin, end, "add" if k else "set", None))
            found.append((cuts[k], cuts[k + 1], end, length, "end", k))
    return found


def back_kernel(length, wide, *refs):
    tok, out_own, early, weights = refs[0:4]
    given = refs[4:12]
    inverse, delta, npar, norm_two, head_two = refs[12:17]
    out_all, grad_all, early_sum, late_sum, squares_out = refs[17:22]
    refs = refs[22:]
    xbuf, probs, dscore, gbd, qnd, gnd, dk, dv, dq_t, joined, grad_low, norm_one, late, squares = refs[0:14]
    sem, own_sems, out_sems, over_sems, beside_sems, pass_sems, square_sems = refs[14:21]
    early_bufs = refs[21:29]
    early_sems = refs[29]
    late_bufs = refs[30:37]
    late_sems = refs[37]
    taken = refs[38:46]
    taken_sems, weight_sems = refs[46:48]
    v_nat, k_t, q_nat, g_nat, g_t, x1, grad_mid, w_in = taken

    padded = x1.shape[0]
    blocks = padded // BLK
    phases = phases_of(length)
    me, row, core, over, beside = narrow_mates()
    soon = (cuts_of(length)[1] if blocks > 1 else blocks) * BLK

    def piece_of(index, ref, first_part):
        part = slice(0, soon) if first_part else slice(soon, None)
        return ref.at[part, :] if index in (0, 2, 3) else ref.at[:, part]

    def bring(first_part, first_sem):
        return save(
            [piece_of(index, given[index], first_part) for index in range(5)],
            [piece_of(index, taken[index], first_part) for index in range(5)],
            taken_sems,
            first_sem,
        )

    fetches = bring(True, 0)

    def width_of(index):
        count = phases[index][1] - phases[index][0]
        return SIDE if count % SIDE == 0 else 1

    def fetch(index, turn, slot):
        begins, _, begin, end = phases[index][0:4]
        return [
            pltpu.make_async_copy(
                weights.at[begins + turn * width_of(index) + k, pair, pl.ds(begin, end - begin)],
                probs.at[slot, k, pair, pl.ds(0, end - begin)],
                weight_sems.at[slot, k, pair],
            )
            for k in range(width_of(index))
            for pair in range(HEADS // 2)
        ]

    for one in fetch(0, 0, 0):
        one.start()
    fetches_next = bring(False, 8) if soon < padded else []
    fetches_late = save(given[5:8], taken[5:8], taken_sems, 5)
    copy = pltpu.make_async_copy(tok.at[me], xbuf.at[pl.ds(0, length)], sem)
    copy.start()
    hold = pltpu.make_async_copy(early.at[core], early_bufs[0], own_sems.at[0])
    hold.start()
    keep_out = pltpu.make_async_copy(out_own, out_all.at[me], own_sems.at[1])
    keep_out.start()
    greet(wide)
    first = WideFirst(early, early_bufs, early_sems, wide)
    last = RowFirst(late, (late.at[core],) + tuple(late_bufs), late_sems, wide)
    out_over = remote(out_own, out_all.at[me], out_sems, 0, "narrow", over)
    out_beside = remote(out_own, out_all.at[me], out_sems, 1, "narrow", beside)
    out_pass = remote(out_all.at[over], out_all.at[over], out_sems, 2, "narrow", beside)
    first.start_beside()
    out_over.start()
    out_beside.start()

    if padded > length:
        xbuf[length:, :] = jnp.zeros((padded - length, D), bf16)
        joined[length:, D:] = jnp.zeros((padded - length, 2 * D), bf16)
    dscore[...] = jnp.zeros(dscore.shape, bf16)
    for ref in (gbd, qnd, gnd):
        ref[...] = jnp.zeros(ref.shape, bf16)
    norm_one[...] = jnp.zeros(norm_one.shape, f32)
    dk[...] = jnp.zeros(dk.shape, f32)
    dv[...] = jnp.zeros(dv.shape, f32)
    scale = HEAD_DIM ** (-0.5)

    def begin():
        for one in fetches_next:
            one.wait()
        if padded > length:
            k_t[:, length:] = jnp.zeros((D, padded - length), bf16)
        hold.wait()
        first.start_spread()

    def hand_on():
        out_over.wait_recv()
        out_pass.start()

    def attention(steps, slot, start, stop, mode):
        spots = [block_of(step) for step in steps]
        size = stop - start
        whole = ceil_to(size, BLK)
        rows = key_chunk(size)

        def pairs_of(ref, pair, here):
            return jnp.concatenate([ref[2 * pair : 2 * pair + 1, here], ref[2 * pair + 1 : 2 * pair + 2, here]], axis=1)

        for pair in range(HEADS // 2):
            low = pair * PAIR
            mid = low + HEAD_DIM
            top = low + PAIR
            for k, here in enumerate(spots):
                gbd[k, pair, 0:HEAD_DIM, 0:BLK] = g_t[low:mid, here]
                gbd[k, pair, HEAD_DIM:PAIR, BLK:WIDE_COLS] = g_t[mid:top, here]
                both = q_nat[here, low:top]
                qnd[k, pair, 0:BLK, 0:HEAD_DIM] = both[:, 0:HEAD_DIM]
                qnd[k, pair, BLK:WIDE_COLS, HEAD_DIM:PAIR] = both[:, HEAD_DIM:PAIR]
                both = g_nat[here, low:top]
                gnd[k, pair, 0:BLK, 0:HEAD_DIM] = both[:, 0:HEAD_DIM]
                gnd[k, pair, BLK:WIDE_COLS, HEAD_DIM:PAIR] = both[:, HEAD_DIM:PAIR]
            for k, here in enumerate(spots):
                grads = gbd[k, pair]
                share = pairs_of(inverse, pair, here)
                inner = pairs_of(delta, pair, here)
                for at in range(0, size, rows):
                    part = slice(start + at, start + at + rows)
                    change = (dot(v_nat[part, low:top], grads) - inner) * share
                    weight = probs[slot, k, pair, at : at + rows, :].astype(f32)
                    dscore[k, at : at + rows, :] = (weight * change).astype(bf16)
            for k, here in enumerate(spots):
                dv[start:stop, low:top] += dot(probs[slot, k, pair, 0:size, :], gnd[k, pair])
            for k, here in enumerate(spots):
                dk[start:stop, low:top] += dot(dscore[k, 0:size, :], qnd[k, pair])
            for k, here in enumerate(spots):
                moved = dot(k_t[low:top, start : start + whole], dscore[k, 0:whole, :])
                one, two = moved[0:HEAD_DIM, 0:BLK], moved[HEAD_DIM:PAIR, BLK:WIDE_COLS]
                if mode != "set":
                    one = one + dq_t[low:mid, here]
                    two = two + dq_t[mid:top, here]
                if mode == "end":
                    joined[here, low:top] = (jnp.concatenate([one, two], axis=0) * scale).astype(bf16).T
                else:
                    dq_t[low:mid, here] = one
                    dq_t[mid:top, here] = two

    def run_phase(index, events):
        begins, ends, start, stop, mode, _ = phases[index]
        side = width_of(index)
        turns = (ends - begins) // side
        done = sum((p[1] - p[0]) // width_of(k) for k, p in enumerate(phases[:index]))

        @pl.loop(0, turns)
        def block(turn):
            slot = lax.rem(turn + done, 2)
            for when, event in events.items():
                pl.when(turn == when)(event)
            for one in fetch(index, turn, slot):
                one.wait()

            @pl.when(turn + 1 < turns)
            def ahead():
                for one in fetch(index, turn + 1, 1 - slot):
                    one.start()

            if index + 1 < len(phases):

                @pl.when(turn + 1 == turns)
                def across():
                    for one in fetch(index + 1, 0, 1 - slot):
                        one.start()

            attention([begins + turn * side + k for k in range(side)], slot, start, stop, mode)

    def settle_keys(start, stop):
        joined[start:stop, D : 2 * D] = (dk[start:stop, :] * scale).astype(bf16)
        joined[start:stop, 2 * D :] = dv[start:stop, :].astype(bf16)

    gain = npar[0:1, :]

    def close(steps):
        spots = [block_of(step) for step in steps]
        totals = [dot(joined[here, :], w_in[...].reshape(3 * D, D)) for here in spots]
        parts = [norm_parts(xbuf[here, :].astype(f32)) for here in spots]
        for here, total, (xhat, spread) in zip(spots, totals, parts):
            norm_one[0:8, :] += row_sums(total * xhat)
            norm_one[8:16, :] += row_sums(total)
            grad_low[here, :] = (grad_mid[here, :] + norm_back(xhat, spread, gain, total)).astype(bf16)

    def piece(index):
        return pl.ds(index * BLK, min(BLK, length - index * BLK))

    def chunk(index, who):
        return grad_all.at[who, piece(index)]

    def held(index):
        return grad_low.at[piece(index)]

    to_over = [remote(held(k), chunk(k, me), over_sems, k, "narrow", over) for k in range(blocks)]
    to_beside = [remote(held(k), chunk(k, me), beside_sems, k, "narrow", beside) for k in range(blocks)]
    passed = [remote(chunk(k, over), chunk(k, over), pass_sems, k, "narrow", beside) for k in range(blocks)]
    mine = pltpu.make_async_copy(grad_low.at[pl.ds(0, length)], grad_all.at[me], own_sems.at[2])

    for one in fetches:
        one.wait()
    events = [{} for _ in phases]
    events[0] = {min(3, blocks // width_of(0) - 1): begin}
    middle_phase = min(2 if len(phases) > 3 else 1, len(phases) - 1)
    events[middle_phase] = {0: first.start_over}
    cuts = cuts_of(length)
    sent = 0
    for index, (begins, ends, start, stop, mode, part) in enumerate(phases):
        run_phase(index, events[index])
        if index == middle_phase:
            hand_on()
        if part is None:
            continue
        settle_keys(cuts[part] * BLK, min(cuts[part + 1] * BLK, length))
        if part == 0:
            copy.wait()
            for one in fetches_late:
                one.wait()
        close(range(cuts[part], cuts[part + 1]))
        if part + 2 < len(cuts):
            sent = cuts[part + 1]
            for k in range(cuts[part], sent):
                to_over[k].start()
                to_beside[k].start()
        if part == max(0, len(cuts) - 3):
            first.start_share()

    late[...] = jnp.zeros(late.shape, bf16)
    grad_w = dot(x1[...], joined[...], TN)
    for which in range(3):
        turned = grad_w[:, which * D : (which + 1) * D].T.astype(bf16)
        for who in range(HEADS):
            late[who % 2, who // 2, which * HEAD_DIM : (which + 1) * HEAD_DIM, :] = turned[
                who * HEAD_DIM : (who + 1) * HEAD_DIM, :
            ]
    sums = [norm_one[0:8, :], norm_one[8:16, :], norm_two[0:8, :], norm_two[8:16, :]]
    extra = jnp.concatenate([jnp.sum(v, axis=0, keepdims=True) for v in sums] + [head_two[0:4, :]], axis=0)
    extra = jnp.concatenate([extra, jnp.zeros_like(extra)], axis=0).astype(bf16)
    for who in range(HEADS):
        late[who % 2, who // 2, 3 * HEAD_DIM : 3 * HEAD_DIM + 16, :] = extra
    last.start_beside()
    mine.start()
    first.finish()
    early_sum[...] = first.total[...].reshape(early_sum.shape)
    last.start_over()
    for k in range(sent, blocks):
        to_over[k].start()
        to_beside[k].start()
    last.start_spread()
    for k in range(sent):
        to_over[k].wait_recv()
        passed[k].start()
    last.start_share()
    last.finish()
    late_sum[...] = last.total[...].reshape(late_sum.shape)
    whole = early_sum[...].astype(f32)
    part = late_sum[0 : 3 * HEAD_DIM, :].astype(f32)
    level = jnp.sum(row_sums(whole * whole) + row_sums(part * part), axis=(0, 1), keepdims=True)
    squares[me] = jnp.broadcast_to(level, squares.shape[1:])
    told = []
    for index, mate in enumerate((over, beside, (1 - row) * 2 + 1 - core)):
        tell = remote(squares.at[me], squares.at[me], square_sems, index, "narrow", mate)
        tell.start()
        told.append(tell)
    for k in range(sent, blocks):
        to_over[k].wait_recv()
        passed[k].start()
    for tell in told:
        tell.wait_recv()
    squares_out[...] = squares[...]
    keep_out.wait()
    mine.wait()
    out_beside.wait_recv()
    out_pass.wait_recv()
    for k in range(blocks):
        to_beside[k].wait_recv()
        passed[k].wait_recv()
    for tell in told + [out_over, out_beside, out_pass] + to_over + to_beside + passed:
        tell.wait_send()
    first.settle()
    last.settle()


def back_stage(wide, tokens, out_own, early, weights, *rest):
    cells, length, _ = tokens.shape
    padded = rest[0].shape[0]
    blocks = padded // BLK
    reach = max(p[3] - p[2] for p in phases_of(length))
    shape = jax.ShapeDtypeStruct
    return pl.pallas_call(
        functools.partial(back_kernel, length, wide),
        out_shape=(
            shape((cells, length, D), bf16),
            shape((cells, length, D), bf16),
            shape((early_rows(wide), D), bf16),
            shape((late_rows(wide), D), bf16),
            shape((HEADS, 8, 128), f32),
        ),
        in_specs=anywhere(12) + vmem(5),
        out_specs=tuple(anywhere(2) + vmem(3)),
        scratch_shapes=[
            pltpu.VMEM((padded, D), bf16),
            pltpu.VMEM((2, SIDE, HEADS // 2, reach, WIDE_COLS), bf16),
            pltpu.VMEM((SIDE, ceil_to(reach, BLK), WIDE_COLS), bf16),
            pltpu.VMEM((SIDE, HEADS // 2, PAIR, WIDE_COLS), bf16),
            pltpu.VMEM((SIDE, HEADS // 2, WIDE_COLS, PAIR), bf16),
            pltpu.VMEM((SIDE, HEADS // 2, WIDE_COLS, PAIR), bf16),
            pltpu.VMEM((length, D), f32),
            pltpu.VMEM((length, D), f32),
            pltpu.VMEM((D, padded), f32),
            pltpu.VMEM((padded, 3 * D), bf16),
            pltpu.VMEM((padded, D), bf16),
            pltpu.VMEM((16, D), f32),
            pltpu.VMEM((2, 2, late_rows(wide), D), bf16),
            pltpu.VMEM((HEADS, 8, 128), f32),
            pltpu.SemaphoreType.DMA,
            pltpu.SemaphoreType.DMA((3,)),
            pltpu.SemaphoreType.DMA((2, 3)),
            pltpu.SemaphoreType.DMA((2, blocks)),
            pltpu.SemaphoreType.DMA((2, blocks)),
            pltpu.SemaphoreType.DMA((2, blocks)),
            pltpu.SemaphoreType.DMA((2, 3)),
        ]
        + share_scratch(early_rows(wide), wide, True)
        + share_scratch(late_rows(wide), wide, False)
        + [pltpu.VMEM(value.shape, value.dtype) for value in rest[0:8]]
        + [pltpu.SemaphoreType.DMA((13,)), pltpu.SemaphoreType.DMA((2, SIDE, HEADS // 2))],
        compiler_params=params(collective_id=2, has_side_effects=True),
        name="back",
    )(tokens, out_own, early, weights, *rest)


def adam_update(grad, first, second, weight, decay_rate, rate):
    first_new = decay_first * first + (1.0 - decay_first) * grad
    second_new = decay_second * second + (1.0 - decay_second) * grad * grad
    fix_first = 1.0 - decay_first**STEP
    fix_second = 1.0 - decay_second**STEP
    direction = first_new / fix_first / (jnp.sqrt(second_new / fix_second) + adam_eps)
    return (first_new, second_new, weight - rate * (direction + decay_rate * weight))


def finish_kernel(early, late, squares, *refs):
    sources, refs = refs[0:26], refs[26:]
    outputs, input_grad, grad_norm_ref = refs[0:3]
    targets, refs = refs[3:33], refs[33:]
    ins, refs = refs[0:24], refs[24:]
    outs, refs = refs[0:30], refs[30:]
    low, wide_out, same, in_sems, out_sems, low_sems, wide_sems, same_sems = refs
    out_all, grad_all = sources[24:26]
    cells, length, _ = grad_all.shape
    slots, deep, _ = low.shape
    pieces = [(cell, at) for cell in range(cells) for at in range(0, length, deep)]

    def load(index):
        cell, at = pieces[index]
        return pltpu.make_async_copy(grad_all.at[cell, pl.ds(at, deep)], low.at[index % slots], low_sems.at[index % slots])

    def store(index):
        cell, at = pieces[index]
        return pltpu.make_async_copy(
            wide_out.at[index % slots], input_grad.at[cell, pl.ds(at, deep)], wide_sems.at[index % slots]
        )

    def carry(index, out):
        cell, at = pieces[index]
        slot = same.at[index % slots]
        if out:
            return pltpu.make_async_copy(slot, outputs.at[cell, pl.ds(at, deep)], same_sems.at[1, index % slots])
        return pltpu.make_async_copy(out_all.at[cell, pl.ds(at, deep)], slot, same_sems.at[0, index % slots])

    def move(index):
        load(index).wait()
        if index >= slots:
            store(index - slots).wait()
        wide_out[index % slots] = low[index % slots].astype(f32)
        store(index).start()
        if index + slots < len(pieces):
            load(index + slots).start()
        carry(index, False).wait()
        carry(index, True).start()
        back = index - 2
        if back >= 0 and back + slots < len(pieces):
            carry(back, True).wait()
            carry(back + slots, False).start()

    early_pieces = min(slots, len(pieces))
    for index in range(early_pieces):
        load(index).start()
        carry(index, False).start()
    fetches = save(sources[0:24], ins, in_sems, 0)
    for index in range(early_pieces):
        move(index)
    for fetch in fetches:
        fetch.wait()
    place = lax.axis_index("wide")
    whole = early[...].astype(f32)
    small = late[...].astype(f32)
    extra = small[3 * HEAD_DIM : 3 * HEAD_DIM + 8, :]
    live = lax.broadcasted_iota(jnp.int32, extra.shape, 0) < 7
    extra = jnp.where(live, extra, 0.0)
    shards = jnp.sum(squares[...], axis=0)[0:1, 0:1]
    grad_norm = jnp.sqrt(shards + jnp.sum(extra * extra, axis=(0, 1), keepdims=True))
    grad_norm_ref[...] = grad_norm
    factor = jnp.minimum(1.0, clip_limit / grad_norm)
    grads = (
        None,
        whole[2 * D : 2 * D + HEAD_DIM, :],
        whole[D : 2 * D, :],
        whole[0:D, :].T,
        extra[0:4, :],
        extra[4:7, :],
    )
    decays = (weight_decay,) * 4 + (0.0, weight_decay)
    rates = (learn_rate,) * 4 + (norm_rate, learn_rate)

    def update(index, grad, at):
        weight, first, second = ins[index][at], ins[6 + index][at], ins[12 + index][at]
        clipped = grad * factor
        first_new, second_new, weight_new = adam_update(clipped, first, second, weight, decays[index], rates[index])
        outs[5 * index][at] = clipped
        outs[5 * index + 1][at] = first_new
        outs[5 * index + 2][at] = second_new
        outs[5 * index + 3][at] = weight_new
        return weight_new

    def mean(index, at, piece):
        outs[5 * index + 4][at] = ema_keep * ins[18 + index][at] + (1.0 - ema_keep) * piece

    def rows_here(values, count):
        return pltpu.roll(values, lax.rem(D - place * count, D), 0)[0:count, :]

    for which in range(3):
        weight_new = update(0, small[which * HEAD_DIM : (which + 1) * HEAD_DIM, :], which)
        mean(0, which, rows_here(weight_new.T, ins[18].shape[1]))
    for index in range(1, 4):
        weight_new = update(index, grads[index], Ellipsis)
        mean(index, Ellipsis, rows_here(weight_new if index == 2 else weight_new.T, ins[18 + index].shape[0]))
    for index in range(4, 6):
        weight_new = update(index, grads[index], Ellipsis)
        rows, count = ins[18 + index].shape
        full = jnp.concatenate([weight_new, jnp.zeros((8 - rows, D), f32)], axis=0)
        turned = pltpu.roll(full, lax.rem(D - place * count, D), 1)
        mean(index, Ellipsis, turned[0:rows, 0:count])

    stores = save(outs, targets, out_sems, 0)
    for index in range(early_pieces, len(pieces)):
        move(index)
    for index in range(max(0, len(pieces) - slots), len(pieces)):
        store(index).wait()
    for index in range(max(0, len(pieces) - slots), len(pieces)):
        carry(index, True).wait()
    for copy in stores:
        copy.wait()


def finish(early, late, squares, state, out_all, grad_all):
    shape = jax.ShapeDtypeStruct
    outs = []
    for index in range(6):
        outs += [(state[index].shape, f32)] * 4 + [(state[18 + index].shape, f32)]
    rows = 736 if grad_all.shape[1] % 736 == 0 else key_chunk(grad_all.shape[1])
    slots = 6
    return pl.pallas_call(
        finish_kernel,
        out_shape=tuple(
            [shape(out_all.shape, bf16), shape(grad_all.shape, f32), shape((1, 1), f32)] + [shape(*what) for what in outs]
        ),
        in_specs=vmem(3) + anywhere(26),
        out_specs=tuple(anywhere(2) + vmem(1) + anywhere(30)),
        scratch_shapes=[pltpu.VMEM(value.shape, f32) for value in state]
        + [pltpu.VMEM(*what) for what in outs]
        + [
            pltpu.VMEM((slots, rows, D), bf16),
            pltpu.VMEM((slots, rows, D), f32),
            pltpu.VMEM((slots, rows, D), bf16),
            pltpu.SemaphoreType.DMA((24,)),
            pltpu.SemaphoreType.DMA((30,)),
            pltpu.SemaphoreType.DMA((slots,)),
            pltpu.SemaphoreType.DMA((slots,)),
            pltpu.SemaphoreType.DMA((2, slots)),
        ],
        compiler_params=params(),
        name="finish",
    )(early, late, squares, *state, out_all, grad_all)


def on_device(cell_tokens, library_size, gene_counts, *state):
    turn = lambda v: jnp.swapaxes(v, -1, -2)
    state = tuple(turn(v) if index in (0, 6, 12, 19, 21) else v for index, v in enumerate(state))
    attend_in, attend_out, up_weight, down_weight, norm_params, head_weight = state[0:6]
    wide = lax.axis_size("wide")
    w_out, w_up, w_down, weights, x1, k_nat, v_nat, q_nat, q_t, k_t, v_t, w_in, out_t, totals = front(
        cell_tokens, attend_in, attend_out, up_weight, down_weight, norm_params
    )
    out_own, grad_mid, g_nat, g_t, early, weights, delta, inverse, norm_two, head_two = middle_stage(
        wide,
        cell_tokens,
        out_t,
        totals,
        q_t,
        k_nat,
        v_t,
        weights,
        w_out,
        w_up,
        w_down,
        norm_params,
        head_weight,
        gene_counts,
        library_size,
    )
    out_all, grad_all, early, late, squares = back_stage(
        wide,
        cell_tokens,
        out_own,
        early,
        weights,
        v_nat,
        k_t,
        q_nat,
        g_nat,
        g_t,
        x1,
        grad_mid,
        w_in,
        inverse,
        delta,
        norm_params,
        norm_two,
        head_two,
    )
    output, input_grad, grad_norm, *updates = finish(early, late, squares, state, out_all, grad_all)
    updates = [turn(v) if index in (0, 1, 2, 3, 9, 19) else v for index, v in enumerate(updates)]
    return (output, input_grad, grad_norm.reshape(()), *updates)


def solution(mesh):
    by_in, by_rows, by_cols = P(None, None, "narrow"), P("narrow", None), P(None, "narrow")
    kinds = (by_in, by_rows, by_cols, by_rows, P(), P())
    means = (
        P(None, "wide", "narrow"),
        P("narrow", "wide"),
        P("wide", "narrow"),
        P("narrow", "wide"),
        P(None, "wide"),
        P(None, "wide"),
    )
    cell = P("wide", None, None)
    outs = (cell, cell, P())
    for kind, mean in zip(kinds, means):
        outs += (kind, kind, kind, kind, mean)
    return jax.shard_map(
        on_device,
        mesh=mesh,
        in_specs=(cell, P("wide"), P("wide", None)) + kinds * 3 + means,
        out_specs=outs,
        check_vma=False,
    )
```

time: 208 us -> 143 us (0.69)
  Pallas kernels: 195 us -> 142 us
  other arithmetic: 6.81 us -> 0 us
  local copies, waits for them, and re-layouts: 5.37 us -> 0 us
    pallas_call x1, Pallas kernels: 116 us -> 75.3 us  [back_stage(): pl.pallas_call(functools.partial(back_kernel, length, wide), out_shape=(s...]
    pallas_call x1, Pallas kernels: 38.9 us -> 24.1 us  [middle_stage(): pl.pallas_call(functools.partial(middle_kernel, length), out_shape=(shape...]
    convert_element_type x1 -> x0, other arithmetic: 6.8 us -> none  [on_device(): return (out_all, grad_all.astype(f32), grad_norm.reshape(()), *updates)]
    pallas_call x2, Pallas kernels: 39.8 us -> 42.7 us  [the longest x1 31 us: front(): pl.pallas_call(functools.partial(front_kernel, length), out_shape=tuple([...]
    unnamed x7 -> x0, local copies, waits for them, and re-layouts: 2.14 us -> none
where the time goes in v3:
time: 143 us
  Pallas kernels  142 us (99%)
    pallas_call x1, Pallas kernels, back_stage(): pl.pallas_call(functools.partial(back_kernel, length, wide), out_shape=(s...  75.3 us
    pallas_call x1, Pallas kernels, front(): pl.pallas_call(functools.partial(front_kernel, length), out_shape=tuple([...  31 us
    pallas_call x1, Pallas kernels, middle_stage(): pl.pallas_call(functools.partial(middle_kernel, length), out_shape=(shape...  24.1 us
    pallas_call x1, Pallas kernels, finish(): pl.pallas_call(finish_kernel, out_shape=tuple([shape(out_all.shape, bf16)...  11.7 us

profile of v3, /device:TPU:0, one launch (start us, length us, event | category | flops | bytes accessed | tf_op | source)
XLA Modules:
  0.0 143.0 jit_solution(8460794587369965732)
XLA Ops:
  0.7 31.0 %front.1 = (bf16[256,256]{1,0:T(8,128)(2,1)}, bf16[256,1024]{1,0:T(8,128)(2,1)}, bf16[1024,256]{1,0:T(8,128)(2,1)}, bf16[9,2,2208,512]{3,2,1,0:T(8,128)(2,1)}, b...) custom-call(bf16[4,2208,256]{2,1,0:T(8,128)(2,1)} %refs_0_.1, ...), custom_call_target="tpu_custom_call" | custom-call | tf_op jit(solution)/shard_map/front/pallas_call | solution.py:315
  31.7 24.1 %middle.1 = (bf16[2208,256]{1,0:T(8,128)(2,1)}, f32[2304,256]{1,0:T(8,128)}, bf16[2304,256]{1,0:T(8,128)(2,1)}, bf16[256,2304]{1,0:T(8,128)(2,1)}, f32[2,2,640,2...) custom-call(bf16[4,2208,256]{2,1,0:T(8,128)(2,1)} %refs_0_.1, ...), custom_call_target="tpu_custom_call", output_to_operand_aliasing={{5}: (6, {})} | custom-call | tf_op jit(solution)/shard_map/middle/pallas_call | solution.py:642
  55.8 75.3 %back.1 = (bf16[4,2208,256]{2,1,0:T(8,128)(2,1)}, bf16[4,2208,256]{2,1,0:T(8,128)(2,1)}, bf16[640,256]{1,0:T(8,128)(2,1)}, bf16[256,256]{1,0:T(8,128)(2,1)}, f32[4,8,128]{2,1,0:T(8,128)}) custom-call(bf16[4,2208,256]{2,1,0:T(8,128)(2,1)} %refs_0_.1, bf16[2208,256]{1,0:T(8,128)(2,1)} %get-tuple-element.104.refs_1_, ...), custom_call_target="tpu_custom_call" | custom-call | tf_op jit(solution)/shard_map/back/pallas_call | solution.py:1112
  131.1 11.7 %finish.1 = (bf16[4,2208,256]{2,1,0:T(8,128)(2,1)}, f32[4,2208,256]{2,1,0:T(8,128)}, f32[1,1]{1,0:T(1,128)}, f32[3,64,256]{2,1,0:T(8,128)}, f32[3,64,256]{2,1,0:...) custom-call(bf16[640,256]{1,0:T(8,128)(2,1)} %get-tuple-element.119., ...), custom_call_target="tpu_custom_call" | custom-call | tf_op jit(solution)/shard_map/finish/pallas_call | solution.py:1285

commit v4 on v3

--- a/solution.py
+++ b/solution.py
@@ -428,6 +428,7 @@
     g_t_out,
     early,
     weights_out,
+    outputs,
     delta,
     inverse_totals,
     grad_norm,
@@ -545,8 +546,9 @@
             found = found.T
             logits[:, here] = found[0:8, :] + found[8:16, :]
 
-    send_out = pltpu.make_async_copy(res_high.at[pl.ds(0, length)], output, sem)
-    send_out.start()
+    send_out = save(
+        [res_high.at[pl.ds(0, length)]] * 2, [output, outputs.at[lax.axis_index("narrow")]], send_sems, 6
+    )
     genes = length - CLASS_TOK
     zero, disp, inflate = head_grads(
         (logits[0:1, :], logits[1:2, :], logits[2:3, :]),
@@ -631,7 +633,7 @@
     sends += put(
         5, 2 * D, early.shape[2], [grad[who * HEAD_DIM : (who + 1) * HEAD_DIM, :] for who in range(HEADS)]
     )
-    for send in [send_out] + sends:
+    for send in send_out + sends:
         send.wait()
 
 
@@ -648,13 +650,14 @@
             shape((D, padded), bf16),
             shape((2, 2, early_rows(wide), D), f32),
             shape(weights.shape, bf16),
+            shape(tokens.shape, bf16),
             shape((8, padded), f32),
             shape((8, padded), f32),
             shape((16, D), f32),
             shape((8, D), f32),
         ),
         in_specs=anywhere(2) + vmem(1) + anywhere(7) + vmem(3) + [pl.BlockSpec(memory_space=pltpu.SMEM)],
-        out_specs=tuple(anywhere(6) + vmem(4)),
+        out_specs=tuple(anywhere(7) + vmem(4)),
         input_output_aliases={6: 5},
         scratch_shapes=[
             pltpu.VMEM((padded, D), bf16),
@@ -682,7 +685,7 @@
             pltpu.VMEM(w_down.shape, bf16),
             pltpu.SemaphoreType.DMA,
             pltpu.SemaphoreType.DMA,
-            pltpu.SemaphoreType.DMA((6,)),
+            pltpu.SemaphoreType.DMA((8,)),
         ],
         compiler_params=params(),
         name="middle",
@@ -757,9 +760,11 @@
         self.to_over().start()
         self.keep[...] = both(self.row)
 
-    def start_spread(self):
+    def start_spread(self, extra):
         self.to_over().wait_recv()
-        whole = (self.keep[...] + self.come[...].astype(f32)).astype(bf16)
+        whole = self.keep[...] + self.come[...].astype(f32)
+        begin, end = 3 * HEAD_DIM, 3 * HEAD_DIM + 16
+        whole = jnp.concatenate([whole[0:begin], extra, jnp.zeros((8, D), f32), whole[end:]], axis=0).astype(bf16)
         self.parts[...] = whole.reshape(self.parts.shape)
         self.start_spreads()
 
@@ -833,7 +838,7 @@
     late_bufs = refs[30:37]
     late_sems = refs[37]
     taken = refs[38:46]
-    taken_sems, weight_sems = refs[46:48]
+    taken_sems, weight_sems, fellows, fellow_sems = refs[46:50]
     v_nat, k_t, q_nat, g_nat, g_t, x1, grad_mid, w_in = taken
 
     padded = x1.shape[0]
@@ -880,8 +885,6 @@
     copy.start()
     hold = pltpu.make_async_copy(early.at[core], early_bufs[0], own_sems.at[0])
     hold.start()
-    keep_out = pltpu.make_async_copy(out_own, out_all.at[me], own_sems.at[1])
-    keep_out.start()
     greet(wide)
     first = WideFirst(early, early_bufs, early_sems, wide)
     last = RowFirst(late, (late.at[core],) + tuple(late_bufs), late_sems, wide)
@@ -1038,8 +1041,8 @@
             copy.wait()
             for one in fetches_late:
                 one.wait()
-        close(range(cuts[part], cuts[part + 1]))
         if part + 2 < len(cuts):
+            close(range(cuts[part], cuts[part + 1]))
             sent = cuts[part + 1]
             for k in range(cuts[part], sent):
                 to_over[k].start()
@@ -1055,20 +1058,24 @@
             late[who % 2, who // 2, which * HEAD_DIM : (which + 1) * HEAD_DIM, :] = turned[
                 who * HEAD_DIM : (who + 1) * HEAD_DIM, :
             ]
+    last.start_beside()
+    close(range(cuts[-2], cuts[-1]))
     sums = [norm_one[0:8, :], norm_one[8:16, :], norm_two[0:8, :], norm_two[8:16, :]]
-    extra = jnp.concatenate([jnp.sum(v, axis=0, keepdims=True) for v in sums] + [head_two[0:4, :]], axis=0)
-    extra = jnp.concatenate([extra, jnp.zeros_like(extra)], axis=0).astype(bf16)
-    for who in range(HEADS):
-        late[who % 2, who // 2, 3 * HEAD_DIM : 3 * HEAD_DIM + 16, :] = extra
-    last.start_beside()
+    fellows[me] = jnp.concatenate([jnp.sum(v, axis=0, keepdims=True) for v in sums] + [head_two[0:4, :]], axis=0)
+    last.start_over()
+    gossip = []
+    for index, mate in enumerate((over, beside, (1 - row) * 2 + 1 - core)):
+        gossip.append(remote(fellows.at[me], fellows.at[me], fellow_sems, index, "narrow", mate))
+        gossip[-1].start()
     mine.start()
     first.finish()
     early_sum[...] = first.total[...].reshape(early_sum.shape)
-    last.start_over()
     for k in range(sent, blocks):
         to_over[k].start()
         to_beside[k].start()
-    last.start_spread()
+    for tell in gossip:
+        tell.wait_recv()
+    last.start_spread(jnp.sum(fellows[...], axis=0))
     for k in range(sent):
         to_over[k].wait_recv()
         passed[k].start()
@@ -1090,14 +1097,13 @@
     for tell in told:
         tell.wait_recv()
     squares_out[...] = squares[...]
-    keep_out.wait()
     mine.wait()
     out_beside.wait_recv()
     out_pass.wait_recv()
     for k in range(blocks):
         to_beside[k].wait_recv()
         passed[k].wait_recv()
-    for tell in told + [out_over, out_beside, out_pass] + to_over + to_beside + passed:
+    for tell in gossip + told + [out_over, out_beside, out_pass] + to_over + to_beside + passed:
         tell.wait_send()
     first.settle()
     last.settle()
@@ -1146,7 +1152,8 @@
         + share_scratch(early_rows(wide), wide, True)
         + share_scratch(late_rows(wide), wide, False)
         + [pltpu.VMEM(value.shape, value.dtype) for value in rest[0:8]]
-        + [pltpu.SemaphoreType.DMA((13,)), pltpu.SemaphoreType.DMA((2, SIDE, HEADS // 2))],
+        + [pltpu.SemaphoreType.DMA((13,)), pltpu.SemaphoreType.DMA((2, SIDE, HEADS // 2))]
+        + [pltpu.VMEM((HEADS, 8, D), f32), pltpu.SemaphoreType.DMA((2, HEADS - 1))],
         compiler_params=params(collective_id=2, has_side_effects=True),
         name="back",
     )(tokens, out_own, early, weights, *rest)
@@ -1162,7 +1169,7 @@
 
 
 def finish_kernel(early, late, squares, *refs):
-    sources, refs = refs[0:26], refs[26:]
+    sources, refs = refs[0:26], refs[27:]
     outputs, input_grad, grad_norm_ref = refs[0:3]
     targets, refs = refs[3:33], refs[33:]
     ins, refs = refs[0:24], refs[24:]
@@ -1183,8 +1190,12 @@
             wide_out.at[index % slots], input_grad.at[cell, pl.ds(at, deep)], wide_sems.at[index % slots]
         )
 
+    me = lax.axis_index("narrow")
+    carried = len(pieces) * (cells - 1) // cells
+
     def carry(index, out):
         cell, at = pieces[index]
+        cell = lax.rem(me + 1 + cell, cells)
         slot = same.at[index % slots]
         if out:
             return pltpu.make_async_copy(slot, outputs.at[cell, pl.ds(at, deep)], same_sems.at[1, index % slots])
@@ -1198,17 +1209,20 @@
         store(index).start()
         if index + slots < len(pieces):
             load(index + slots).start()
+        if index >= carried:
+            return
         carry(index, False).wait()
         carry(index, True).start()
         back = index - 2
-        if back >= 0 and back + slots < len(pieces):
+        if back >= 0 and back + slots < carried:
             carry(back, True).wait()
             carry(back + slots, False).start()
 
     early_pieces = min(slots, len(pieces))
     for index in range(early_pieces):
         load(index).start()
-        carry(index, False).start()
+        if index < carried:
+            carry(index, False).start()
     fetches = save(sources[0:24], ins, in_sems, 0)
     for index in range(early_pieces):
         move(index)
@@ -1269,13 +1283,13 @@
         move(index)
     for index in range(max(0, len(pieces) - slots), len(pieces)):
         store(index).wait()
-    for index in range(max(0, len(pieces) - slots), len(pieces)):
+    for index in range(max(0, carried - slots), carried):
         carry(index, True).wait()
     for copy in stores:
         copy.wait()
 
 
-def finish(early, late, squares, state, out_all, grad_all):
+def finish(early, late, squares, state, out_all, grad_all, outputs):
     shape = jax.ShapeDtypeStruct
     outs = []
     for index in range(6):
@@ -1287,7 +1301,8 @@
         out_shape=tuple(
             [shape(out_all.shape, bf16), shape(grad_all.shape, f32), shape((1, 1), f32)] + [shape(*what) for what in outs]
         ),
-        in_specs=vmem(3) + anywhere(26),
+        in_specs=vmem(3) + anywhere(27),
+        input_output_aliases={29: 0},
         out_specs=tuple(anywhere(2) + vmem(1) + anywhere(30)),
         scratch_shapes=[pltpu.VMEM(value.shape, f32) for value in state]
         + [pltpu.VMEM(*what) for what in outs]
@@ -1303,7 +1318,7 @@
         ],
         compiler_params=params(),
         name="finish",
-    )(early, late, squares, *state, out_all, grad_all)
+    )(early, late, squares, *state, out_all, grad_all, outputs)
 
 
 def on_device(cell_tokens, library_size, gene_counts, *state):
@@ -1314,7 +1329,7 @@
     w_out, w_up, w_down, weights, x1, k_nat, v_nat, q_nat, q_t, k_t, v_t, w_in, out_t, totals = front(
         cell_tokens, attend_in, attend_out, up_weight, down_weight, norm_params
     )
-    out_own, grad_mid, g_nat, g_t, early, weights, delta, inverse, norm_two, head_two = middle_stage(
+    out_own, grad_mid, g_nat, g_t, early, weights, outputs, delta, inverse, norm_two, head_two = middle_stage(
         wide,
         cell_tokens,
         out_t,
@@ -1351,7 +1366,7 @@
         norm_two,
         head_two,
     )
-    output, input_grad, grad_norm, *updates = finish(early, late, squares, state, out_all, grad_all)
+    output, input_grad, grad_norm, *updates = finish(early, late, squares, state, out_all, grad_all, outputs)
     updates = [turn(v) if index in (0, 1, 2, 3, 9, 19) else v for index, v in enumerate(updates)]
     return (output, input_grad, grad_norm.reshape(()), *updates)
 

time: 143 us -> 142 us (level)
  no operation moved by 1% of the time
where the time goes in v4:
time: 142 us
  Pallas kernels  141 us (99%)
    pallas_call x1, Pallas kernels, back_stage(): pl.pallas_call(functools.partial(back_kernel, length, wide), out_shape=(s...  74.8 us
    pallas_call x1, Pallas kernels, front(): pl.pallas_call(functools.partial(front_kernel, length), out_shape=tuple([...  31 us
    pallas_call x1, Pallas kernels, middle_stage(): pl.pallas_call(functools.partial(middle_kernel, length), out_shape=(shape...  24.1 us
    pallas_call x1, Pallas kernels, finish(): pl.pallas_call(finish_kernel, out_shape=tuple([shape(out_all.shape, bf16)...  10.9 us

profile of v4, /device:TPU:0, one launch (start us, length us, event | category | flops | bytes accessed | tf_op | source)
XLA Modules:
  0.0 141.7 jit_solution(5867583324478426503)
XLA Ops:
  0.7 31.0 %front.1 = (bf16[256,256]{1,0:T(8,128)(2,1)}, bf16[256,1024]{1,0:T(8,128)(2,1)}, bf16[1024,256]{1,0:T(8,128)(2,1)}, bf16[9,2,2208,512]{3,2,1,0:T(8,128)(2,1)}, b...) custom-call(bf16[4,2208,256]{2,1,0:T(8,128)(2,1)} %refs_0_.1, ...), custom_call_target="tpu_custom_call" | custom-call | tf_op jit(solution)/shard_map/front/pallas_call | solution.py:315
  31.7 24.1 %middle.1 = (bf16[2208,256]{1,0:T(8,128)(2,1)}, f32[2304,256]{1,0:T(8,128)}, bf16[2304,256]{1,0:T(8,128)(2,1)}, bf16[256,2304]{1,0:T(8,128)(2,1)}, f32[2,2,640,2...) custom-call(bf16[4,2208,256]{2,1,0:T(8,128)(2,1)} %refs_0_.1, ...), custom_call_target="tpu_custom_call", output_to_operand_aliasing={{5}: (6, {})} | custom-call | tf_op jit(solution)/shard_map/middle/pallas_call | solution.py:644
  55.8 74.8 %back.1 = (bf16[4,2208,256]{2,1,0:T(8,128)(2,1)}, bf16[4,2208,256]{2,1,0:T(8,128)(2,1)}, bf16[640,256]{1,0:T(8,128)(2,1)}, bf16[256,256]{1,0:T(8,128)(2,1)}, f32[4,8,128]{2,1,0:T(8,128)}) custom-call(bf16[4,2208,256]{2,1,0:T(8,128)(2,1)} %refs_0_.1, bf16[2208,256]{1,0:T(8,128)(2,1)} %get-tuple-element.105.refs_1_, ...), custom_call_target="tpu_custom_call" | custom-call | tf_op jit(solution)/shard_map/back/pallas_call | solution.py:1118
  130.6 10.9 %finish.1 = (bf16[4,2208,256]{2,1,0:T(8,128)(2,1)}, f32[4,2208,256]{2,1,0:T(8,128)}, f32[1,1]{1,0:T(1,128)}, f32[3,64,256]{2,1,0:T(8,128)}, f32[3,64,256]{2,1,0:...) custom-call(bf16[640,256]{1,0:T(8,128)(2,1)} %get-tuple-element.120., ...), custom_call_target="tpu_custom_call", output_to_operand_aliasing={{0}: (29, {})} | custom-call | tf_op jit(solution)/shard_map/finish/pallas_call | solution.py:1299
